TPU v7x, 256 devices: a whole 4x4x8 slice. The times are simulated.
256 devices in a mesh: seq: 32 (over x, z_lo, core), chan: 8 (over z_hi, y).
Axes of the slice: x: 4, y: 4, z: 8 (z_hi: 2, z_lo: 4; z = z_hi * 4 + z_lo), core: 2. Of those that a mesh axis runs over, the one named last changes fastest.
Arguments:
- query_in: bfloat16 [8, 1048576], P('chan', 'seq'), may hold values from -6 to 6
- key_in: bfloat16 [8, 1048576], P('chan', 'seq'), may hold values from -6 to 6
- value_in: bfloat16 [8, 1048576], P('chan', 'seq'), may hold values from -6 to 6
- short_taps: float32 [3, 8, 3], P(None, 'chan'), may hold values from -3 to 3
- long_filter: float32 [8, 1048576], P('chan', 'seq'), may hold values from -1 to 1
- skip_gain: float32 [8], P('chan'), may hold values from -4 to 4
- w_out: bfloat16 [8, 8], replicated, may hold values from -2 to 2
Outputs:
- block_out: bfloat16 [8, 1048576], P('chan', 'seq')
All inputs are finite; a program needn't handle non-finite values.
Results may differ from a plain program's by a relative error of at most 0.018.
Values may be sent and summed in bfloat16 or wider, within the bound.
No kernel may reach another device: no remote copies, remote signals or barrier semaphores. Data moves between devices by JAX's collectives and lax.ppermute only.
A program may use at most 192 MiB of HBM per device.

v0:
```python
import functools
import math

import jax
import jax.numpy as jnp
import ml_dtypes
import numpy as np
from jax import lax
from jax.experimental import pallas as pl
from jax.experimental.pallas import tpu as pltpu
from jax.sharding import PartitionSpec as P

LANES = 128
F32 = jnp.float32
BF16 = jnp.bfloat16
VMEM_LIMIT = 40 * 1024 * 1024


def tables(rows, devices):
    length = rows * LANES
    per = rows // devices
    k1 = np.arange(rows)
    first = 2.0 * math.pi * np.outer(k1 + 0.25, np.arange(rows)) / rows
    forward_first = np.stack([np.cos(first), -np.sin(first)])
    forward_first = forward_first.reshape(2, devices, per, rows).transpose(1, 0, 2, 3).reshape(2 * rows, rows)
    inverse_first = np.concatenate([np.cos(first), -np.sin(first)]).T / length
    turn = 2.0 * math.pi * np.outer(k1 + 0.25, np.arange(LANES)) / length
    turn = np.stack([np.cos(turn), np.sin(turn)])
    second = 2.0 * math.pi * np.outer(np.arange(LANES), np.arange(LANES)) / LANES
    cos, sin = np.cos(second), np.sin(second)
    forward_second = np.block([[cos, -sin], [sin, cos]])
    inverse_second = np.block([[cos, sin], [-sin, cos]])
    half = lambda values: values.astype(ml_dtypes.bfloat16)
    return (
        half(forward_first),
        turn.astype(np.float32),
        half(forward_second),
        half(inverse_second),
        half(inverse_first),
    )


def dot(left, right):
    return jnp.dot(left, right, preferred_element_type=F32)


def shifted(values, before, lane, row):
    turned = pltpu.roll(values, 1, 1)
    carried = pltpu.roll(turned, 1, 0)
    carried = jnp.where(row == 0, pltpu.roll(before, 1, 1), carried)
    return jnp.where(lane == 0, carried, turned)


def featurized(signal, before, taps_ref, stream):
    lane = lax.broadcasted_iota(jnp.int32, signal.shape, 1)
    row = lax.broadcasted_iota(jnp.int32, signal.shape, 0)
    before = jnp.broadcast_to(before, signal.shape)
    once = shifted(signal, before, lane, row)
    twice = shifted(once, pltpu.roll(before, 1, 1), lane, row)
    summed = (
        taps_ref[stream, 0] * signal + taps_ref[stream, 1] * once + taps_ref[stream, 2] * twice
    )
    return summed.astype(BF16)


def forward_kernel(devices, taps_ref, q_ref, k_ref, v_ref, rim_ref, filter_ref, first_ref, turn_ref, second_ref,
                   spectra_ref, q_feat_ref, product_ref):
    rims = rim_ref[...].astype(F32)
    rows = q_ref.shape[0]
    per = rows // devices
    q_feat_ref[...] = featurized(q_ref[...].astype(F32), rims[0:1], taps_ref, 0)
    k_feat = featurized(k_ref[...].astype(F32), rims[1:2], taps_ref, 1)
    v_feat = featurized(v_ref[...].astype(F32), rims[2:3], taps_ref, 2)
    product = k_feat.astype(F32) * v_feat.astype(F32)
    product_ref[...] = product
    signals = jnp.concatenate([product, filter_ref[...]], axis=1).astype(BF16)
    values = dot(first_ref[...], signals).reshape(devices, 2, per, 2 * LANES)
    real, imag = values[:, 0], values[:, 1]
    turn_real = turn_ref[0].reshape(devices, per, LANES)
    turn_imag = turn_ref[1].reshape(devices, per, LANES)
    packed = []
    for signal in range(2):
        lanes = slice(signal * LANES, (signal + 1) * LANES)
        a, b = real[:, :, lanes], imag[:, :, lanes]
        packed.append(
            jnp.concatenate([a * turn_real + b * turn_imag, b * turn_real - a * turn_imag], axis=2)
        )
    packed = jnp.concatenate(packed, axis=1).reshape(2 * rows, 2 * LANES).astype(BF16)
    spectra = dot(packed, second_ref[...])
    spectra_ref[...] = spectra.reshape(devices, 2 * per, 2 * LANES).astype(BF16)


def middle_kernel(devices, spectra_ref, out_ref):
    per = spectra_ref.shape[1] // 2
    blocks = []
    for p in range(devices):
        block = spectra_ref[p].astype(F32)
        blocks.append(
            (block[:per, :LANES], block[:per, LANES:], block[per:, :LANES], block[per:, LANES:])
        )
    behind_real = jnp.zeros((per, LANES), F32)
    behind_imag = behind_real
    for p in range(devices):
        real = imag = None
        for q in range(p + 1):
            a, b = blocks[q][0], blocks[q][1]
            c, d = blocks[p - q][2], blocks[p - q][3]
            term_real, term_imag = a * c - b * d, a * d + b * c
            real = term_real if real is None else real + term_real
            imag = term_imag if imag is None else imag + term_imag
        out_ref[p] = jnp.concatenate([real - behind_imag, imag + behind_real], axis=0).astype(BF16)
        behind_real, behind_imag = real, imag


def inverse_kernel(devices, skip_ref, spectra_ref, turn_ref, second_ref, first_ref, q_feat_ref, product_ref,
                   gating_ref):
    rows = q_feat_ref.shape[0]
    per = rows // devices
    packed = jnp.concatenate(
        [spectra_ref[:, :per, :].astype(F32), spectra_ref[:, per:, :].astype(F32)], axis=2
    )
    values = dot(packed.reshape(rows, 2 * LANES).astype(BF16), second_ref[...])
    a, b = values[:, :LANES], values[:, LANES:]
    turn_real, turn_imag = turn_ref[0], turn_ref[1]
    turned = jnp.concatenate([a * turn_real - b * turn_imag, a * turn_imag + b * turn_real], axis=0)
    convolved = dot(first_ref[...], turned.astype(BF16))
    gating = q_feat_ref[...].astype(F32) * (convolved + skip_ref[0] * product_ref[...])
    gating_ref[...] = gating.astype(BF16)


def project_kernel(weights_ref, gating_ref, out_ref):
    total = weights_ref[0] * gating_ref[0].astype(F32)
    for c in range(1, gating_ref.shape[0]):
        total = total + weights_ref[c] * gating_ref[c].astype(F32)
    out_ref[...] = total.astype(BF16)


SMEM = pl.BlockSpec(memory_space=pltpu.SMEM)
VMEM = pl.BlockSpec(memory_space=pltpu.VMEM)
PARAMS = pltpu.CompilerParams(vmem_limit_bytes=VMEM_LIMIT)


def on_device(devices, chans, query_in, key_in, value_in, short_taps, long_filter, skip_gain, w_out):
    width = query_in.shape[1]
    rows = width // LANES
    per = rows // devices
    forward_first, turn, forward_second, inverse_second, inverse_first = tables(rows, devices)
    query, key, value = (a.reshape(rows, LANES) for a in (query_in, key_in, value_in))
    rims = jnp.stack([a[0, -LANES:] for a in (query_in, key_in, value_in)])
    rims = lax.ppermute(rims, "seq", [(i, i + 1) for i in range(devices - 1)])
    spectra, q_feat, product = pl.pallas_call(
        functools.partial(forward_kernel, devices),
        in_specs=[SMEM] + [VMEM] * 8,
        out_specs=[VMEM] * 3,
        out_shape=[
            jax.ShapeDtypeStruct((devices, 2 * per, 2 * LANES), BF16),
            jax.ShapeDtypeStruct((rows, LANES), BF16),
            jax.ShapeDtypeStruct((rows, LANES), F32),
        ],
        compiler_params=PARAMS,
        name="forward",
    )(short_taps[:, 0], query, key, value, rims, long_filter.reshape(rows, LANES), forward_first, turn, forward_second)
    spectra = lax.all_to_all(spectra, "seq", 0, 0)
    spectra = pl.pallas_call(
        functools.partial(middle_kernel, devices),
        in_specs=[VMEM],
        out_specs=VMEM,
        out_shape=jax.ShapeDtypeStruct((devices, 2 * per, LANES), BF16),
        compiler_params=PARAMS,
        name="middle",
    )(spectra)
    spectra = lax.all_to_all(spectra, "seq", 0, 0)
    gating = pl.pallas_call(
        functools.partial(inverse_kernel, devices),
        in_specs=[SMEM] + [VMEM] * 6,
        out_specs=VMEM,
        out_shape=jax.ShapeDtypeStruct((rows, LANES), BF16),
        compiler_params=PARAMS,
        name="inverse",
    )(skip_gain, spectra, turn, inverse_second, inverse_first, q_feat, product)
    gathered = lax.all_to_all(jnp.broadcast_to(gating[None], (chans, rows, LANES)), "chan", 0, 0)
    weights = lax.dynamic_index_in_dim(w_out, lax.axis_index("chan"), axis=1, keepdims=False).astype(F32)
    out = pl.pallas_call(
        project_kernel,
        in_specs=[SMEM, VMEM],
        out_specs=VMEM,
        out_shape=jax.ShapeDtypeStruct((rows, LANES), BF16),
        compiler_params=PARAMS,
        name="project",
    )(weights, gathered)
    return out.reshape(1, width)


def solution(mesh):
    return jax.shard_map(
        functools.partial(on_device, mesh.shape["seq"], mesh.shape["chan"]),
        mesh=mesh,
        in_specs=(
            P("chan", "seq"),
            P("chan", "seq"),
            P("chan", "seq"),
            P(None, "chan", None),
            P("chan", "seq"),
            P("chan"),
            P(),
        ),
        out_specs=P("chan", "seq"),
        check_vma=False,
    )
```

profile of v0, /device:TPU:32, one launch (start us, length us, event | category | flops | bytes accessed | tf_op | source)
XLA Modules:
  0.0 74.6 jit_solution(12707322735300647323)
XLA Ops:
  0.0 0.0 slice-start
  0.0 0.0 slice-start.1
  0.0 0.0 slice-start.2
  0.0 0.6 slice-done
  0.7 0.0 slice-done.1
  0.7 0.0 slice-done.2
  0.7 0.0 copy-start
  0.7 0.0 copy-start.1
  0.7 2.1 %collective-permute-start = (bf16[3,128]{1,0:T(4,128)(2,1)S(1)}, bf16[3,128]{1,0:T(4,128)(2,1)S(1)}, u32[]{:S(2)}, u32[]{:S(2)}) collective-permute-start(bf16[3,128]{1,0:T(4,128)(2,1)S(1)} %pad_maximum_fusion), channel_id=1, source_target_pairs={{0,8},{8,16},{16,24},{24,32},{32,40},{40,48},{48,56},{56,64},{64,7... | collective-permute-start | bytes 2312 | tf_op jit(solution)/shard_map/ppermute | solution.py:150
  2.8 1.3 %reduce.1 = bf16[32768]{0:T(1024)(128)(2,1)S(1)} reduce(bf16[1,32768]{1,0:T(2,128)(2,1)} %param.12, bf16[]{:T(256)} %constant.32), dimensions={0}, to_apply=%param.12.reduce_sub_computation | reduce | bytes 131074 | tf_op args[0]
  4.1 1.3 %reduce.2 = bf16[32768]{0:T(1024)(128)(2,1)S(1)} reduce(bf16[1,32768]{1,0:T(2,128)(2,1)} %param.13, bf16[]{:T(256)} %constant.32), dimensions={0}, to_apply=%param.13.reduce_sub_computation | reduce | bytes 131074 | tf_op args[1]
  5.3 0.0 copy-start.7
  5.3 1.3 %reduce.3 = bf16[32768]{0:T(1024)(128)(2,1)S(1)} reduce(bf16[1,32768]{1,0:T(2,128)(2,1)} %param.14, bf16[]{:T(256)} %constant.32), dimensions={0}, to_apply=%param.14.reduce_sub_computation | reduce | bytes 131074 | tf_op args[2]
  6.6 0.0 copy-done.7
  6.6 0.0 collective-permute-done.rim_ref
  6.6 0.0 copy-done
  6.6 0.0 copy-done.1
  6.7 0.0 copy-start.3
  6.7 0.9 %copy-done.3 = f32[1,32768]{1,0:T(1,128)S(1)} copy-done((f32[1,32768]{1,0:T(1,128)S(1)}, f32[1,32768]{1,0:T(1,128)}, u32[]{:S(2)}) %copy-start.3) | copy-done | bytes 131096
  7.6 0.0 copy-start.4
  7.6 0.9 %copy-done.4 = bf16[256,256]{1,0:T(8,128)(2,1)S(1)} copy-done((bf16[256,256]{1,0:T(8,128)(2,1)S(1)}, bf16[256,256]{1,0:T(8,128)(2,1)}, u32[]{:S(2)}) %copy-start.4) | copy-done | bytes 131096
  8.5 1.2 %forward.1 = (bf16[32,16,256]{2,1,0:T(8,128)(2,1)S(1)}, bf16[256,128]{1,0:T(8,128)(2,1)S(1)}, f32[256,128]{1,0:T(8,128)S(1)}) custom-call(f32[3,3]{1,0:T(4,128)S(1)} %bitcast.17, bf16[256,128]{1,0:T(8,128)(2,1)S(1)} %bitcast.12, bf16[256,128]{1,0:T(8,128)(2,1)S(1)} %bitcast.13, bf16[256,128]{1,0:T(8,128)(2,1)S(1)} %bitcast.14, ...), custom_call_target="tpu_custom_call" | custom-call | tf_op jit(solution)/shard_map/forward/pallas_call | solution.py:151
  9.6 18.1 %all_to_all.15.spectra_ref = bf16[32,16,256]{2,1,0:T(8,128)(2,1)S(1)} all-to-all(bf16[32,16,256]{2,1,0:T(8,128)(2,1)S(1)} %get-tuple-element.8), channel_id=1, replica_groups=mesh['seq'=32,'chan'=8] {'seq'}, dimensions={0} | all-to-all | bytes 524288 | tf_op jit(solution)/shard_map/all_to_all | solution.py:163
  27.7 0.0 copy-start.2
  27.7 1.2 %middle.1 = bf16[32,16,128]{2,1,0:T(8,128)(2,1)} custom-call(bf16[32,16,256]{2,1,0:T(8,128)(2,1)S(1)} %all_to_all.15.spectra_ref), custom_call_target="tpu_custom_call" | custom-call | tf_op jit(solution)/shard_map/middle/pallas_call | solution.py:164
  29.0 0.0 copy-start.5
  29.0 5.6 %all-to-all-start.1 = ((bf16[32,16,128]{2,1,0:T(8,128)(2,1)}), bf16[32,16,128]{2,1,0:T(8,128)(2,1)S(1)}, u32[]{:S(2)}, u32[]{:S(2)}) async-start(bf16[32,16,128]{2,1,0:T(8,128)(2,1)} %middle.1), calls=%async_computation.1 | async-start | bytes 262144 | tf_op jit(solution)/shard_map/all_to_all | solution.py:172
  35.2 6.7 %all-to-all-done.1.spectra_ref = bf16[32,16,128]{2,1,0:T(8,128)(2,1)S(1)} async-done(((bf16[32,16,128]{2,1,0:T(8,128)(2,1)}), bf16[32,16,128]{2,1,0:T(8,128)(2,1)S(1)}, u32[]{:S(2)}, u32[]{:S(2)}) %all-to-all-start.1) | async-done | bytes 131104 | tf_op jit(solution)/shard_map/all_to_all | solution.py:172
  42.0 0.0 copy-done.2
  42.0 0.0 copy-done.5
  42.0 0.5 inverse.1
  42.4 0.9 %broadcast_in_dim.2 = bf16[8,256,128]{2,1,0:T(8,128)(2,1)} broadcast(bf16[256,128]{1,0:T(8,128)(2,1)S(1)} %inverse.1), dimensions={1,2} | broadcast | bytes 589824 | tf_op jit(solution)/shard_map/broadcast_in_dim | solution.py:181
  43.3 10.4 %all-to-all-start.2 = ((bf16[8,256,128]{2,1,0:T(8,128)(2,1)}), bf16[8,256,128]{2,1,0:T(8,128)(2,1)S(1)}, u32[]{:S(2)}, u32[]{:S(2)}) async-start(bf16[8,256,128]{2,1,0:T(8,128)(2,1)} %broadcast_in_dim.2), calls=%async_computation.2 | async-start | bytes 1048576 | tf_op jit(solution)/shard_map/all_to_all | solution.py:181
  53.7 0.0 copy-start.6
  53.7 0.7 copy-done.6
  54.4 0.2 convert_reduce_fusion.weights_ref
  54.5 18.6 %all-to-all-done.2.gating_ref = bf16[8,256,128]{2,1,0:T(8,128)(2,1)S(1)} async-done(((bf16[8,256,128]{2,1,0:T(8,128)(2,1)}), bf16[8,256,128]{2,1,0:T(8,128)(2,1)S(1)}, u32[]{:S(2)}, u32[]{:S(2)}) %all-to-all-start.2) | async-done | bytes 524320 | tf_op jit(solution)/shard_map/all_to_all | solution.py:181
  73.2 0.6 project.1
  73.8 0.8 %copy.17 = bf16[1,1,256,128]{3,1,2,0:T(2,128)(2,1)} copy(bf16[1,1,256,128]{3,2,1,0:T(8,128)(2,1)S(1)} %bitcast.15) | data formatting | bytes 131072
  (2 shorter events, 0.0 us)
Async XLA Ops:
  0.0 0.7 slice-start
  0.0 0.7 slice-start.1
  0.0 0.7 slice-start.2
  0.7 5.9 %copy-start = (f32[2,256,128]{2,1,0:T(8,128)S(1)}, f32[2,256,128]{2,1,0:T(8,128)}, u32[]{:S(2)}) copy-start(f32[2,256,128]{2,1,0:T(8,128)} %constant.21.clone.turn_ref) | copy-start | bytes 786436
  0.7 5.9 %copy-start.1 = (bf16[512,256]{1,0:T(8,128)(2,1)S(1)}, bf16[512,256]{1,0:T(8,128)(2,1)}, u32[]{:S(2)}) copy-start(bf16[512,256]{1,0:T(8,128)(2,1)} %constant.20.clone.first_ref) | copy-start | bytes 786436
  0.7 5.9 %collective-permute-start = (bf16[3,128]{1,0:T(4,128)(2,1)S(1)}, bf16[3,128]{1,0:T(4,128)(2,1)S(1)}, u32[]{:S(2)}, u32[]{:S(2)}) collective-permute-start(bf16[3,128]{1,0:T(4,128)(2,1)S(1)} %pad_maximum_fusion), channel_id=1, source_target_pairs={{0,8},{8,16},{16,24},{24,32},{32,40},{40,48},{48,56},{56,64},{64,7... | collective-permute-start | bytes 2312 | tf_op jit(solution)/shard_map/ppermute | solution.py:150
  5.3 1.3 %copy-start.7 = (f32[3,1,3]{2,1,0:T(1,128)S(1)}, f32[3,1,3]{2,1,0:T(1,128)}, u32[]{:S(2)}) copy-start(f32[3,1,3]{2,1,0:T(1,128)} %param.15) | copy-start | bytes 112
  6.7 0.9 %copy-start.3 = (f32[1,32768]{1,0:T(1,128)S(1)}, f32[1,32768]{1,0:T(1,128)}, u32[]{:S(2)}) copy-start(f32[1,32768]{1,0:T(1,128)} %param.16) | copy-start | bytes 393220
  7.6 0.9 %copy-start.4 = (bf16[256,256]{1,0:T(8,128)(2,1)S(1)}, bf16[256,256]{1,0:T(8,128)(2,1)}, u32[]{:S(2)}) copy-start(bf16[256,256]{1,0:T(8,128)(2,1)} %constant.22.clone.second_ref) | copy-start | bytes 393220
  27.7 14.2 %copy-start.2 = (bf16[256,512]{1,0:T(8,128)(2,1)S(1)}, bf16[256,512]{1,0:T(8,128)(2,1)}, u32[]{:S(2)}) copy-start(bf16[256,512]{1,0:T(8,128)(2,1)} %constant.24.clone.first_ref) | copy-start | bytes 786436
  29.0 13.0 %copy-start.5 = (bf16[256,256]{1,0:T(8,128)(2,1)S(1)}, bf16[256,256]{1,0:T(8,128)(2,1)}, u32[]{:S(2)}) copy-start(bf16[256,256]{1,0:T(8,128)(2,1)} %constant.23.clone.second_ref) | copy-start | bytes 393220
  29.0 13.0 %all-to-all-start.1 = ((bf16[32,16,128]{2,1,0:T(8,128)(2,1)}), bf16[32,16,128]{2,1,0:T(8,128)(2,1)S(1)}, u32[]{:S(2)}, u32[]{:S(2)}) async-start(bf16[32,16,128]{2,1,0:T(8,128)(2,1)} %middle.1), calls=%async_computation.1 | async-start | bytes 262144 | tf_op jit(solution)/shard_map/all_to_all | solution.py:172
  43.3 29.9 %all-to-all-start.2 = ((bf16[8,256,128]{2,1,0:T(8,128)(2,1)}), bf16[8,256,128]{2,1,0:T(8,128)(2,1)S(1)}, u32[]{:S(2)}, u32[]{:S(2)}) async-start(bf16[8,256,128]{2,1,0:T(8,128)(2,1)} %broadcast_in_dim.2), calls=%async_computation.2 | async-start | bytes 1048576 | tf_op jit(solution)/shard_map/all_to_all | solution.py:181
  53.7 0.7 copy-start.6
where the time goes:
time: 75 us; the launch traced here: 74.6 us
  waiting for transfers between devices  25.4 us (34%)
  blocking collectives  18.1 us (24%)
  starting transfers between devices  18 us (24%)
  local copies, waits for them, and re-layouts  4.82 us (6%)
  other arithmetic  3.99 us (5%)
  Pallas kernels  3.51 us (5%)
  between operations  0.78 us (1%)
    all_to_all x1, waiting for transfers between devices, on_device(): lax.all_to_all(jnp.broadcast_to(gating[None], (chans, rows, LANES)), 'cha...  18.6 us
    all_to_all x1, blocking collectives, on_device(): spectra = lax.all_to_all(spectra, 'seq', 0, 0)  18.1 us
    all_to_all x1, starting transfers between devices, on_device(): lax.all_to_all(jnp.broadcast_to(gating[None], (chans, rows, LANES)), 'cha...  10.4 us
    all_to_all x1, waiting for transfers between devices, on_device(): spectra = lax.all_to_all(spectra, 'seq', 0, 0)  6.72 us
    all_to_all x1, starting transfers between devices, on_device(): spectra = lax.all_to_all(spectra, 'seq', 0, 0)  5.61 us
    unnamed x3, other arithmetic  3.79 us
    unnamed x18, local copies, waits for them, and re-layouts  3.27 us
    ppermute x1, starting transfers between devices, on_device(): rims = lax.ppermute(rims, 'seq', [(i, i + 1) for i in range(devices - 1)])  2.05 us
  transfers between devices with their start and end apart: 3, of which 2 were waited for; matrix products, arithmetic and copies ran while one was open for 5% of the time, Pallas kernels for 0%

commit v1 on v0

v1 whole, which is shorter than its diff:
```python
import functools
import math

import jax
import jax.numpy as jnp
import ml_dtypes
import numpy as np
from jax import lax
from jax.experimental import pallas as pl
from jax.experimental.pallas import tpu as pltpu
from jax.sharding import PartitionSpec as P

LANES = 128
F32 = jnp.float32
BF16 = jnp.bfloat16
VMEM_LIMIT = 40 * 1024 * 1024


def tables(rows, devices):
    length = rows * LANES
    per = rows // devices
    k1 = np.arange(rows)
    first = 2.0 * math.pi * np.outer(k1 + 0.25, np.arange(rows)) / rows
    forward_first = np.stack([np.cos(first), -np.sin(first)])
    forward_first = forward_first.reshape(2, devices, per, rows).transpose(1, 0, 2, 3).reshape(2 * rows, rows)
    inverse_first = np.concatenate([np.cos(first), -np.sin(first)]).T / length
    turn = 2.0 * math.pi * np.outer(k1 + 0.25, np.arange(LANES)) / length
    turn = np.stack([np.cos(turn), np.sin(turn)])
    second = 2.0 * math.pi * np.outer(np.arange(LANES), np.arange(LANES)) / LANES
    cos, sin = np.cos(second), np.sin(second)
    forward_second = np.block([[cos, -sin], [sin, cos]])
    inverse_second = np.block([[cos, sin], [-sin, cos]])
    basis = 2.0 * math.pi * (np.arange(per)[:, None] + 0.25 + rows * np.arange(LANES)[None, :]) / length
    basis = np.stack([np.cos(basis), -np.sin(basis)])
    half = lambda values: values.astype(ml_dtypes.bfloat16)
    return (
        half(forward_first),
        turn.astype(np.float32),
        half(forward_second),
        half(inverse_second),
        half(inverse_first),
        basis.astype(np.float32),
    )


def dot(left, right):
    return jnp.dot(left, right, preferred_element_type=F32)


def shifted(values, before, lane, row):
    turned = pltpu.roll(values, 1, 1)
    carried = pltpu.roll(turned, 1, 0)
    carried = jnp.where(row == 0, pltpu.roll(before, 1, 1), carried)
    return jnp.where(lane == 0, carried, turned)


def featurized(signal, before, taps_ref, stream):
    lane = lax.broadcasted_iota(jnp.int32, signal.shape, 1)
    row = lax.broadcasted_iota(jnp.int32, signal.shape, 0)
    before = jnp.broadcast_to(before, signal.shape)
    once = shifted(signal, before, lane, row)
    twice = shifted(once, pltpu.roll(before, 1, 1), lane, row)
    summed = (
        taps_ref[stream, 0] * signal + taps_ref[stream, 1] * once + taps_ref[stream, 2] * twice
    )
    return summed.astype(BF16)


def head_mask(shape):
    lane = lax.broadcasted_iota(jnp.int32, shape, len(shape) - 1)
    row = lax.broadcasted_iota(jnp.int32, shape, len(shape) - 2)
    return (row == 0) & (lane < 2)


def forward_kernel(devices, taps_ref, q_hbm, k_hbm, v_hbm, filter_hbm, first_hbm, turn_hbm, second_hbm,
                   message_ref, q_feat_ref, product_ref,
                   q_ref, k_ref, v_ref, filter_ref, first_ref, turn_ref, second_ref, sems):
    pairs = (
        (k_hbm, k_ref), (v_hbm, v_ref), (filter_hbm, filter_ref), (first_hbm, first_ref),
        (q_hbm, q_ref), (turn_hbm, turn_ref), (second_hbm, second_ref),
    )
    copies = [pltpu.make_async_copy(source, target, sems.at[i]) for i, (source, target) in enumerate(pairs)]
    for copy in copies:
        copy.start()
    rows = product_ref.shape[0]
    per = rows // devices
    nothing = jnp.zeros((1, LANES), F32)
    copies[0].wait()
    key = k_ref[...].astype(F32).reshape(rows, LANES)
    k_feat = featurized(key, nothing, taps_ref, 1)
    copies[1].wait()
    value = v_ref[...].astype(F32).reshape(rows, LANES)
    v_feat = featurized(value, nothing, taps_ref, 2)
    product = k_feat.astype(F32) * v_feat.astype(F32)
    product_ref[...] = product
    copies[2].wait()
    signals = jnp.concatenate([product, filter_ref[...]], axis=1).astype(BF16)
    copies[3].wait()
    values = dot(first_ref[...], signals).reshape(devices, 2, per, 2 * LANES)
    copies[4].wait()
    query = q_ref[...].astype(F32).reshape(rows, LANES)
    q_feat_ref[...] = featurized(query, nothing, taps_ref, 0)
    rims = [a[r : r + 1] for a in (key, value, query) for r in (0, rows - 1)]
    rims = jnp.concatenate(rims + [nothing, nothing], axis=0)
    copies[5].wait()
    real, imag = values[:, 0], values[:, 1]
    turn_real = turn_ref[0].reshape(devices, per, LANES)
    turn_imag = turn_ref[1].reshape(devices, per, LANES)
    packed = []
    for signal in range(2):
        lanes = slice(signal * LANES, (signal + 1) * LANES)
        a, b = real[:, :, lanes], imag[:, :, lanes]
        packed.append(
            jnp.concatenate([a * turn_real + b * turn_imag, b * turn_real - a * turn_imag], axis=2)
        )
    packed = jnp.concatenate(packed, axis=1).reshape(2 * rows, 2 * LANES).astype(BF16)
    copies[6].wait()
    spectra = dot(packed, second_ref[...]).reshape(devices, 2 * per, 2 * LANES)
    message_ref[...] = jnp.concatenate(
        [
            spectra[:, :per, :LANES],
            spectra[:, :per, LANES:],
            spectra[:, per:, :LANES],
            spectra[:, per:, LANES:],
            jnp.broadcast_to(rims[None], (devices, 8, LANES)),
        ],
        axis=1,
    ).astype(BF16)


def rounded(values):
    return values.astype(BF16).astype(F32)


def head_features(rims, taps_ref):
    lane = lax.broadcasted_iota(jnp.int32, rims.shape, 2)
    row = lax.broadcasted_iota(jnp.int32, rims.shape[1:], 0)[None]
    taps = [
        jnp.where(row < 2, taps_ref[1, j], jnp.where(row < 4, taps_ref[2, j], taps_ref[0, j])) for j in range(3)
    ]
    before = jnp.concatenate([jnp.zeros_like(rims[:1]), rims[:-1]], axis=0)
    before = pltpu.roll(before, rims.shape[1] - 1, 1)
    once, twice = pltpu.roll(rims, 1, 2), pltpu.roll(rims, 2, 2)
    with_before = (
        taps[0] * rims
        + taps[1] * jnp.where(lane < 1, pltpu.roll(before, 1, 2), once)
        + taps[2] * jnp.where(lane < 2, pltpu.roll(before, 2, 2), twice)
    )
    alone = taps[0] * rims + taps[1] * jnp.where(lane < 1, 0.0, once) + taps[2] * jnp.where(lane < 2, 0.0, twice)
    return rounded(with_before), rounded(alone)


def middle_kernel(devices, taps_ref, message_ref, basis_ref, out_ref, heads_ref, heads_scratch):
    per = (message_ref.shape[1] - 8) // 4
    own = lax.axis_index("seq")
    heads, alone = head_features(message_ref[:, 4 * per :, :].astype(F32), taps_ref)
    heads_scratch[...] = heads
    heads_ref[...] = heads_scratch[own]
    error = heads * pltpu.roll(heads, 6, 1) - alone * pltpu.roll(alone, 6, 1)
    angle = jnp.full((per, LANES), own, jnp.int32).astype(F32) * (2.0 * math.pi / (devices * LANES))
    square = angle * angle
    cos = 1.0 - square * (0.5 - square * (1.0 / 24.0))
    sin = angle * (1.0 - square * (1.0 / 6.0 - square * (1.0 / 120.0)))
    basis_real, basis_imag = basis_ref[0], basis_ref[1]
    point_real = basis_real * cos + basis_imag * sin
    point_imag = basis_imag * cos - basis_real * sin
    blocks = []
    for p in range(devices):
        block = message_ref[p].astype(F32)
        real, imag = block[:per], block[per : 2 * per]
        if p > 0:
            zeroth, first = error[p, 0:1, 0:1], error[p, 0:1, 1:2]
            real = real + (zeroth + first * point_real)
            imag = imag + first * point_imag
        blocks.append((real, imag, block[2 * per : 3 * per], block[3 * per : 4 * per]))
    behind_real = jnp.zeros((per, LANES), F32)
    behind_imag = behind_real
    for p in range(devices):
        real = imag = None
        for q in range(p + 1):
            a, b = blocks[q][0], blocks[q][1]
            c, d = blocks[p - q][2], blocks[p - q][3]
            term_real, term_imag = a * c - b * d, a * d + b * c
            real = term_real if real is None else real + term_real
            imag = term_imag if imag is None else imag + term_imag
        out_ref[p] = jnp.concatenate([real - behind_imag, imag + behind_real], axis=0).astype(BF16)
        behind_real, behind_imag = real, imag


def inverse_kernel(devices, skip_ref, spectra_ref, turn_ref, second_ref, first_ref, q_feat_ref, product_ref, heads_ref,
                   gating_ref):
    rows = q_feat_ref.shape[0]
    per = rows // devices
    packed = jnp.concatenate(
        [spectra_ref[:, :per, :].astype(F32), spectra_ref[:, per:, :].astype(F32)], axis=2
    )
    values = dot(packed.reshape(rows, 2 * LANES).astype(BF16), second_ref[...])
    a, b = values[:, :LANES], values[:, LANES:]
    turn_real, turn_imag = turn_ref[0], turn_ref[1]
    turned = jnp.concatenate([a * turn_real - b * turn_imag, a * turn_imag + b * turn_real], axis=0)
    convolved = dot(first_ref[...], turned.astype(BF16))
    head = head_mask((rows, LANES))
    heads = heads_ref[...]
    product = jnp.where(head, heads[0:1] * heads[2:3], product_ref[...])
    q_feat = jnp.where(head, heads[4:5], q_feat_ref[...].astype(F32))
    gating = (q_feat * (convolved + skip_ref[0] * product)).astype(BF16)
    for copy in range(gating_ref.shape[0]):
        gating_ref[copy] = gating


def mix_kernel(weights_ref, gating_ref, own_ref, other_ref):
    count = gating_ref.shape[0]
    own = other = None
    for c in range(count):
        gating = gating_ref[c].astype(F32)
        to_own, to_other = weights_ref[c] * gating, weights_ref[count + c] * gating
        own = to_own if own is None else own + to_own
        other = to_other if other is None else other + to_other
    own_ref[...] = own
    other_ref[...] = other.astype(BF16)


def add_kernel(own_ref, other_ref, out_ref):
    out_ref[...] = (own_ref[...] + other_ref[...].astype(F32)).reshape(out_ref.shape).astype(BF16)


SMEM = pl.BlockSpec(memory_space=pltpu.SMEM)
VMEM = pl.BlockSpec(memory_space=pltpu.VMEM)
HBM = pl.BlockSpec(memory_space=pl.ANY)
PARAMS = pltpu.CompilerParams(vmem_limit_bytes=VMEM_LIMIT)


def on_device(devices, chans, query_in, key_in, value_in, short_taps, long_filter, skip_gain, w_out):
    width = query_in.shape[1]
    rows = width // LANES
    per = rows // devices
    near = chans // 2
    forward_first, turn, forward_second, inverse_second, inverse_first, basis = tables(rows, devices)
    taps = short_taps[:, 0]
    message, q_feat, product = pl.pallas_call(
        functools.partial(forward_kernel, devices),
        in_specs=[SMEM] + [HBM] * 7,
        out_specs=[VMEM] * 3,
        out_shape=[
            jax.ShapeDtypeStruct((devices, 4 * per + 8, LANES), BF16),
            jax.ShapeDtypeStruct((rows, LANES), BF16),
            jax.ShapeDtypeStruct((rows, LANES), F32),
        ],
        scratch_shapes=[
            pltpu.VMEM((1, width), BF16),
            pltpu.VMEM((1, width), BF16),
            pltpu.VMEM((1, width), BF16),
            pltpu.VMEM((rows, LANES), F32),
            pltpu.VMEM(forward_first.shape, BF16),
            pltpu.VMEM(turn.shape, F32),
            pltpu.VMEM(forward_second.shape, BF16),
            pltpu.SemaphoreType.DMA((7,)),
        ],
        compiler_params=PARAMS,
        name="forward",
    )(taps, query_in, key_in, value_in, long_filter.reshape(rows, LANES), forward_first, turn, forward_second)
    message = lax.all_to_all(message, "seq", 0, 0)
    spectra, heads = pl.pallas_call(
        functools.partial(middle_kernel, devices),
        in_specs=[SMEM, VMEM, VMEM],
        out_specs=[VMEM] * 2,
        out_shape=[
            jax.ShapeDtypeStruct((devices, 2 * per, LANES), BF16),
            jax.ShapeDtypeStruct((8, LANES), F32),
        ],
        scratch_shapes=[pltpu.VMEM((devices, 8, LANES), F32)],
        compiler_params=PARAMS,
        name="middle",
    )(taps, message, basis)
    spectra = lax.all_to_all(spectra, "seq", 0, 0)
    gating = pl.pallas_call(
        functools.partial(inverse_kernel, devices),
        in_specs=[SMEM] + [VMEM] * 7,
        out_specs=VMEM,
        out_shape=jax.ShapeDtypeStruct((near, rows, LANES), BF16),
        compiler_params=PARAMS,
        name="inverse",
    )(skip_gain, spectra, turn, inverse_second, inverse_first, q_feat, product, heads)
    groups = [list(range(near)), list(range(near, chans))]
    gathered = lax.all_to_all(gating, "chan", 0, 0, axis_index_groups=groups)
    own_chan = lax.axis_index("chan")
    weights = lax.dynamic_slice_in_dim(w_out.astype(F32), own_chan // near * near, near, axis=0)
    weights = jnp.concatenate(
        [
            lax.dynamic_index_in_dim(weights, column, axis=1, keepdims=False)
            for column in (own_chan, (own_chan + near) % chans)
        ]
    )
    own, other = pl.pallas_call(
        mix_kernel,
        in_specs=[SMEM, VMEM],
        out_specs=[VMEM] * 2,
        out_shape=[jax.ShapeDtypeStruct((rows, LANES), F32), jax.ShapeDtypeStruct((rows, LANES), BF16)],
        compiler_params=PARAMS,
        name="mix",
    )(weights, gathered)
    other = lax.ppermute(other, "chan", [(c, (c + near) % chans) for c in range(chans)])
    return pl.pallas_call(
        add_kernel,
        in_specs=[VMEM] * 2,
        out_specs=VMEM,
        out_shape=jax.ShapeDtypeStruct((1, width), BF16),
        compiler_params=PARAMS,
        name="add",
    )(own, other)


def solution(mesh):
    return jax.shard_map(
        functools.partial(on_device, mesh.shape["seq"], mesh.shape["chan"]),
        mesh=mesh,
        in_specs=(
            P("chan", "seq"),
            P("chan", "seq"),
            P("chan", "seq"),
            P(None, "chan", None),
            P("chan", "seq"),
            P("chan"),
            P(),
        ),
        out_specs=P("chan", "seq"),
        check_vma=False,
    )
```

time: 75 us -> 68.2 us (0.909)
  the two profiles are of different devices: /device:TPU:32 before, /device:TPU:2 now
where the time goes in v1:
time: 68.2 us; the launch traced here: 67.7 us
  blocking collectives  19 us (28%)
  waiting for transfers between devices  17.2 us (25%)
  starting transfers between devices  15.3 us (22%)
  local copies, waits for them, and re-layouts  8.02 us (12%)
  Pallas kernels  7.4 us (11%)
  between operations  0.71 us (1%)
    all_to_all x1, blocking collectives, on_device(): message = lax.all_to_all(message, 'seq', 0, 0)  19 us
    unnamed x25, local copies, waits for them, and re-layouts  7.8 us
    all_to_all x1, waiting for transfers between devices, on_device(): spectra = lax.all_to_all(spectra, 'seq', 0, 0)  7.12 us
    all_to_all x1, starting transfers between devices, on_device(): spectra = lax.all_to_all(spectra, 'seq', 0, 0)  6.3 us
    all_to_all x1, waiting for transfers between devices, on_device(): gathered = lax.all_to_all(gating, 'chan', 0, 0, axis_index_groups=groups)  5.7 us
    ppermute x1, starting transfers between devices, on_device(): lax.ppermute(other, 'chan', [(c, (c + near) % chans) for c in range(chans)])  4.58 us
    all_to_all x1, starting transfers between devices, on_device(): gathered = lax.all_to_all(gating, 'chan', 0, 0, axis_index_groups=groups)  4.46 us
    ppermute x1, waiting for transfers between devices, on_device(): lax.ppermute(other, 'chan', [(c, (c + near) % chans) for c in range(chans)])  4.35 us
  transfers between devices with their start and end apart: 3, of which 3 were waited for; matrix products, arithmetic and copies ran while one was open for 0% of the time, Pallas kernels for 0%

profile of v1, /device:TPU:2, one launch (start us, length us, event | category | flops | bytes accessed | tf_op | source)
XLA Modules:
  0.0 67.7 jit_solution(1381298804959514659)
XLA Ops:
  0.0 0.7 %copy.16 = f32[3,1,3]{2,0,1:T(4,128)S(1)} copy(f32[3,1,3]{2,1,0:T(1,128)} %param.16) | data formatting | bytes 72
  0.7 0.0 copy-start
  0.7 0.9 %copy-done = f32[2,256,128]{2,1,0:T(8,128)S(1)} copy-done((f32[2,256,128]{2,1,0:T(8,128)S(1)}, f32[2,256,128]{2,1,0:T(8,128)}, u32[]{:S(2)}) %copy-start) | copy-done | bytes 262168
  1.6 0.0 copy-start.3
  1.6 0.9 %copy-done.3 = bf16[512,256]{1,0:T(8,128)(2,1)S(1)} copy-done((bf16[512,256]{1,0:T(8,128)(2,1)S(1)}, bf16[512,256]{1,0:T(8,128)(2,1)}, u32[]{:S(2)}) %copy-start.3) | copy-done | bytes 262168
  2.6 0.0 copy-start.4
  2.6 0.9 %copy-done.4 = bf16[1,32768]{1,0:T(2,128)(2,1)S(1)} copy-done((bf16[1,32768]{1,0:T(2,128)(2,1)S(1)}, bf16[1,32768]{1,0:T(2,128)(2,1)}, u32[]{:S(2)}) %copy-start.4) | copy-done | bytes 65560
  3.5 0.0 copy-start.5
  3.5 0.9 %copy-done.5 = bf16[1,32768]{1,0:T(2,128)(2,1)S(1)} copy-done((bf16[1,32768]{1,0:T(2,128)(2,1)S(1)}, bf16[1,32768]{1,0:T(2,128)(2,1)}, u32[]{:S(2)}) %copy-start.5) | copy-done | bytes 65560
  4.4 0.0 copy-start.6
  4.4 0.9 %copy-done.6 = bf16[1,32768]{1,0:T(2,128)(2,1)S(1)} copy-done((bf16[1,32768]{1,0:T(2,128)(2,1)S(1)}, bf16[1,32768]{1,0:T(2,128)(2,1)}, u32[]{:S(2)}) %copy-start.6) | copy-done | bytes 65560
  5.3 0.0 copy-start.7
  5.3 0.9 %copy-done.7 = f32[1,32768]{1,0:T(1,128)S(1)} copy-done((f32[1,32768]{1,0:T(1,128)S(1)}, f32[1,32768]{1,0:T(1,128)}, u32[]{:S(2)}) %copy-start.7) | copy-done | bytes 131096
  6.2 0.0 copy-start.9
  6.2 0.9 %copy-done.9 = bf16[256,256]{1,0:T(8,128)(2,1)S(1)} copy-done((bf16[256,256]{1,0:T(8,128)(2,1)S(1)}, bf16[256,256]{1,0:T(8,128)(2,1)}, u32[]{:S(2)}) %copy-start.9) | copy-done | bytes 131096
  7.1 2.8 %forward.1 = (bf16[32,40,128]{2,1,0:T(8,128)(2,1)S(1)}, bf16[256,128]{1,0:T(8,128)(2,1)S(1)}, f32[256,128]{1,0:T(8,128)S(1)}) custom-call(f32[3,3]{1,0:T(4,128)S(1)} %bitcast.5, bf16[1,32768]{1,0:T(2,128)(2,1)S(1)} %copy-done.4, bf16[1,32768]{1,0:T(2,128)(2,1)S(1)} %copy-done.5, bf16[1,32768]{1,0:T(2,128)(2,1)S(1)} %copy-done.6, f32[256,128]{1,0:T(8,128)S(1)} %bitcast.4, ...), custom_call_target="tpu_custom_call" | custom-call | tf_op jit(solution)/shard_map/forward/pallas_call | solution.py:240
  9.9 0.0 copy-start.10
  9.9 0.0 copy-start.8
  9.9 19.0 %all_to_all.15.message_ref = bf16[32,40,128]{2,1,0:T(8,128)(2,1)S(1)} all-to-all(bf16[32,40,128]{2,1,0:T(8,128)(2,1)S(1)} %get-tuple-element.12), channel_id=1, replica_groups=mesh['seq'=32,'chan'=8] {'seq'}, dimensions={0} | all-to-all | bytes 655360 | tf_op jit(solution)/shard_map/all_to_all | solution.py:262
  28.9 0.0 copy-done.10
  28.9 0.0 copy-start.1
  28.9 0.0 copy-start.2
  28.9 2.1 %middle.1 = (bf16[32,16,128]{2,1,0:T(8,128)(2,1)}, f32[8,128]{1,0:T(8,128)S(1)}) custom-call(f32[3,3]{1,0:T(4,128)S(1)} %bitcast.6, bf16[32,40,128]{2,1,0:T(8,128)(2,1)S(1)} %all_to_all.15.message_ref, f32[2,8,128]{2,1,0:T(8,128)S(1)} %copy-done.10), custom_call_target="tpu_custom_call" | custom-call | tf_op jit(solution)/shard_map/middle/pallas_call | solution.py:263
  31.0 6.3 %all-to-all-start.1 = ((bf16[32,16,128]{2,1,0:T(8,128)(2,1)}), bf16[32,16,128]{2,1,0:T(8,128)(2,1)S(1)}, u32[]{:S(2)}, u32[]{:S(2)}) async-start(bf16[32,16,128]{2,1,0:T(8,128)(2,1)} %get-tuple-element.13), calls=%async_computation.1 | async-start | bytes 262144 | tf_op jit(solution)/shard_map/all_to_all | solution.py:275
  37.9 7.1 %all-to-all-done.1.spectra_ref = bf16[32,16,128]{2,1,0:T(8,128)(2,1)S(1)} async-done(((bf16[32,16,128]{2,1,0:T(8,128)(2,1)}), bf16[32,16,128]{2,1,0:T(8,128)(2,1)S(1)}, u32[]{:S(2)}, u32[]{:S(2)}) %all-to-all-start.1) | async-done | bytes 131104 | tf_op jit(solution)/shard_map/all_to_all | solution.py:275
  45.0 0.0 copy-done.8
  45.0 0.0 copy-done.1
  45.0 0.0 copy-done.2
  45.0 1.2 %inverse.1 = bf16[4,256,128]{2,1,0:T(8,128)(2,1)} custom-call(f32[1]{0:T(128)S(6)} %copy.17.skip_ref, bf16[32,16,128]{2,1,0:T(8,128)(2,1)S(1)} %all-to-all-done.1.spectra_ref, f32[2,256,128]{2,1,0:T(8,128)S(1)} %copy-done.1, bf16[256,256]{1,0:T(8,128)(2,1)S(1)} %copy-done.8, bf16[256,512]{1,0:T(8,128)(2,1)S(1)} %copy-done.2, ...), custom_call_target="tpu_custom_call" | custom-call | tf_op jit(solution)/shard_map/inverse/pallas_call | solution.py:276
  46.2 4.5 %all-to-all-start.2 = ((bf16[4,256,128]{2,1,0:T(8,128)(2,1)}), bf16[4,256,128]{2,1,0:T(8,128)(2,1)S(1)}, u32[]{:S(2)}, u32[]{:S(2)}) async-start(bf16[4,256,128]{2,1,0:T(8,128)(2,1)} %inverse.1), calls=%async_computation.2 | async-start | bytes 524288 | tf_op jit(solution)/shard_map/all_to_all | solution.py:285
  50.7 0.0 copy-start.11
  50.7 0.7 %copy-done.11 = bf16[8,8]{1,0:T(8,128)(2,1)S(1)} copy-done((bf16[8,8]{1,0:T(8,128)(2,1)S(1)}, bf16[8,8]{1,0:T(8,128)(2,1)}, u32[]{:S(2)}) %copy-start.11) | copy-done | bytes 152
  51.4 0.2 dynamic-slice_reduce_fusion.1
  51.6 0.1 pad_maximum_fusion.weights_ref
  51.6 5.7 %all-to-all-done.2.gating_ref = bf16[4,256,128]{2,1,0:T(8,128)(2,1)S(1)} async-done(((bf16[4,256,128]{2,1,0:T(8,128)(2,1)}), bf16[4,256,128]{2,1,0:T(8,128)(2,1)S(1)}, u32[]{:S(2)}, u32[]{:S(2)}) %all-to-all-start.2) | async-done | bytes 262176 | tf_op jit(solution)/shard_map/all_to_all | solution.py:285
  57.3 0.6 mix.1
  58.0 4.6 %collective-permute-start = (bf16[256,128]{1,0:T(8,128)(2,1)S(1)}, bf16[256,128]{1,0:T(8,128)(2,1)S(1)}, u32[]{:S(2)}, u32[]{:S(2)}) collective-permute-start(bf16[256,128]{1,0:T(8,128)(2,1)S(1)} %get-tuple-element.18), channel_id=1, source_target_pairs={{0,4},{1,5},{2,6},{3,7},{4,0},{5,1},{6,2},{7,3},{8,12},{9,13},{10,... | collective-permute-start | bytes 196616 | tf_op jit(solution)/shard_map/ppermute | solution.py:302
  62.6 4.4 %collective-permute-done.other_ref = bf16[256,128]{1,0:T(8,128)(2,1)S(1)} collective-permute-done((bf16[256,128]{1,0:T(8,128)(2,1)S(1)}, bf16[256,128]{1,0:T(8,128)(2,1)S(1)}, u32[]{:S(2)}, u32[]{:S(2)}) %collective-permute-start) | collective-permute-done | bytes 65568 | tf_op jit(solution)/shard_map/ppermute | solution.py:302
  66.9 0.8 %add.30 = bf16[1,32768]{1,0:T(2,128)(2,1)} custom-call(f32[256,128]{1,0:T(8,128)S(1)} %get-tuple-element.17.own_ref, bf16[256,128]{1,0:T(8,128)(2,1)S(1)} %collective-permute-done.other_ref), custom_call_target="tpu_custom_call" | custom-call | tf_op jit(solution)/shard_map/add/pallas_call | solution.py:303
  (1 shorter events, 0.0 us)
Async XLA Ops:
  0.7 0.9 %copy-start = (f32[2,256,128]{2,1,0:T(8,128)S(1)}, f32[2,256,128]{2,1,0:T(8,128)}, u32[]{:S(2)}) copy-start(f32[2,256,128]{2,1,0:T(8,128)} %constant.73.clone.turn_hbm.turn_ref) | copy-start | bytes 786436
  1.6 0.9 %copy-start.3 = (bf16[512,256]{1,0:T(8,128)(2,1)S(1)}, bf16[512,256]{1,0:T(8,128)(2,1)}, u32[]{:S(2)}) copy-start(bf16[512,256]{1,0:T(8,128)(2,1)} %constant.72.clone.first_hbm) | copy-start | bytes 786436
  2.6 0.9 %copy-start.4 = (bf16[1,32768]{1,0:T(2,128)(2,1)S(1)}, bf16[1,32768]{1,0:T(2,128)(2,1)}, u32[]{:S(2)}) copy-start(bf16[1,32768]{1,0:T(2,128)(2,1)} %q_hbm.1) | copy-start | bytes 196612
  3.5 0.9 %copy-start.5 = (bf16[1,32768]{1,0:T(2,128)(2,1)S(1)}, bf16[1,32768]{1,0:T(2,128)(2,1)}, u32[]{:S(2)}) copy-start(bf16[1,32768]{1,0:T(2,128)(2,1)} %k_hbm.1) | copy-start | bytes 196612
  4.4 0.9 %copy-start.6 = (bf16[1,32768]{1,0:T(2,128)(2,1)S(1)}, bf16[1,32768]{1,0:T(2,128)(2,1)}, u32[]{:S(2)}) copy-start(bf16[1,32768]{1,0:T(2,128)(2,1)} %v_hbm.1) | copy-start | bytes 196612
  5.3 0.9 %copy-start.7 = (f32[1,32768]{1,0:T(1,128)S(1)}, f32[1,32768]{1,0:T(1,128)}, u32[]{:S(2)}) copy-start(f32[1,32768]{1,0:T(1,128)} %param.17) | copy-start | bytes 393220
  6.2 0.9 %copy-start.9 = (bf16[256,256]{1,0:T(8,128)(2,1)S(1)}, bf16[256,256]{1,0:T(8,128)(2,1)}, u32[]{:S(2)}) copy-start(bf16[256,256]{1,0:T(8,128)(2,1)} %constant.74.clone.second_hbm) | copy-start | bytes 393220
  9.9 19.0 %copy-start.10 = (f32[2,8,128]{2,1,0:T(8,128)S(1)}, f32[2,8,128]{2,1,0:T(8,128)}, u32[]{:S(2)}) copy-start(f32[2,8,128]{2,1,0:T(8,128)} %constant.75.clone.basis_ref) | copy-start | bytes 24580
  9.9 35.1 %copy-start.8 = (bf16[256,256]{1,0:T(8,128)(2,1)S(1)}, bf16[256,256]{1,0:T(8,128)(2,1)}, u32[]{:S(2)}) copy-start(bf16[256,256]{1,0:T(8,128)(2,1)} %constant.76.clone.second_ref) | copy-start | bytes 393220
  28.9 16.1 %copy-start.1 = (f32[2,256,128]{2,1,0:T(8,128)S(1)}, f32[2,256,128]{2,1,0:T(8,128)}, u32[]{:S(2)}) copy-start(f32[2,256,128]{2,1,0:T(8,128)} %constant.73.clone.turn_hbm.turn_ref) | copy-start | bytes 786436
  28.9 16.1 %copy-start.2 = (bf16[256,512]{1,0:T(8,128)(2,1)S(1)}, bf16[256,512]{1,0:T(8,128)(2,1)}, u32[]{:S(2)}) copy-start(bf16[256,512]{1,0:T(8,128)(2,1)} %constant.77.clone.first_ref) | copy-start | bytes 786436
  31.0 14.1 %all-to-all-start.1 = ((bf16[32,16,128]{2,1,0:T(8,128)(2,1)}), bf16[32,16,128]{2,1,0:T(8,128)(2,1)S(1)}, u32[]{:S(2)}, u32[]{:S(2)}) async-start(bf16[32,16,128]{2,1,0:T(8,128)(2,1)} %get-tuple-element.13), calls=%async_computation.1 | async-start | bytes 262144 | tf_op jit(solution)/shard_map/all_to_all | solution.py:275
  46.2 11.1 %all-to-all-start.2 = ((bf16[4,256,128]{2,1,0:T(8,128)(2,1)}), bf16[4,256,128]{2,1,0:T(8,128)(2,1)S(1)}, u32[]{:S(2)}, u32[]{:S(2)}) async-start(bf16[4,256,128]{2,1,0:T(8,128)(2,1)} %inverse.1), calls=%async_computation.2 | async-start | bytes 524288 | tf_op jit(solution)/shard_map/all_to_all | solution.py:285
  50.7 0.7 %copy-start.11 = (bf16[8,8]{1,0:T(8,128)(2,1)S(1)}, bf16[8,8]{1,0:T(8,128)(2,1)}, u32[]{:S(2)}) copy-start(bf16[8,8]{1,0:T(8,128)(2,1)} %param.19) | copy-start | bytes 388
  58.0 8.9 %collective-permute-start = (bf16[256,128]{1,0:T(8,128)(2,1)S(1)}, bf16[256,128]{1,0:T(8,128)(2,1)S(1)}, u32[]{:S(2)}, u32[]{:S(2)}) collective-permute-start(bf16[256,128]{1,0:T(8,128)(2,1)S(1)} %get-tuple-element.18), channel_id=1, source_target_pairs={{0,4},{1,5},{2,6},{3,7},{4,0},{5,1},{6,2},{7,3},{8,12},{9,13},{10,... | collective-permute-start | bytes 196616 | tf_op jit(solution)/shard_map/ppermute | solution.py:302

commit v2 on v1

--- a/solution.py
+++ b/solution.py
@@ -61,30 +61,35 @@
     once = shifted(signal, before, lane, row)
     twice = shifted(once, pltpu.roll(before, 1, 1), lane, row)
     summed = (
-        taps_ref[stream, 0] * signal + taps_ref[stream, 1] * once + taps_ref[stream, 2] * twice
+        taps_ref[stream, 0, 0] * signal + taps_ref[stream, 0, 1] * once + taps_ref[stream, 0, 2] * twice
     )
     return summed.astype(BF16)
 
 
-def head_mask(shape):
-    lane = lax.broadcasted_iota(jnp.int32, shape, len(shape) - 1)
-    row = lax.broadcasted_iota(jnp.int32, shape, len(shape) - 2)
-    return (row == 0) & (lane < 2)
-
-
-def forward_kernel(devices, taps_ref, q_hbm, k_hbm, v_hbm, filter_hbm, first_hbm, turn_hbm, second_hbm,
-                   message_ref, q_feat_ref, product_ref,
-                   q_ref, k_ref, v_ref, filter_ref, first_ref, turn_ref, second_ref, sems):
+def at_lanes(values, first):
+    return pltpu.roll(values, first, 1) if first else values
+
+
+def forward_kernel(devices, taps_ref, skip_ref, q_hbm, k_hbm, v_hbm, filter_hbm, first_hbm, turn_hbm, second_hbm, w_hbm,
+                   message_ref, q_feat_ref, skipped_ref, scalars_ref,
+                   q_ref, k_ref, v_ref, filter_ref, first_ref, turn_ref, second_ref, w_ref, sems):
     pairs = (
         (k_hbm, k_ref), (v_hbm, v_ref), (filter_hbm, filter_ref), (first_hbm, first_ref),
-        (q_hbm, q_ref), (turn_hbm, turn_ref), (second_hbm, second_ref),
+        (q_hbm, q_ref), (turn_hbm, turn_ref), (second_hbm, second_ref), (w_hbm, w_ref),
     )
     copies = [pltpu.make_async_copy(source, target, sems.at[i]) for i, (source, target) in enumerate(pairs)]
     for copy in copies:
         copy.start()
-    rows = product_ref.shape[0]
+    rows = q_feat_ref.shape[0]
     per = rows // devices
+    own, own_chan = lax.axis_index("seq"), lax.axis_index("chan")
     nothing = jnp.zeros((1, LANES), F32)
+    lane = lax.broadcasted_iota(jnp.int32, (1, LANES), 1)
+    for j in range(3):
+        scalars_ref[j : j + 1, :] = jnp.where(
+            lane < 4, taps_ref[1, 0, j], jnp.where(lane < 8, taps_ref[2, 0, j], taps_ref[0, 0, j])
+        )
+    scalars_ref[3:4, :] = jnp.full((1, LANES), skip_ref[0], F32)
     copies[0].wait()
     key = k_ref[...].astype(F32).reshape(rows, LANES)
     k_feat = featurized(key, nothing, taps_ref, 1)
@@ -92,7 +97,7 @@
     value = v_ref[...].astype(F32).reshape(rows, LANES)
     v_feat = featurized(value, nothing, taps_ref, 2)
     product = k_feat.astype(F32) * v_feat.astype(F32)
-    product_ref[...] = product
+    skipped_ref[...] = skip_ref[0] * product
     copies[2].wait()
     signals = jnp.concatenate([product, filter_ref[...]], axis=1).astype(BF16)
     copies[3].wait()
@@ -100,8 +105,12 @@
     copies[4].wait()
     query = q_ref[...].astype(F32).reshape(rows, LANES)
     q_feat_ref[...] = featurized(query, nothing, taps_ref, 0)
-    rims = [a[r : r + 1] for a in (key, value, query) for r in (0, rows - 1)]
-    rims = jnp.concatenate(rims + [nothing, nothing], axis=0)
+    edges = nothing
+    for first, signal in enumerate((key, value, query)):
+        ends = jnp.where(lane < 2, signal[:1], jnp.where(lane < LANES - 2, 0.0, signal[rows - 1 :]))
+        edges = edges + at_lanes(ends, 4 * first)
+    row = lax.broadcasted_iota(jnp.int32, (8, LANES), 0)
+    edges = jnp.where(row == own % 8, jnp.broadcast_to(edges, (8, LANES)), 0.0)
     copies[5].wait()
     real, imag = values[:, 0], values[:, 1]
     turn_real = turn_ref[0].reshape(devices, per, LANES)
@@ -122,41 +131,47 @@
             spectra[:, :per, LANES:],
             spectra[:, per:, :LANES],
             spectra[:, per:, LANES:],
-            jnp.broadcast_to(rims[None], (devices, 8, LANES)),
+            jnp.broadcast_to(edges[None], (devices, 8, LANES)),
         ],
         axis=1,
     ).astype(BF16)
+    copies[7].wait()
+    chans = w_ref.shape[0]
+    weights = w_ref[...].astype(F32)
+    column = lax.broadcasted_iota(jnp.int32, weights.shape, 1)
+    for i, chan in enumerate((own_chan, (own_chan + chans // 2) % chans)):
+        picked = jnp.sum(jnp.where(column == chan, weights, 0.0), axis=1, keepdims=True)
+        scalars_ref[8 + i * chans : 8 + (i + 1) * chans, :] = jnp.broadcast_to(picked, (chans, LANES))
 
 
 def rounded(values):
     return values.astype(BF16).astype(F32)
 
 
-def head_features(rims, taps_ref):
-    lane = lax.broadcasted_iota(jnp.int32, rims.shape, 2)
-    row = lax.broadcasted_iota(jnp.int32, rims.shape[1:], 0)[None]
-    taps = [
-        jnp.where(row < 2, taps_ref[1, j], jnp.where(row < 4, taps_ref[2, j], taps_ref[0, j])) for j in range(3)
-    ]
-    before = jnp.concatenate([jnp.zeros_like(rims[:1]), rims[:-1]], axis=0)
-    before = pltpu.roll(before, rims.shape[1] - 1, 1)
-    once, twice = pltpu.roll(rims, 1, 2), pltpu.roll(rims, 2, 2)
-    with_before = (
-        taps[0] * rims
-        + taps[1] * jnp.where(lane < 1, pltpu.roll(before, 1, 2), once)
-        + taps[2] * jnp.where(lane < 2, pltpu.roll(before, 2, 2), twice)
-    )
-    alone = taps[0] * rims + taps[1] * jnp.where(lane < 1, 0.0, once) + taps[2] * jnp.where(lane < 2, 0.0, twice)
-    return rounded(with_before), rounded(alone)
-
-
-def middle_kernel(devices, taps_ref, message_ref, basis_ref, out_ref, heads_ref, heads_scratch):
+def middle_kernel(devices, scalars_ref, message_ref, basis_ref, out_ref, heads_ref, heads_scratch, error_scratch):
     per = (message_ref.shape[1] - 8) // 4
     own = lax.axis_index("seq")
-    heads, alone = head_features(message_ref[:, 4 * per :, :].astype(F32), taps_ref)
-    heads_scratch[...] = heads
-    heads_ref[...] = heads_scratch[own]
-    error = heads * pltpu.roll(heads, 6, 1) - alone * pltpu.roll(alone, 6, 1)
+    groups = [
+        sum(message_ref[p, 4 * per :, :].astype(F32) for p in range(group, group + 8)) for group in range(0, devices, 8)
+    ]
+    edges = jnp.concatenate(groups, axis=0)
+    before = jnp.concatenate([jnp.zeros((1, LANES), F32), edges[:-1]], axis=0)
+    lane = lax.broadcasted_iota(jnp.int32, edges.shape, 1)
+    taps = [scalars_ref[j : j + 1, :] for j in range(3)]
+    once = pltpu.roll(edges, 1, 1)
+    alone = taps[0] * edges + taps[1] * jnp.where(lane % 4 == 0, 0.0, once)
+    once = jnp.where(lane % 4 == 0, pltpu.roll(before, 1, 1), once)
+    heads = rounded(taps[0] * edges + taps[1] * once + taps[2] * pltpu.roll(before, 2, 1))
+    alone = rounded(alone)
+    product = heads * pltpu.roll(heads, LANES - 4, 1)
+    error = product - alone * pltpu.roll(alone, LANES - 4, 1)
+    error = jnp.where(lax.broadcasted_iota(jnp.int32, edges.shape, 0) == 0, 0.0, error)
+    for i in range(2):
+        error_scratch[i] = jnp.broadcast_to(error[:, i : i + 1], edges.shape)
+    heads_scratch[0] = pltpu.roll(heads, LANES - 8, 1)
+    heads_scratch[1] = scalars_ref[3:4, :] * product
+    for i in range(2):
+        heads_ref[i : i + 1, :] = heads_scratch[i, pl.ds(own, 1), :]
     angle = jnp.full((per, LANES), own, jnp.int32).astype(F32) * (2.0 * math.pi / (devices * LANES))
     square = angle * angle
     cos = 1.0 - square * (0.5 - square * (1.0 / 24.0))
@@ -169,8 +184,8 @@
         block = message_ref[p].astype(F32)
         real, imag = block[:per], block[per : 2 * per]
         if p > 0:
-            zeroth, first = error[p, 0:1, 0:1], error[p, 0:1, 1:2]
-            real = real + (zeroth + first * point_real)
+            first = error_scratch[1, p : p + 1, :]
+            real = real + (error_scratch[0, p : p + 1, :] + first * point_real)
             imag = imag + first * point_imag
         blocks.append((real, imag, block[2 * per : 3 * per], block[3 * per : 4 * per]))
     behind_real = jnp.zeros((per, LANES), F32)
@@ -187,8 +202,7 @@
         behind_real, behind_imag = real, imag
 
 
-def inverse_kernel(devices, skip_ref, spectra_ref, turn_ref, second_ref, first_ref, q_feat_ref, product_ref, heads_ref,
-                   gating_ref):
+def inverse_kernel(devices, spectra_ref, turn_ref, second_ref, first_ref, q_feat_ref, skipped_ref, heads_ref, gating_ref):
     rows = q_feat_ref.shape[0]
     per = rows // devices
     packed = jnp.concatenate(
@@ -199,21 +213,25 @@
     turn_real, turn_imag = turn_ref[0], turn_ref[1]
     turned = jnp.concatenate([a * turn_real - b * turn_imag, a * turn_imag + b * turn_real], axis=0)
     convolved = dot(first_ref[...], turned.astype(BF16))
-    head = head_mask((rows, LANES))
-    heads = heads_ref[...]
-    product = jnp.where(head, heads[0:1] * heads[2:3], product_ref[...])
-    q_feat = jnp.where(head, heads[4:5], q_feat_ref[...].astype(F32))
-    gating = (q_feat * (convolved + skip_ref[0] * product)).astype(BF16)
+    lane = lax.broadcasted_iota(jnp.int32, (rows, LANES), 1)
+    row = lax.broadcasted_iota(jnp.int32, (rows, LANES), 0)
+    head = (row == 0) & (lane < 2)
+    q_feat = jnp.where(head, heads_ref[0:1, :], q_feat_ref[...].astype(F32))
+    skipped = jnp.where(head, heads_ref[1:2, :], skipped_ref[...])
+    gating = (q_feat * (convolved + skipped)).astype(BF16)
     for copy in range(gating_ref.shape[0]):
         gating_ref[copy] = gating
 
 
-def mix_kernel(weights_ref, gating_ref, own_ref, other_ref):
-    count = gating_ref.shape[0]
+def mix_kernel(scalars_ref, gating_ref, own_ref, other_ref):
+    near = gating_ref.shape[0]
+    chans = 2 * near
+    start = 8 + lax.axis_index("chan") // near * near
     own = other = None
-    for c in range(count):
+    for c in range(near):
         gating = gating_ref[c].astype(F32)
-        to_own, to_other = weights_ref[c] * gating, weights_ref[count + c] * gating
+        to_own = scalars_ref[pl.ds(start + c, 1), :] * gating
+        to_other = scalars_ref[pl.ds(start + chans + c, 1), :] * gating
         own = to_own if own is None else own + to_own
         other = to_other if other is None else other + to_other
     own_ref[...] = own
@@ -226,7 +244,7 @@
 
 SMEM = pl.BlockSpec(memory_space=pltpu.SMEM)
 VMEM = pl.BlockSpec(memory_space=pltpu.VMEM)
-HBM = pl.BlockSpec(memory_space=pl.ANY)
+HBM = pl.BlockSpec(memory_space=pltpu.HBM)
 PARAMS = pltpu.CompilerParams(vmem_limit_bytes=VMEM_LIMIT)
 
 
@@ -236,15 +254,15 @@
     per = rows // devices
     near = chans // 2
     forward_first, turn, forward_second, inverse_second, inverse_first, basis = tables(rows, devices)
-    taps = short_taps[:, 0]
-    message, q_feat, product = pl.pallas_call(
+    message, q_feat, skipped, scalars = pl.pallas_call(
         functools.partial(forward_kernel, devices),
-        in_specs=[SMEM] + [HBM] * 7,
-        out_specs=[VMEM] * 3,
+        in_specs=[SMEM] * 2 + [HBM] * 8,
+        out_specs=[VMEM] * 4,
         out_shape=[
             jax.ShapeDtypeStruct((devices, 4 * per + 8, LANES), BF16),
             jax.ShapeDtypeStruct((rows, LANES), BF16),
             jax.ShapeDtypeStruct((rows, LANES), F32),
+            jax.ShapeDtypeStruct((8 + 2 * chans, LANES), F32),
         ],
         scratch_shapes=[
             pltpu.VMEM((1, width), BF16),
@@ -254,51 +272,54 @@
             pltpu.VMEM(forward_first.shape, BF16),
             pltpu.VMEM(turn.shape, F32),
             pltpu.VMEM(forward_second.shape, BF16),
-            pltpu.SemaphoreType.DMA((7,)),
+            pltpu.VMEM(w_out.shape, BF16),
+            pltpu.SemaphoreType.DMA((8,)),
         ],
         compiler_params=PARAMS,
         name="forward",
-    )(taps, query_in, key_in, value_in, long_filter.reshape(rows, LANES), forward_first, turn, forward_second)
+    )(
+        short_taps,
+        skip_gain,
+        *(
+            pltpu.with_memory_space_constraint(jnp.asarray(operand), pltpu.HBM)
+            for operand in (
+                query_in, key_in, value_in, long_filter.reshape(rows, LANES),
+                forward_first, turn, forward_second, w_out,
+            )
+        ),
+    )
     message = lax.all_to_all(message, "seq", 0, 0)
     spectra, heads = pl.pallas_call(
         functools.partial(middle_kernel, devices),
-        in_specs=[SMEM, VMEM, VMEM],
+        in_specs=[VMEM] * 3,
         out_specs=[VMEM] * 2,
         out_shape=[
             jax.ShapeDtypeStruct((devices, 2 * per, LANES), BF16),
             jax.ShapeDtypeStruct((8, LANES), F32),
         ],
-        scratch_shapes=[pltpu.VMEM((devices, 8, LANES), F32)],
+        scratch_shapes=[pltpu.VMEM((2, devices, LANES), F32)] * 2,
         compiler_params=PARAMS,
         name="middle",
-    )(taps, message, basis)
+    )(scalars, message, basis)
     spectra = lax.all_to_all(spectra, "seq", 0, 0)
     gating = pl.pallas_call(
         functools.partial(inverse_kernel, devices),
-        in_specs=[SMEM] + [VMEM] * 7,
+        in_specs=[VMEM] * 7,
         out_specs=VMEM,
         out_shape=jax.ShapeDtypeStruct((near, rows, LANES), BF16),
         compiler_params=PARAMS,
         name="inverse",
-    )(skip_gain, spectra, turn, inverse_second, inverse_first, q_feat, product, heads)
+    )(spectra, turn, inverse_second, inverse_first, q_feat, skipped, heads)
     groups = [list(range(near)), list(range(near, chans))]
     gathered = lax.all_to_all(gating, "chan", 0, 0, axis_index_groups=groups)
-    own_chan = lax.axis_index("chan")
-    weights = lax.dynamic_slice_in_dim(w_out.astype(F32), own_chan // near * near, near, axis=0)
-    weights = jnp.concatenate(
-        [
-            lax.dynamic_index_in_dim(weights, column, axis=1, keepdims=False)
-            for column in (own_chan, (own_chan + near) % chans)
-        ]
-    )
     own, other = pl.pallas_call(
         mix_kernel,
-        in_specs=[SMEM, VMEM],
+        in_specs=[VMEM] * 2,
         out_specs=[VMEM] * 2,
         out_shape=[jax.ShapeDtypeStruct((rows, LANES), F32), jax.ShapeDtypeStruct((rows, LANES), BF16)],
         compiler_params=PARAMS,
         name="mix",
-    )(weights, gathered)
+    )(scalars, gathered)
     other = lax.ppermute(other, "chan", [(c, (c + near) % chans) for c in range(chans)])
     return pl.pallas_call(
         add_kernel,

time: 68.2 us -> 58.7 us (0.86)
  blocking collectives: 19 us -> 43.7 us
  waiting for transfers between devices: 17.2 us -> 4.36 us
  starting transfers between devices: 15.3 us -> 4.58 us
  local copies, waits for them, and re-layouts: 8.02 us -> 0.04 us
  Pallas kernels: 7.4 us -> 5.11 us
    all_to_all x0 -> x2, blocking collectives: none -> 24.7 us  [the longest x1 13.7 us: on_device(): spectra = lax.all_to_all(spectra, 'seq', 0, 0)]
    all_to_all x2 -> x0, waiting for transfers between devices: 12.8 us -> none  [the longest x1 7.12 us: on_device(): spectra = lax.all_to_all(spectra, 'seq', 0, 0)]
    all_to_all x2 -> x0, starting transfers between devices: 10.8 us -> none  [the longest x1 6.3 us: on_device(): spectra = lax.all_to_all(spectra, 'seq', 0, 0)]
    unnamed x25 -> x10, local copies, waits for them, and re-layouts: 7.8 us -> 0.04 us
    pallas_call x3, Pallas kernels: 3.85 us -> 1.45 us  [the longest x1 0.88 us: on_device(): pl.pallas_call(functools.partial(middle_kernel, devices), in_specs=[VMEM]...]
  transfers between devices with their start and end apart: 3 -> 1, of which waited for: 3 -> 1; matrix products, arithmetic and copies ran while one was open for 0% -> 0% of each run, Pallas kernels for 0% -> 0%
where the time goes in v2:
time: 58.7 us; the launch traced here: 58.5 us
  blocking collectives  43.7 us (74%)
  Pallas kernels  5.11 us (9%)
  starting transfers between devices  4.58 us (8%)
  waiting for transfers between devices  4.36 us (7%)
  between operations  0.72 us (1%)
    all_to_all x1, blocking collectives, on_device(): message = lax.all_to_all(message, 'seq', 0, 0)  19 us
    all_to_all x1, blocking collectives, on_device(): spectra = lax.all_to_all(spectra, 'seq', 0, 0)  13.7 us
    all_to_all x1, blocking collectives, on_device(): gathered = lax.all_to_all(gating, 'chan', 0, 0, axis_index_groups=groups)  10.9 us
    ppermute x1, starting transfers between devices, on_device(): lax.ppermute(other, 'chan', [(c, (c + near) % chans) for c in range(chans)])  4.58 us
    ppermute x1, waiting for transfers between devices, on_device(): lax.ppermute(other, 'chan', [(c, (c + near) % chans) for c in range(chans)])  4.36 us
    pallas_call x1, Pallas kernels, on_device(): pl.pallas_call(functools.partial(forward_kernel, devices), in_specs=[SMEM...  2.9 us
  transfers between devices with their start and end apart: 1, of which 1 were waited for; matrix products, arithmetic and copies ran while one was open for 0% of the time, Pallas kernels for 0%

profile of v2, /device:TPU:2, one launch (start us, length us, event | category | flops | bytes accessed | tf_op | source)
XLA Modules:
  0.0 58.5 jit_solution(5253863190402292536)
XLA Ops:
  0.0 0.0 copy-start.4
  0.7 0.0 copy-done.4
  0.7 2.9 %forward.1 = (bf16[32,40,128]{2,1,0:T(8,128)(2,1)S(1)}, bf16[256,128]{1,0:T(8,128)(2,1)S(1)}, f32[256,128]{1,0:T(8,128)S(1)}, f32[24,128]{1,0:T(8,128)S(1)}) custom-call(f32[3,1,3]{2,1,0:T(1,128)S(1)} %copy-done.4, f32[1]{0:T(128)S(6)} %copy.14.skip_ref, bf16[1,32768]{1,0:T(2,128)(2,1)} %q_hbm.1, bf16[1,32768]{1,0:T(2,128)(2,1)} %k_hbm.1, ...), custom_call_target="tpu_custom_call" | custom-call | tf_op jit(solution)/shard_map/forward/pallas_call | solution.py:257
  3.6 0.0 copy-start.3
  3.6 0.0 copy-start.2
  3.6 19.0 %all_to_all.15.message_ref = bf16[32,40,128]{2,1,0:T(8,128)(2,1)S(1)} all-to-all(bf16[32,40,128]{2,1,0:T(8,128)(2,1)S(1)} %get-tuple-element.14), channel_id=1, replica_groups=mesh['seq'=32,'chan'=8] {'seq'}, dimensions={0} | all-to-all | bytes 655360 | tf_op jit(solution)/shard_map/all_to_all | solution.py:291
  22.6 0.0 copy-done.3
  22.6 0.0 copy-start
  22.6 0.0 copy-start.1
  22.6 0.9 %middle.1 = (bf16[32,16,128]{2,1,0:T(8,128)(2,1)S(1)}, f32[8,128]{1,0:T(8,128)S(1)}) custom-call(f32[24,128]{1,0:T(8,128)S(1)} %get-tuple-element.13.scalars_ref, bf16[32,40,128]{2,1,0:T(8,128)(2,1)S(1)} %all_to_all.15.message_ref, f32[2,8,128]{2,1,0:T(8,128)S(1)} %copy-done.3), custom_call_target="tpu_custom_call" | custom-call | tf_op jit(solution)/shard_map/middle/pallas_call | solution.py:292
  23.5 13.7 %all_to_all.16.spectra_ref = bf16[32,16,128]{2,1,0:T(8,128)(2,1)S(1)} all-to-all(bf16[32,16,128]{2,1,0:T(8,128)(2,1)S(1)} %get-tuple-element.15), channel_id=1, replica_groups=mesh['seq'=32,'chan'=8] {'seq'}, dimensions={0} | all-to-all | bytes 262144 | tf_op jit(solution)/shard_map/all_to_all | solution.py:304
  37.2 0.0 copy-done.2
  37.2 0.0 copy-done
  37.2 0.0 copy-done.1
  37.2 0.5 inverse.1
  37.7 10.9 %all_to_all.17.gating_ref = bf16[4,256,128]{2,1,0:T(8,128)(2,1)S(1)} all-to-all(bf16[4,256,128]{2,1,0:T(8,128)(2,1)S(1)} %inverse.1), channel_id=1, replica_groups={{0,1,2,3},{4,5,6,7},{8,9,10,11},{12,13,14,15},{16,17,18,19},{20,21,22,2..., dimensions={0} | all-to-all | bytes 524288 | tf_op jit(solution)/shard_map/all_to_all | solution.py:314
  48.7 0.1 mix.1
  48.8 4.6 %collective-permute-start = (bf16[256,128]{1,0:T(8,128)(2,1)S(1)}, bf16[256,128]{1,0:T(8,128)(2,1)S(1)}, u32[]{:S(2)}, u32[]{:S(2)}) collective-permute-start(bf16[256,128]{1,0:T(8,128)(2,1)S(1)} %get-tuple-element.20), channel_id=1, source_target_pairs={{0,4},{1,5},{2,6},{3,7},{4,0},{5,1},{6,2},{7,3},{8,12},{9,13},{10,... | collective-permute-start | bytes 196616 | tf_op jit(solution)/shard_map/ppermute | solution.py:323
  53.3 4.4 %collective-permute-done.other_ref = bf16[256,128]{1,0:T(8,128)(2,1)S(1)} collective-permute-done((bf16[256,128]{1,0:T(8,128)(2,1)S(1)}, bf16[256,128]{1,0:T(8,128)(2,1)S(1)}, u32[]{:S(2)}, u32[]{:S(2)}) %collective-permute-start) | collective-permute-done | bytes 65568 | tf_op jit(solution)/shard_map/ppermute | solution.py:323
  57.7 0.8 %add.1 = bf16[1,32768]{1,0:T(2,128)(2,1)} custom-call(f32[256,128]{1,0:T(8,128)S(1)} %get-tuple-element.19.own_ref, bf16[256,128]{1,0:T(8,128)(2,1)S(1)} %collective-permute-done.other_ref), custom_call_target="tpu_custom_call" | custom-call | tf_op jit(solution)/shard_map/add/pallas_call | solution.py:324
Async XLA Ops:
  0.0 0.7 %copy-start.4 = (f32[3,1,3]{2,1,0:T(1,128)S(1)}, f32[3,1,3]{2,1,0:T(1,128)}, u32[]{:S(2)}) copy-start(f32[3,1,3]{2,1,0:T(1,128)} %taps_ref.1) | copy-start | bytes 112
  3.6 19.0 %copy-start.3 = (f32[2,8,128]{2,1,0:T(8,128)S(1)}, f32[2,8,128]{2,1,0:T(8,128)}, u32[]{:S(2)}) copy-start(f32[2,8,128]{2,1,0:T(8,128)} %constant.15.clone.basis_ref) | copy-start | bytes 24580
  3.6 33.6 %copy-start.2 = (bf16[256,256]{1,0:T(8,128)(2,1)S(1)}, bf16[256,256]{1,0:T(8,128)(2,1)}, u32[]{:S(2)}) copy-start(bf16[256,256]{1,0:T(8,128)(2,1)} %constant.16.clone.second_ref) | copy-start | bytes 393220
  22.6 14.6 %copy-start = (f32[2,256,128]{2,1,0:T(8,128)S(1)}, f32[2,256,128]{2,1,0:T(8,128)}, u32[]{:S(2)}) copy-start(f32[2,256,128]{2,1,0:T(8,128)} %constant.13.clone.turn_hbm.turn_ref) | copy-start | bytes 786436
  22.6 14.6 %copy-start.1 = (bf16[256,512]{1,0:T(8,128)(2,1)S(1)}, bf16[256,512]{1,0:T(8,128)(2,1)}, u32[]{:S(2)}) copy-start(bf16[256,512]{1,0:T(8,128)(2,1)} %constant.17.clone.first_ref) | copy-start | bytes 786436
  48.8 8.9 %collective-permute-start = (bf16[256,128]{1,0:T(8,128)(2,1)S(1)}, bf16[256,128]{1,0:T(8,128)(2,1)S(1)}, u32[]{:S(2)}, u32[]{:S(2)}) collective-permute-start(bf16[256,128]{1,0:T(8,128)(2,1)S(1)} %get-tuple-element.20), channel_id=1, source_target_pairs={{0,4},{1,5},{2,6},{3,7},{4,0},{5,1},{6,2},{7,3},{8,12},{9,13},{10,... | collective-permute-start | bytes 196616 | tf_op jit(solution)/shard_map/ppermute | solution.py:323

commit v3 on v2

--- a/solution.py
+++ b/solution.py
@@ -54,15 +54,13 @@
     return jnp.where(lane == 0, carried, turned)
 
 
-def featurized(signal, before, taps_ref, stream):
+def featurized(signal, before, taps, stream):
     lane = lax.broadcasted_iota(jnp.int32, signal.shape, 1)
     row = lax.broadcasted_iota(jnp.int32, signal.shape, 0)
     before = jnp.broadcast_to(before, signal.shape)
     once = shifted(signal, before, lane, row)
     twice = shifted(once, pltpu.roll(before, 1, 1), lane, row)
-    summed = (
-        taps_ref[stream, 0, 0] * signal + taps_ref[stream, 0, 1] * once + taps_ref[stream, 0, 2] * twice
-    )
+    summed = taps[stream][0] * signal + taps[stream][1] * once + taps[stream][2] * twice
     return summed.astype(BF16)
 
 
@@ -70,10 +68,11 @@
     return pltpu.roll(values, first, 1) if first else values
 
 
-def forward_kernel(devices, taps_ref, skip_ref, q_hbm, k_hbm, v_hbm, filter_hbm, first_hbm, turn_hbm, second_hbm, w_hbm,
+def forward_kernel(devices, skip_ref, taps_hbm, q_hbm, k_hbm, v_hbm, filter_hbm, first_hbm, turn_hbm, second_hbm, w_hbm,
                    message_ref, q_feat_ref, skipped_ref, scalars_ref,
-                   q_ref, k_ref, v_ref, filter_ref, first_ref, turn_ref, second_ref, w_ref, sems):
+                   taps_ref, q_ref, k_ref, v_ref, filter_ref, first_ref, turn_ref, second_ref, w_ref, sems):
     pairs = (
+        (taps_hbm, taps_ref),
         (k_hbm, k_ref), (v_hbm, v_ref), (filter_hbm, filter_ref), (first_hbm, first_ref),
         (q_hbm, q_ref), (turn_hbm, turn_ref), (second_hbm, second_ref), (w_hbm, w_ref),
     )
@@ -85,33 +84,34 @@
     own, own_chan = lax.axis_index("seq"), lax.axis_index("chan")
     nothing = jnp.zeros((1, LANES), F32)
     lane = lax.broadcasted_iota(jnp.int32, (1, LANES), 1)
+    copies[0].wait()
+    taps = [[taps_ref[stream, :, j : j + 1] for j in range(3)] for stream in range(3)]
+    skip = skip_ref[0]
     for j in range(3):
-        scalars_ref[j : j + 1, :] = jnp.where(
-            lane < 4, taps_ref[1, 0, j], jnp.where(lane < 8, taps_ref[2, 0, j], taps_ref[0, 0, j])
-        )
-    scalars_ref[3:4, :] = jnp.full((1, LANES), skip_ref[0], F32)
-    copies[0].wait()
+        scalars_ref[j : j + 1, :] = jnp.where(lane < 4, taps[1][j], jnp.where(lane < 8, taps[2][j], taps[0][j]))
+    scalars_ref[3:4, :] = jnp.full((1, LANES), skip, F32)
+    copies[1].wait()
     key = k_ref[...].astype(F32).reshape(rows, LANES)
-    k_feat = featurized(key, nothing, taps_ref, 1)
-    copies[1].wait()
+    k_feat = featurized(key, nothing, taps, 1)
+    copies[2].wait()
     value = v_ref[...].astype(F32).reshape(rows, LANES)
-    v_feat = featurized(value, nothing, taps_ref, 2)
+    v_feat = featurized(value, nothing, taps, 2)
     product = k_feat.astype(F32) * v_feat.astype(F32)
-    skipped_ref[...] = skip_ref[0] * product
-    copies[2].wait()
+    skipped_ref[...] = skip * product
+    copies[3].wait()
     signals = jnp.concatenate([product, filter_ref[...]], axis=1).astype(BF16)
-    copies[3].wait()
+    copies[4].wait()
     values = dot(first_ref[...], signals).reshape(devices, 2, per, 2 * LANES)
-    copies[4].wait()
+    copies[5].wait()
     query = q_ref[...].astype(F32).reshape(rows, LANES)
-    q_feat_ref[...] = featurized(query, nothing, taps_ref, 0)
+    q_feat_ref[...] = featurized(query, nothing, taps, 0)
     edges = nothing
     for first, signal in enumerate((key, value, query)):
         ends = jnp.where(lane < 2, signal[:1], jnp.where(lane < LANES - 2, 0.0, signal[rows - 1 :]))
         edges = edges + at_lanes(ends, 4 * first)
     row = lax.broadcasted_iota(jnp.int32, (8, LANES), 0)
     edges = jnp.where(row == own % 8, jnp.broadcast_to(edges, (8, LANES)), 0.0)
-    copies[5].wait()
+    copies[6].wait()
     real, imag = values[:, 0], values[:, 1]
     turn_real = turn_ref[0].reshape(devices, per, LANES)
     turn_imag = turn_ref[1].reshape(devices, per, LANES)
@@ -123,7 +123,7 @@
             jnp.concatenate([a * turn_real + b * turn_imag, b * turn_real - a * turn_imag], axis=2)
         )
     packed = jnp.concatenate(packed, axis=1).reshape(2 * rows, 2 * LANES).astype(BF16)
-    copies[6].wait()
+    copies[7].wait()
     spectra = dot(packed, second_ref[...]).reshape(devices, 2 * per, 2 * LANES)
     message_ref[...] = jnp.concatenate(
         [
@@ -135,7 +135,7 @@
         ],
         axis=1,
     ).astype(BF16)
-    copies[7].wait()
+    copies[8].wait()
     chans = w_ref.shape[0]
     weights = w_ref[...].astype(F32)
     column = lax.broadcasted_iota(jnp.int32, weights.shape, 1)
@@ -219,19 +219,21 @@
     q_feat = jnp.where(head, heads_ref[0:1, :], q_feat_ref[...].astype(F32))
     skipped = jnp.where(head, heads_ref[1:2, :], skipped_ref[...])
     gating = (q_feat * (convolved + skipped)).astype(BF16)
-    for copy in range(gating_ref.shape[0]):
-        gating_ref[copy] = gating
-
-
-def mix_kernel(scalars_ref, gating_ref, own_ref, other_ref):
-    near = gating_ref.shape[0]
+    gating_ref[...] = gating
+
+
+def mix_kernel(scalars_ref, *refs):
+    *gating_refs, own_ref, other_ref = refs
+    near = len(gating_refs)
     chans = 2 * near
-    start = 8 + lax.axis_index("chan") // near * near
+    own_chan = lax.axis_index("chan")
+    start = 8 + own_chan // near * near
     own = other = None
-    for c in range(near):
-        gating = gating_ref[c].astype(F32)
-        to_own = scalars_ref[pl.ds(start + c, 1), :] * gating
-        to_other = scalars_ref[pl.ds(start + chans + c, 1), :] * gating
+    for step, gating_ref in enumerate(gating_refs):
+        gating = gating_ref[...].astype(F32)
+        row = start + (own_chan + near - step) % near
+        to_own = scalars_ref[pl.ds(row, 1), :] * gating
+        to_other = scalars_ref[pl.ds(row + chans, 1), :] * gating
         own = to_own if own is None else own + to_own
         other = to_other if other is None else other + to_other
     own_ref[...] = own
@@ -256,7 +258,7 @@
     forward_first, turn, forward_second, inverse_second, inverse_first, basis = tables(rows, devices)
     message, q_feat, skipped, scalars = pl.pallas_call(
         functools.partial(forward_kernel, devices),
-        in_specs=[SMEM] * 2 + [HBM] * 8,
+        in_specs=[SMEM] + [HBM] * 9,
         out_specs=[VMEM] * 4,
         out_shape=[
             jax.ShapeDtypeStruct((devices, 4 * per + 8, LANES), BF16),
@@ -265,6 +267,7 @@
             jax.ShapeDtypeStruct((8 + 2 * chans, LANES), F32),
         ],
         scratch_shapes=[
+            pltpu.VMEM(short_taps.shape, F32),
             pltpu.VMEM((1, width), BF16),
             pltpu.VMEM((1, width), BF16),
             pltpu.VMEM((1, width), BF16),
@@ -273,16 +276,16 @@
             pltpu.VMEM(turn.shape, F32),
             pltpu.VMEM(forward_second.shape, BF16),
             pltpu.VMEM(w_out.shape, BF16),
-            pltpu.SemaphoreType.DMA((8,)),
+            pltpu.SemaphoreType.DMA((9,)),
         ],
         compiler_params=PARAMS,
         name="forward",
     )(
-        short_taps,
         skip_gain,
         *(
             pltpu.with_memory_space_constraint(jnp.asarray(operand), pltpu.HBM)
             for operand in (
+                short_taps,
                 query_in, key_in, value_in, long_filter.reshape(rows, LANES),
                 forward_first, turn, forward_second, w_out,
             )
@@ -306,20 +309,22 @@
         functools.partial(inverse_kernel, devices),
         in_specs=[VMEM] * 7,
         out_specs=VMEM,
-        out_shape=jax.ShapeDtypeStruct((near, rows, LANES), BF16),
+        out_shape=jax.ShapeDtypeStruct((rows, LANES), BF16),
         compiler_params=PARAMS,
         name="inverse",
     )(spectra, turn, inverse_second, inverse_first, q_feat, skipped, heads)
-    groups = [list(range(near)), list(range(near, chans))]
-    gathered = lax.all_to_all(gating, "chan", 0, 0, axis_index_groups=groups)
+    gathered = [gating] + [
+        lax.ppermute(gating, "chan", [(c, c // near * near + (c + step) % near) for c in range(chans)])
+        for step in range(1, near)
+    ]
     own, other = pl.pallas_call(
         mix_kernel,
-        in_specs=[VMEM] * 2,
+        in_specs=[VMEM] * (near + 1),
         out_specs=[VMEM] * 2,
         out_shape=[jax.ShapeDtypeStruct((rows, LANES), F32), jax.ShapeDtypeStruct((rows, LANES), BF16)],
         compiler_params=PARAMS,
         name="mix",
-    )(scalars, gathered)
+    )(scalars, *gathered)
     other = lax.ppermute(other, "chan", [(c, (c + near) % chans) for c in range(chans)])
     return pl.pallas_call(
         add_kernel,

time: 58.7 us -> 56.9 us (0.969)
  blocking collectives: 43.7 us -> 32.7 us
  waiting for transfers between devices: 4.36 us -> 9.25 us
  starting transfers between devices: 4.58 us -> 9.27 us
    all_to_all x1 -> x0, blocking collectives: 10.9 us -> none  [on_device(): gathered = lax.all_to_all(gating, 'chan', 0, 0, axis_index_groups=groups)]
    ppermute x0 -> x3, waiting for transfers between devices: none -> 4.87 us  [on_device(): lax.ppermute(gating, 'chan', [(c, c // near * near + (c + step) % near) f...]
    ppermute x0 -> x3, starting transfers between devices: none -> 4.69 us  [on_device(): lax.ppermute(gating, 'chan', [(c, c // near * near + (c + step) % near) f...]
  transfers between devices with their start and end apart: 1 -> 4, of which waited for: 1 -> 4; matrix products, arithmetic and copies ran while one was open for 0% -> 0% of each run, Pallas kernels for 0% -> 0%
where the time goes in v3:
time: 56.9 us; the launch traced here: 56.7 us
  blocking collectives  32.7 us (57%)
  starting transfers between devices  9.27 us (16%)
  waiting for transfers between devices  9.25 us (16%)
  Pallas kernels  4.68 us (8%)
  between operations  0.7 us (1%)
    all_to_all x1, blocking collectives, on_device(): message = lax.all_to_all(message, 'seq', 0, 0)  19 us
    all_to_all x1, blocking collectives, on_device(): spectra = lax.all_to_all(spectra, 'seq', 0, 0)  13.7 us
    ppermute x3, waiting for transfers between devices, on_device(): lax.ppermute(gating, 'chan', [(c, c // near * near + (c + step) % near) f...  4.87 us
    ppermute x3, starting transfers between devices, on_device(): lax.ppermute(gating, 'chan', [(c, c // near * near + (c + step) % near) f...  4.69 us
    ppermute x1, starting transfers between devices, on_device(): lax.ppermute(other, 'chan', [(c, (c + near) % chans) for c in range(chans)])  4.58 us
    ppermute x1, waiting for transfers between devices, on_device(): lax.ppermute(other, 'chan', [(c, (c + near) % chans) for c in range(chans)])  4.38 us
    pallas_call x1, Pallas kernels, on_device(): pl.pallas_call(functools.partial(forward_kernel, devices), in_specs=[SMEM...  2.46 us
  transfers between devices with their start and end apart: 4, of which 4 were waited for; matrix products, arithmetic and copies ran while one was open for 0% of the time, Pallas kernels for 0%

profile of v3, /device:TPU:2, one launch (start us, length us, event | category | flops | bytes accessed | tf_op | source)
XLA Modules:
  0.0 56.7 jit_solution(14840130019134422775)
XLA Ops:
  0.7 2.5 %forward.1 = (bf16[32,40,128]{2,1,0:T(8,128)(2,1)S(1)}, bf16[256,128]{1,0:T(8,128)(2,1)S(1)}, f32[256,128]{1,0:T(8,128)S(1)}, f32[24,128]{1,0:T(8,128)S(1)}) custom-call(f32[1]{0:T(128)S(6)} %copy.14.skip_ref, f32[3,1,3]{2,1,0:T(1,128)} %taps_hbm.1, bf16[1,32768]{1,0:T(2,128)(2,1)} %q_hbm.1, bf16[1,32768]{1,0:T(2,128)(2,1)} %k_hbm.1, ...), custom_call_target="tpu_custom_call" | custom-call | tf_op jit(solution)/shard_map/forward/pallas_call | solution.py:259
  3.1 0.0 copy-start.3
  3.1 0.0 copy-start.2
  3.1 19.0 %all_to_all.10.message_ref = bf16[32,40,128]{2,1,0:T(8,128)(2,1)S(1)} all-to-all(bf16[32,40,128]{2,1,0:T(8,128)(2,1)S(1)} %get-tuple-element.14), channel_id=1, replica_groups=mesh['seq'=32,'chan'=8] {'seq'}, dimensions={0} | all-to-all | bytes 655360 | tf_op jit(solution)/shard_map/all_to_all | solution.py:294
  22.1 0.0 copy-done.3
  22.1 0.0 copy-start
  22.1 0.0 copy-start.1
  22.1 0.9 %middle.1 = (bf16[32,16,128]{2,1,0:T(8,128)(2,1)S(1)}, f32[8,128]{1,0:T(8,128)S(1)}) custom-call(f32[24,128]{1,0:T(8,128)S(1)} %get-tuple-element.13.scalars_ref, bf16[32,40,128]{2,1,0:T(8,128)(2,1)S(1)} %all_to_all.10.message_ref, f32[2,8,128]{2,1,0:T(8,128)S(1)} %copy-done.3), custom_call_target="tpu_custom_call" | custom-call | tf_op jit(solution)/shard_map/middle/pallas_call | solution.py:295
  23.0 13.7 %all_to_all.11.spectra_ref = bf16[32,16,128]{2,1,0:T(8,128)(2,1)S(1)} all-to-all(bf16[32,16,128]{2,1,0:T(8,128)(2,1)S(1)} %get-tuple-element.15), channel_id=1, replica_groups=mesh['seq'=32,'chan'=8] {'seq'}, dimensions={0} | all-to-all | bytes 262144 | tf_op jit(solution)/shard_map/all_to_all | solution.py:307
  36.8 0.0 copy-done.2
  36.8 0.0 copy-done
  36.8 0.0 copy-done.1
  36.8 0.5 inverse.1.refs_0_
  37.2 3.1 %collective-permute-start.2 = (bf16[256,128]{1,0:T(8,128)(2,1)S(1)}, bf16[256,128]{1,0:T(8,128)(2,1)S(1)}, u32[]{:S(2)}, u32[]{:S(2)}) collective-permute-start(bf16[256,128]{1,0:T(8,128)(2,1)S(1)} %inverse.1.refs_0_), channel_id=1, source_target_pairs={{0,3},{1,0},{2,1},{3,2},{4,7},{5,4},{6,5},{7,6},{8,11},{9,8},{10,9... | collective-permute-start | bytes 196616 | tf_op jit(solution)/shard_map/ppermute | solution.py:317
  40.3 0.6 %collective-permute-start.1 = (bf16[256,128]{1,0:T(8,128)(2,1)S(1)}, bf16[256,128]{1,0:T(8,128)(2,1)S(1)}, u32[]{:S(2)}, u32[]{:S(2)}) collective-permute-start(bf16[256,128]{1,0:T(8,128)(2,1)S(1)} %inverse.1.refs_0_), channel_id=1, source_target_pairs={{0,2},{1,3},{2,0},{3,1},{4,6},{5,7},{6,4},{7,5},{8,10},{9,11},{10,... | collective-permute-start | bytes 196616 | tf_op jit(solution)/shard_map/ppermute | solution.py:317
  41.0 1.0 %collective-permute-start = (bf16[256,128]{1,0:T(8,128)(2,1)S(1)}, bf16[256,128]{1,0:T(8,128)(2,1)S(1)}, u32[]{:S(2)}, u32[]{:S(2)}) collective-permute-start(bf16[256,128]{1,0:T(8,128)(2,1)S(1)} %inverse.1.refs_0_), channel_id=1, source_target_pairs={{0,1},{1,2},{2,3},{3,0},{4,5},{5,6},{6,7},{7,4},{8,9},{9,10},{10,1... | collective-permute-start | bytes 196616 | tf_op jit(solution)/shard_map/ppermute | solution.py:317
  41.9 0.3 collective-permute-done.2.refs_3_
  42.2 3.9 %collective-permute-done.1.refs_2_ = bf16[256,128]{1,0:T(8,128)(2,1)S(1)} collective-permute-done((bf16[256,128]{1,0:T(8,128)(2,1)S(1)}, bf16[256,128]{1,0:T(8,128)(2,1)S(1)}, u32[]{:S(2)}, u32[]{:S(2)}) %collective-permute-start.1) | collective-permute-done | bytes 65568 | tf_op jit(solution)/shard_map/ppermute | solution.py:317
  46.1 0.7 %collective-permute-done.refs_1_ = bf16[256,128]{1,0:T(8,128)(2,1)S(1)} collective-permute-done((bf16[256,128]{1,0:T(8,128)(2,1)S(1)}, bf16[256,128]{1,0:T(8,128)(2,1)S(1)}, u32[]{:S(2)}, u32[]{:S(2)}) %collective-permute-start) | collective-permute-done | bytes 65568 | tf_op jit(solution)/shard_map/ppermute | solution.py:317
  46.8 0.1 mix.1
  46.9 4.6 %collective-permute-start.3 = (bf16[256,128]{1,0:T(8,128)(2,1)S(1)}, bf16[256,128]{1,0:T(8,128)(2,1)S(1)}, u32[]{:S(2)}, u32[]{:S(2)}) collective-permute-start(bf16[256,128]{1,0:T(8,128)(2,1)S(1)} %get-tuple-element.20), channel_id=1, source_target_pairs={{0,4},{1,5},{2,6},{3,7},{4,0},{5,1},{6,2},{7,3},{8,12},{9,13},{10,... | collective-permute-start | bytes 196616 | tf_op jit(solution)/shard_map/ppermute | solution.py:328
  51.5 4.4 %collective-permute-done.3.other_ref = bf16[256,128]{1,0:T(8,128)(2,1)S(1)} collective-permute-done((bf16[256,128]{1,0:T(8,128)(2,1)S(1)}, bf16[256,128]{1,0:T(8,128)(2,1)S(1)}, u32[]{:S(2)}, u32[]{:S(2)}) %collective-permute-start.3) | collective-permute-done | bytes 65568 | tf_op jit(solution)/shard_map/ppermute | solution.py:328
  55.9 0.8 %add.1 = bf16[1,32768]{1,0:T(2,128)(2,1)} custom-call(f32[256,128]{1,0:T(8,128)S(1)} %get-tuple-element.19.own_ref, bf16[256,128]{1,0:T(8,128)(2,1)S(1)} %collective-permute-done.3.other_ref), custom_call_target="tpu_custom_call" | custom-call | tf_op jit(solution)/shard_map/add/pallas_call | solution.py:329
Async XLA Ops:
  3.1 19.0 %copy-start.3 = (f32[2,8,128]{2,1,0:T(8,128)S(1)}, f32[2,8,128]{2,1,0:T(8,128)}, u32[]{:S(2)}) copy-start(f32[2,8,128]{2,1,0:T(8,128)} %constant.15.clone.basis_ref) | copy-start | bytes 24580
  3.1 33.6 %copy-start.2 = (bf16[256,256]{1,0:T(8,128)(2,1)S(1)}, bf16[256,256]{1,0:T(8,128)(2,1)}, u32[]{:S(2)}) copy-start(bf16[256,256]{1,0:T(8,128)(2,1)} %constant.16.clone.second_ref) | copy-start | bytes 393220
  22.1 14.6 %copy-start = (f32[2,256,128]{2,1,0:T(8,128)S(1)}, f32[2,256,128]{2,1,0:T(8,128)}, u32[]{:S(2)}) copy-start(f32[2,256,128]{2,1,0:T(8,128)} %constant.13.clone.turn_hbm.turn_ref) | copy-start | bytes 786436
  22.1 14.6 %copy-start.1 = (bf16[256,512]{1,0:T(8,128)(2,1)S(1)}, bf16[256,512]{1,0:T(8,128)(2,1)}, u32[]{:S(2)}) copy-start(bf16[256,512]{1,0:T(8,128)(2,1)} %constant.17.clone.first_ref) | copy-start | bytes 786436
  37.2 5.0 %collective-permute-start.2 = (bf16[256,128]{1,0:T(8,128)(2,1)S(1)}, bf16[256,128]{1,0:T(8,128)(2,1)S(1)}, u32[]{:S(2)}, u32[]{:S(2)}) collective-permute-start(bf16[256,128]{1,0:T(8,128)(2,1)S(1)} %inverse.1.refs_0_), channel_id=1, source_target_pairs={{0,3},{1,0},{2,1},{3,2},{4,7},{5,4},{6,5},{7,6},{8,11},{9,8},{10,9... | collective-permute-start | bytes 196616 | tf_op jit(solution)/shard_map/ppermute | solution.py:317
  40.3 5.8 %collective-permute-start.1 = (bf16[256,128]{1,0:T(8,128)(2,1)S(1)}, bf16[256,128]{1,0:T(8,128)(2,1)S(1)}, u32[]{:S(2)}, u32[]{:S(2)}) collective-permute-start(bf16[256,128]{1,0:T(8,128)(2,1)S(1)} %inverse.1.refs_0_), channel_id=1, source_target_pairs={{0,2},{1,3},{2,0},{3,1},{4,6},{5,7},{6,4},{7,5},{8,10},{9,11},{10,... | collective-permute-start | bytes 196616 | tf_op jit(solution)/shard_map/ppermute | solution.py:317
  41.0 5.8 %collective-permute-start = (bf16[256,128]{1,0:T(8,128)(2,1)S(1)}, bf16[256,128]{1,0:T(8,128)(2,1)S(1)}, u32[]{:S(2)}, u32[]{:S(2)}) collective-permute-start(bf16[256,128]{1,0:T(8,128)(2,1)S(1)} %inverse.1.refs_0_), channel_id=1, source_target_pairs={{0,1},{1,2},{2,3},{3,0},{4,5},{5,6},{6,7},{7,4},{8,9},{9,10},{10,1... | collective-permute-start | bytes 196616 | tf_op jit(solution)/shard_map/ppermute | solution.py:317
  46.9 9.0 %collective-permute-start.3 = (bf16[256,128]{1,0:T(8,128)(2,1)S(1)}, bf16[256,128]{1,0:T(8,128)(2,1)S(1)}, u32[]{:S(2)}, u32[]{:S(2)}) collective-permute-start(bf16[256,128]{1,0:T(8,128)(2,1)S(1)} %get-tuple-element.20), channel_id=1, source_target_pairs={{0,4},{1,5},{2,6},{3,7},{4,0},{5,1},{6,2},{7,3},{8,12},{9,13},{10,... | collective-permute-start | bytes 196616 | tf_op jit(solution)/shard_map/ppermute | solution.py:328

commit v4 on v3

--- a/solution.py
+++ b/solution.py
@@ -11,6 +11,7 @@
 from jax.sharding import PartitionSpec as P
 
 LANES = 128
+PACK = 2
 F32 = jnp.float32
 BF16 = jnp.bfloat16
 VMEM_LIMIT = 40 * 1024 * 1024
@@ -68,7 +69,7 @@
     return pltpu.roll(values, first, 1) if first else values
 
 
-def forward_kernel(devices, skip_ref, taps_hbm, q_hbm, k_hbm, v_hbm, filter_hbm, first_hbm, turn_hbm, second_hbm, w_hbm,
+def forward_kernel(devices, taps_hbm, q_hbm, k_hbm, v_hbm, filter_hbm, first_hbm, turn_hbm, second_hbm, w_hbm,
                    message_ref, q_feat_ref, skipped_ref, scalars_ref,
                    taps_ref, q_ref, k_ref, v_ref, filter_ref, first_ref, turn_ref, second_ref, w_ref, sems):
     pairs = (
@@ -86,10 +87,8 @@
     lane = lax.broadcasted_iota(jnp.int32, (1, LANES), 1)
     copies[0].wait()
     taps = [[taps_ref[stream, :, j : j + 1] for j in range(3)] for stream in range(3)]
-    skip = skip_ref[0]
     for j in range(3):
         scalars_ref[j : j + 1, :] = jnp.where(lane < 4, taps[1][j], jnp.where(lane < 8, taps[2][j], taps[0][j]))
-    scalars_ref[3:4, :] = jnp.full((1, LANES), skip, F32)
     copies[1].wait()
     key = k_ref[...].astype(F32).reshape(rows, LANES)
     k_feat = featurized(key, nothing, taps, 1)
@@ -97,7 +96,7 @@
     value = v_ref[...].astype(F32).reshape(rows, LANES)
     v_feat = featurized(value, nothing, taps, 2)
     product = k_feat.astype(F32) * v_feat.astype(F32)
-    skipped_ref[...] = skip * product
+    skipped_ref[...] = product
     copies[3].wait()
     signals = jnp.concatenate([product, filter_ref[...]], axis=1).astype(BF16)
     copies[4].wait()
@@ -110,7 +109,7 @@
         ends = jnp.where(lane < 2, signal[:1], jnp.where(lane < LANES - 2, 0.0, signal[rows - 1 :]))
         edges = edges + at_lanes(ends, 4 * first)
     row = lax.broadcasted_iota(jnp.int32, (8, LANES), 0)
-    edges = jnp.where(row == own % 8, jnp.broadcast_to(edges, (8, LANES)), 0.0)
+    edges = jnp.where(row == 0, jnp.broadcast_to(edges, (8, LANES)), 0.0)[:PACK]
     copies[6].wait()
     real, imag = values[:, 0], values[:, 1]
     turn_real = turn_ref[0].reshape(devices, per, LANES)
@@ -125,16 +124,18 @@
     packed = jnp.concatenate(packed, axis=1).reshape(2 * rows, 2 * LANES).astype(BF16)
     copies[7].wait()
     spectra = dot(packed, second_ref[...]).reshape(devices, 2 * per, 2 * LANES)
-    message_ref[...] = jnp.concatenate(
+    spectra = jnp.concatenate(
         [
             spectra[:, :per, :LANES],
             spectra[:, :per, LANES:],
             spectra[:, per:, :LANES],
             spectra[:, per:, LANES:],
-            jnp.broadcast_to(edges[None], (devices, 8, LANES)),
         ],
         axis=1,
     ).astype(BF16)
+    packs = 4 * per // PACK
+    message_ref[:, :packs] = spectra.reshape(devices, packs, PACK, LANES)
+    message_ref[:, packs] = jnp.broadcast_to(edges.astype(BF16)[None], (devices, PACK, LANES))
     copies[8].wait()
     chans = w_ref.shape[0]
     weights = w_ref[...].astype(F32)
@@ -148,13 +149,12 @@
     return values.astype(BF16).astype(F32)
 
 
-def middle_kernel(devices, scalars_ref, message_ref, basis_ref, out_ref, heads_ref, heads_scratch, error_scratch):
-    per = (message_ref.shape[1] - 8) // 4
+def middle_kernel(devices, skip_ref, scalars_ref, message_ref, basis_ref, out_ref, heads_ref, heads_scratch, error_scratch, aligned_ref):
+    pitch = message_ref.shape[0] // devices
+    per = (pitch - PACK) // 4
+    message = message_ref[...].astype(F32)
     own = lax.axis_index("seq")
-    groups = [
-        sum(message_ref[p, 4 * per :, :].astype(F32) for p in range(group, group + 8)) for group in range(0, devices, 8)
-    ]
-    edges = jnp.concatenate(groups, axis=0)
+    edges = jnp.concatenate([message[(p + 1) * pitch - PACK : (p + 1) * pitch - PACK + 1] for p in range(devices)], axis=0)
     before = jnp.concatenate([jnp.zeros((1, LANES), F32), edges[:-1]], axis=0)
     lane = lax.broadcasted_iota(jnp.int32, edges.shape, 1)
     taps = [scalars_ref[j : j + 1, :] for j in range(3)]
@@ -169,9 +169,10 @@
     for i in range(2):
         error_scratch[i] = jnp.broadcast_to(error[:, i : i + 1], edges.shape)
     heads_scratch[0] = pltpu.roll(heads, LANES - 8, 1)
-    heads_scratch[1] = scalars_ref[3:4, :] * product
+    heads_scratch[1] = product
     for i in range(2):
         heads_ref[i : i + 1, :] = heads_scratch[i, pl.ds(own, 1), :]
+    heads_ref[2:3, :] = jnp.full((1, LANES), skip_ref[0], F32)
     angle = jnp.full((per, LANES), own, jnp.int32).astype(F32) * (2.0 * math.pi / (devices * LANES))
     square = angle * angle
     cos = 1.0 - square * (0.5 - square * (1.0 / 24.0))
@@ -181,23 +182,25 @@
     point_imag = basis_imag * cos - basis_real * sin
     blocks = []
     for p in range(devices):
-        block = message_ref[p].astype(F32)
+        aligned_ref[p] = message[p * pitch : p * pitch + 4 * per]
+    for p in range(devices):
+        block = aligned_ref[p]
         real, imag = block[:per], block[per : 2 * per]
         if p > 0:
             first = error_scratch[1, p : p + 1, :]
             real = real + (error_scratch[0, p : p + 1, :] + first * point_real)
             imag = imag + first * point_imag
-        blocks.append((real, imag, block[2 * per : 3 * per], block[3 * per : 4 * per]))
+        c, d = block[2 * per : 3 * per], block[3 * per : 4 * per]
+        blocks.append((real + imag, real, imag, c, d - c, c + d))
     behind_real = jnp.zeros((per, LANES), F32)
     behind_imag = behind_real
     for p in range(devices):
-        real = imag = None
+        sums = [None] * 3
         for q in range(p + 1):
-            a, b = blocks[q][0], blocks[q][1]
-            c, d = blocks[p - q][2], blocks[p - q][3]
-            term_real, term_imag = a * c - b * d, a * d + b * c
-            real = term_real if real is None else real + term_real
-            imag = term_imag if imag is None else imag + term_imag
+            for i in range(3):
+                term = blocks[q][i] * blocks[p - q][3 + i]
+                sums[i] = term if sums[i] is None else sums[i] + term
+        real, imag = sums[0] - sums[2], sums[0] + sums[1]
         out_ref[p] = jnp.concatenate([real - behind_imag, imag + behind_real], axis=0).astype(BF16)
         behind_real, behind_imag = real, imag
 
@@ -217,7 +220,7 @@
     row = lax.broadcasted_iota(jnp.int32, (rows, LANES), 0)
     head = (row == 0) & (lane < 2)
     q_feat = jnp.where(head, heads_ref[0:1, :], q_feat_ref[...].astype(F32))
-    skipped = jnp.where(head, heads_ref[1:2, :], skipped_ref[...])
+    skipped = heads_ref[2:3, :] * jnp.where(head, heads_ref[1:2, :], skipped_ref[...])
     gating = (q_feat * (convolved + skipped)).astype(BF16)
     gating_ref[...] = gating
 
@@ -258,10 +261,10 @@
     forward_first, turn, forward_second, inverse_second, inverse_first, basis = tables(rows, devices)
     message, q_feat, skipped, scalars = pl.pallas_call(
         functools.partial(forward_kernel, devices),
-        in_specs=[SMEM] + [HBM] * 9,
+        in_specs=[HBM] * 9,
         out_specs=[VMEM] * 4,
         out_shape=[
-            jax.ShapeDtypeStruct((devices, 4 * per + 8, LANES), BF16),
+            jax.ShapeDtypeStruct((devices, 4 * per // PACK + 1, PACK, LANES), BF16),
             jax.ShapeDtypeStruct((rows, LANES), BF16),
             jax.ShapeDtypeStruct((rows, LANES), F32),
             jax.ShapeDtypeStruct((8 + 2 * chans, LANES), F32),
@@ -281,7 +284,6 @@
         compiler_params=PARAMS,
         name="forward",
     )(
-        skip_gain,
         *(
             pltpu.with_memory_space_constraint(jnp.asarray(operand), pltpu.HBM)
             for operand in (
@@ -294,16 +296,16 @@
     message = lax.all_to_all(message, "seq", 0, 0)
     spectra, heads = pl.pallas_call(
         functools.partial(middle_kernel, devices),
-        in_specs=[VMEM] * 3,
+        in_specs=[SMEM] + [VMEM] * 3,
         out_specs=[VMEM] * 2,
         out_shape=[
             jax.ShapeDtypeStruct((devices, 2 * per, LANES), BF16),
             jax.ShapeDtypeStruct((8, LANES), F32),
         ],
-        scratch_shapes=[pltpu.VMEM((2, devices, LANES), F32)] * 2,
+        scratch_shapes=[pltpu.VMEM((2, devices, LANES), F32)] * 2 + [pltpu.VMEM((devices, 4 * per, LANES), F32)],
         compiler_params=PARAMS,
         name="middle",
-    )(scalars, message, basis)
+    )(skip_gain, scalars, message.reshape(-1, LANES), basis)
     spectra = lax.all_to_all(spectra, "seq", 0, 0)
     gating = pl.pallas_call(
         functools.partial(inverse_kernel, devices),

time: 56.9 us -> 55.1 us (0.968)
  blocking collectives: 32.7 us -> 13.3 us
  starting transfers between devices: 9.27 us -> 19.7 us
  waiting for transfers between devices: 9.25 us -> 15.8 us
  Pallas kernels: 4.68 us -> 5.25 us
    all_to_all x1 -> x0, blocking collectives: 19 us -> none  [on_device(): message = lax.all_to_all(message, 'seq', 0, 0)]
    all_to_all x0 -> x1, starting transfers between devices: none -> 9.2 us  [on_device(): message = lax.all_to_all(message, 'seq', 0, 0)]
    all_to_all x0 -> x1, waiting for transfers between devices: none -> 8.75 us  [on_device(): message = lax.all_to_all(message, 'seq', 0, 0)]
    ppermute x3, waiting for transfers between devices: 4.87 us -> 2.92 us  [on_device(): lax.ppermute(gating, 'chan', [(c, c // near * near + (c + step) % near) f...]
    ppermute x3, starting transfers between devices: 4.69 us -> 5.9 us  [on_device(): lax.ppermute(gating, 'chan', [(c, c // near * near + (c + step) % near) f...]
  transfers between devices with their start and end apart: 4 -> 5, of which waited for: 4 -> 5; matrix products, arithmetic and copies ran while one was open for 0% -> 0% of each run, Pallas kernels for 0% -> 0%
where the time goes in v4:
time: 55.1 us; the launch traced here: 54.8 us
  starting transfers between devices  19.7 us (36%)
  waiting for transfers between devices  15.8 us (29%)
  blocking collectives  13.3 us (24%)
  Pallas kernels  5.25 us (10%)
  between operations  0.7 us (1%)
    all_to_all x1, blocking collectives, on_device(): spectra = lax.all_to_all(spectra, 'seq', 0, 0)  13.3 us
    all_to_all x1, starting transfers between devices, on_device(): message = lax.all_to_all(message, 'seq', 0, 0)  9.2 us
    all_to_all x1, waiting for transfers between devices, on_device(): message = lax.all_to_all(message, 'seq', 0, 0)  8.75 us
    ppermute x3, starting transfers between devices, on_device(): lax.ppermute(gating, 'chan', [(c, c // near * near + (c + step) % near) f...  5.9 us
    ppermute x1, starting transfers between devices, on_device(): lax.ppermute(other, 'chan', [(c, (c + near) % chans) for c in range(chans)])  4.58 us
    ppermute x1, waiting for transfers between devices, on_device(): lax.ppermute(other, 'chan', [(c, (c + near) % chans) for c in range(chans)])  4.13 us
    pallas_call x1, Pallas kernels, on_device(): pl.pallas_call(functools.partial(forward_kernel, devices), in_specs=[HBM]...  3.1 us
    ppermute x3, waiting for transfers between devices, on_device(): lax.ppermute(gating, 'chan', [(c, c // near * near + (c + step) % near) f...  2.92 us
  transfers between devices with their start and end apart: 5, of which 5 were waited for; matrix products, arithmetic and copies ran while one was open for 0% of the time, Pallas kernels for 0%

profile of v4, /device:TPU:2, one launch (start us, length us, event | category | flops | bytes accessed | tf_op | source)
XLA Modules:
  0.0 54.8 jit_solution(12772272091142635895)
XLA Ops:
  0.0 3.1 %forward.1 = (bf16[32,17,2,128]{3,2,1,0:T(2,128)(2,1)}, bf16[256,128]{1,0:T(8,128)(2,1)S(1)}, f32[256,128]{1,0:T(8,128)S(1)}, f32[24,128]{1,0:T(8,128)S(1)}) custom-call(f32[3,1,3]{2,1,0:T(1,128)} %taps_hbm.1, bf16[1,32768]{1,0:T(2,128)(2,1)} %q_hbm.1, bf16[1,32768]{1,0:T(2,128)(2,1)} %k_hbm.1, bf16[1,32768]{1,0:T(2,128)(2,1)} %v_hbm.1, f32[256,128]{1,0:T(8,128)} %bitcast.3, ...), custom_call_target="tpu_custom_call" | custom-call | tf_op jit(solution)/shard_map/forward/pallas_call | solution.py:262
  3.1 0.0 copy-start.3
  3.1 0.0 copy-start.2
  3.1 9.2 %all-to-all-start = ((bf16[32,17,2,128]{3,2,1,0:T(2,128)(2,1)}), bf16[32,17,2,128]{3,2,1,0:T(2,128)(2,1)S(1)}, u32[]{:S(2)}, u32[]{:S(2)}) async-start(bf16[32,17,2,128]{3,2,1,0:T(2,128)(2,1)} %get-tuple-element.14), calls=%async_computation | async-start | bytes 557056 | tf_op jit(solution)/shard_map/all_to_all | solution.py:296
  13.0 8.8 %all-to-all-done = bf16[32,17,2,128]{3,2,1,0:T(2,128)(2,1)S(1)} async-done(((bf16[32,17,2,128]{3,2,1,0:T(2,128)(2,1)}), bf16[32,17,2,128]{3,2,1,0:T(2,128)(2,1)S(1)}, u32[]{:S(2)}, u32[]{:S(2)}) %all-to-all-start) | async-done | bytes 278560 | tf_op jit(solution)/shard_map/all_to_all | solution.py:296
  21.7 0.0 copy-done.3
  21.7 0.0 copy-start
  21.7 0.0 copy-start.1
  21.7 0.8 %middle.1 = (bf16[32,16,128]{2,1,0:T(8,128)(2,1)S(1)}, f32[8,128]{1,0:T(8,128)S(1)}) custom-call(f32[1]{0:T(128)S(6)} %copy.14.skip_ref, f32[24,128]{1,0:T(8,128)S(1)} %get-tuple-element.13.scalars_ref, bf16[1088,128]{1,0:T(8,128)(2,1)S(1)} %bitcast.2, f32[2,8,128]{2,1,0:T(8,128)S(1)} %copy-done.3), custom_call_target="tpu_custom_call" | custom-call | tf_op jit(solution)/shard_map/middle/pallas_call | solution.py:297
  22.6 13.3 %all_to_all.10.spectra_ref = bf16[32,16,128]{2,1,0:T(8,128)(2,1)S(1)} all-to-all(bf16[32,16,128]{2,1,0:T(8,128)(2,1)S(1)} %get-tuple-element.15), channel_id=1, replica_groups=mesh['seq'=32,'chan'=8] {'seq'}, dimensions={0} | all-to-all | bytes 262144 | tf_op jit(solution)/shard_map/all_to_all | solution.py:309
  35.9 0.0 copy-done.2
  35.9 0.0 copy-done
  35.9 0.0 copy-done.1
  35.9 0.5 inverse.1.refs_0_
  36.3 1.7 %collective-permute-start = (bf16[256,128]{1,0:T(8,128)(2,1)S(1)}, bf16[256,128]{1,0:T(8,128)(2,1)S(1)}, u32[]{:S(2)}, u32[]{:S(2)}) collective-permute-start(bf16[256,128]{1,0:T(8,128)(2,1)S(1)} %inverse.1.refs_0_), channel_id=1, source_target_pairs={{0,1},{1,2},{2,3},{3,0},{4,5},{5,6},{6,7},{7,4},{8,9},{9,10},{10,1... | collective-permute-start | bytes 196616 | tf_op jit(solution)/shard_map/ppermute | solution.py:319
  38.0 2.9 %collective-permute-start.1 = (bf16[256,128]{1,0:T(8,128)(2,1)S(1)}, bf16[256,128]{1,0:T(8,128)(2,1)S(1)}, u32[]{:S(2)}, u32[]{:S(2)}) collective-permute-start(bf16[256,128]{1,0:T(8,128)(2,1)S(1)} %inverse.1.refs_0_), channel_id=1, source_target_pairs={{0,2},{1,3},{2,0},{3,1},{4,6},{5,7},{6,4},{7,5},{8,10},{9,11},{10,... | collective-permute-start | bytes 196616 | tf_op jit(solution)/shard_map/ppermute | solution.py:319
  40.9 1.3 %collective-permute-start.2 = (bf16[256,128]{1,0:T(8,128)(2,1)S(1)}, bf16[256,128]{1,0:T(8,128)(2,1)S(1)}, u32[]{:S(2)}, u32[]{:S(2)}) collective-permute-start(bf16[256,128]{1,0:T(8,128)(2,1)S(1)} %inverse.1.refs_0_), channel_id=1, source_target_pairs={{0,3},{1,0},{2,1},{3,2},{4,7},{5,4},{6,5},{7,6},{8,11},{9,8},{10,9... | collective-permute-start | bytes 196616 | tf_op jit(solution)/shard_map/ppermute | solution.py:319
  42.3 0.4 collective-permute-done.refs_1_
  42.6 1.3 %collective-permute-done.1.refs_2_ = bf16[256,128]{1,0:T(8,128)(2,1)S(1)} collective-permute-done((bf16[256,128]{1,0:T(8,128)(2,1)S(1)}, bf16[256,128]{1,0:T(8,128)(2,1)S(1)}, u32[]{:S(2)}, u32[]{:S(2)}) %collective-permute-start.1) | collective-permute-done | bytes 65568 | tf_op jit(solution)/shard_map/ppermute | solution.py:319
  43.9 1.3 %collective-permute-done.2.refs_3_ = bf16[256,128]{1,0:T(8,128)(2,1)S(1)} collective-permute-done((bf16[256,128]{1,0:T(8,128)(2,1)S(1)}, bf16[256,128]{1,0:T(8,128)(2,1)S(1)}, u32[]{:S(2)}, u32[]{:S(2)}) %collective-permute-start.2) | collective-permute-done | bytes 65568 | tf_op jit(solution)/shard_map/ppermute | solution.py:319
  45.2 0.1 mix.1
  45.3 4.6 %collective-permute-start.3 = (bf16[256,128]{1,0:T(8,128)(2,1)S(1)}, bf16[256,128]{1,0:T(8,128)(2,1)S(1)}, u32[]{:S(2)}, u32[]{:S(2)}) collective-permute-start(bf16[256,128]{1,0:T(8,128)(2,1)S(1)} %get-tuple-element.20), channel_id=1, source_target_pairs={{0,4},{1,5},{2,6},{3,7},{4,0},{5,1},{6,2},{7,3},{8,12},{9,13},{10,... | collective-permute-start | bytes 196616 | tf_op jit(solution)/shard_map/ppermute | solution.py:330
  49.9 4.1 %collective-permute-done.3.other_ref = bf16[256,128]{1,0:T(8,128)(2,1)S(1)} collective-permute-done((bf16[256,128]{1,0:T(8,128)(2,1)S(1)}, bf16[256,128]{1,0:T(8,128)(2,1)S(1)}, u32[]{:S(2)}, u32[]{:S(2)}) %collective-permute-start.3) | collective-permute-done | bytes 65568 | tf_op jit(solution)/shard_map/ppermute | solution.py:330
  54.0 0.8 %add.1 = bf16[1,32768]{1,0:T(2,128)(2,1)} custom-call(f32[256,128]{1,0:T(8,128)S(1)} %get-tuple-element.19.own_ref, bf16[256,128]{1,0:T(8,128)(2,1)S(1)} %collective-permute-done.3.other_ref), custom_call_target="tpu_custom_call" | custom-call | tf_op jit(solution)/shard_map/add/pallas_call | solution.py:331
Async XLA Ops:
  3.1 18.6 %copy-start.3 = (f32[2,8,128]{2,1,0:T(8,128)S(1)}, f32[2,8,128]{2,1,0:T(8,128)}, u32[]{:S(2)}) copy-start(f32[2,8,128]{2,1,0:T(8,128)} %constant.15.clone.basis_ref) | copy-start | bytes 24580
  3.1 32.8 %copy-start.2 = (bf16[256,256]{1,0:T(8,128)(2,1)S(1)}, bf16[256,256]{1,0:T(8,128)(2,1)}, u32[]{:S(2)}) copy-start(bf16[256,256]{1,0:T(8,128)(2,1)} %constant.16.clone.second_ref) | copy-start | bytes 393220
  3.1 18.6 %all-to-all-start = ((bf16[32,17,2,128]{3,2,1,0:T(2,128)(2,1)}), bf16[32,17,2,128]{3,2,1,0:T(2,128)(2,1)S(1)}, u32[]{:S(2)}, u32[]{:S(2)}) async-start(bf16[32,17,2,128]{3,2,1,0:T(2,128)(2,1)} %get-tuple-element.14), calls=%async_computation | async-start | bytes 557056 | tf_op jit(solution)/shard_map/all_to_all | solution.py:296
  21.7 14.1 %copy-start = (f32[2,256,128]{2,1,0:T(8,128)S(1)}, f32[2,256,128]{2,1,0:T(8,128)}, u32[]{:S(2)}) copy-start(f32[2,256,128]{2,1,0:T(8,128)} %constant.13.clone.turn_hbm.turn_ref) | copy-start | bytes 786436
  21.7 14.1 %copy-start.1 = (bf16[256,512]{1,0:T(8,128)(2,1)S(1)}, bf16[256,512]{1,0:T(8,128)(2,1)}, u32[]{:S(2)}) copy-start(bf16[256,512]{1,0:T(8,128)(2,1)} %constant.17.clone.first_ref) | copy-start | bytes 786436
  36.3 6.3 %collective-permute-start = (bf16[256,128]{1,0:T(8,128)(2,1)S(1)}, bf16[256,128]{1,0:T(8,128)(2,1)S(1)}, u32[]{:S(2)}, u32[]{:S(2)}) collective-permute-start(bf16[256,128]{1,0:T(8,128)(2,1)S(1)} %inverse.1.refs_0_), channel_id=1, source_target_pairs={{0,1},{1,2},{2,3},{3,0},{4,5},{5,6},{6,7},{7,4},{8,9},{9,10},{10,1... | collective-permute-start | bytes 196616 | tf_op jit(solution)/shard_map/ppermute | solution.py:319
  38.0 5.9 %collective-permute-start.1 = (bf16[256,128]{1,0:T(8,128)(2,1)S(1)}, bf16[256,128]{1,0:T(8,128)(2,1)S(1)}, u32[]{:S(2)}, u32[]{:S(2)}) collective-permute-start(bf16[256,128]{1,0:T(8,128)(2,1)S(1)} %inverse.1.refs_0_), channel_id=1, source_target_pairs={{0,2},{1,3},{2,0},{3,1},{4,6},{5,7},{6,4},{7,5},{8,10},{9,11},{10,... | collective-permute-start | bytes 196616 | tf_op jit(solution)/shard_map/ppermute | solution.py:319
  40.9 4.3 %collective-permute-start.2 = (bf16[256,128]{1,0:T(8,128)(2,1)S(1)}, bf16[256,128]{1,0:T(8,128)(2,1)S(1)}, u32[]{:S(2)}, u32[]{:S(2)}) collective-permute-start(bf16[256,128]{1,0:T(8,128)(2,1)S(1)} %inverse.1.refs_0_), channel_id=1, source_target_pairs={{0,3},{1,0},{2,1},{3,2},{4,7},{5,4},{6,5},{7,6},{8,11},{9,8},{10,9... | collective-permute-start | bytes 196616 | tf_op jit(solution)/shard_map/ppermute | solution.py:319
  45.3 8.7 %collective-permute-start.3 = (bf16[256,128]{1,0:T(8,128)(2,1)S(1)}, bf16[256,128]{1,0:T(8,128)(2,1)S(1)}, u32[]{:S(2)}, u32[]{:S(2)}) collective-permute-start(bf16[256,128]{1,0:T(8,128)(2,1)S(1)} %get-tuple-element.20), channel_id=1, source_target_pairs={{0,4},{1,5},{2,6},{3,7},{4,0},{5,1},{6,2},{7,3},{8,12},{9,13},{10,... | collective-permute-start | bytes 196616 | tf_op jit(solution)/shard_map/ppermute | solution.py:330

commit v5 on v4

--- a/solution.py
+++ b/solution.py
@@ -12,6 +12,7 @@
 
 LANES = 128
 PACK = 2
+CHUNKS = 2
 F32 = jnp.float32
 BF16 = jnp.bfloat16
 VMEM_LIMIT = 40 * 1024 * 1024
@@ -48,19 +49,17 @@
     return jnp.dot(left, right, preferred_element_type=F32)
 
 
-def shifted(values, before, lane, row):
+def moved_on(values, lane, row):
     turned = pltpu.roll(values, 1, 1)
-    carried = pltpu.roll(turned, 1, 0)
-    carried = jnp.where(row == 0, pltpu.roll(before, 1, 1), carried)
+    carried = jnp.where(row == 0, 0.0, pltpu.roll(turned, 1, 0))
     return jnp.where(lane == 0, carried, turned)
 
 
-def featurized(signal, before, taps, stream):
+def featurized(signal, taps, stream):
     lane = lax.broadcasted_iota(jnp.int32, signal.shape, 1)
     row = lax.broadcasted_iota(jnp.int32, signal.shape, 0)
-    before = jnp.broadcast_to(before, signal.shape)
-    once = shifted(signal, before, lane, row)
-    twice = shifted(once, pltpu.roll(before, 1, 1), lane, row)
+    once = moved_on(signal, lane, row)
+    twice = moved_on(once, lane, row)
     summed = taps[stream][0] * signal + taps[stream][1] * once + taps[stream][2] * twice
     return summed.astype(BF16)
 
@@ -69,74 +68,89 @@
     return pltpu.roll(values, first, 1) if first else values
 
 
-def forward_kernel(devices, taps_hbm, q_hbm, k_hbm, v_hbm, filter_hbm, first_hbm, turn_hbm, second_hbm, w_hbm,
-                   message_ref, q_feat_ref, skipped_ref, scalars_ref,
-                   taps_ref, q_ref, k_ref, v_ref, filter_ref, first_ref, turn_ref, second_ref, w_ref, sems):
+def forward_kernel(devices, taps_hbm, k_hbm, v_hbm, q_hbm, filter_hbm, first_hbm, turn_hbm, second_hbm,
+                   message_hbm, product_ref,
+                   taps_ref, k_ref, v_ref, q_ref, filter_ref, first_ref, turn_ref, second_ref, sems, message_ref, out_sems):
+    width = k_hbm.shape[1]
     pairs = (
         (taps_hbm, taps_ref),
-        (k_hbm, k_ref), (v_hbm, v_ref), (filter_hbm, filter_ref), (first_hbm, first_ref),
-        (q_hbm, q_ref), (turn_hbm, turn_ref), (second_hbm, second_ref), (w_hbm, w_ref),
+        (k_hbm, k_ref),
+        (v_hbm, v_ref),
+        (filter_hbm, filter_ref),
+        (first_hbm, first_ref),
+        (q_hbm.at[:, pl.ds(0, LANES)], q_ref.at[0]),
+        (q_hbm.at[:, pl.ds(width - LANES, LANES)], q_ref.at[1]),
+        (turn_hbm, turn_ref),
+        (second_hbm, second_ref),
     )
     copies = [pltpu.make_async_copy(source, target, sems.at[i]) for i, (source, target) in enumerate(pairs)]
     for copy in copies:
         copy.start()
-    rows = q_feat_ref.shape[0]
+    rows = product_ref.shape[0]
     per = rows // devices
-    own, own_chan = lax.axis_index("seq"), lax.axis_index("chan")
-    nothing = jnp.zeros((1, LANES), F32)
     lane = lax.broadcasted_iota(jnp.int32, (1, LANES), 1)
     copies[0].wait()
     taps = [[taps_ref[stream, :, j : j + 1] for j in range(3)] for stream in range(3)]
+    for copy in copies[1:]:
+        copy.wait()
+    key = k_ref[...].astype(F32).reshape(rows, LANES)
+    k_feat = featurized(key, taps, 1)
+    value = v_ref[...].astype(F32).reshape(rows, LANES)
+    v_feat = featurized(value, taps, 2)
+    product = k_feat.astype(F32) * v_feat.astype(F32)
+    product_ref[...] = product
+    signals = jnp.concatenate([product, filter_ref[...]], axis=1).astype(BF16)
+    values = dot(first_ref[...], signals).reshape(devices, 2, per, 2 * LANES)
+    edges = jnp.zeros((1, LANES), F32)
+    pieces = ((key[:1], key[rows - 1 :]), (value[:1], value[rows - 1 :]), (q_ref[0].astype(F32), q_ref[1].astype(F32)))
+    for i, (head, tail) in enumerate(pieces):
+        ends = jnp.where(lane < 2, head, jnp.where(lane < LANES - 2, 0.0, tail))
+        edges = edges + at_lanes(ends, 4 * i)
+    row = lax.broadcasted_iota(jnp.int32, (8, LANES), 0)
+    edges = jnp.where(row == 0, jnp.broadcast_to(edges, (8, LANES)), 0.0)[:PACK].astype(BF16)
+    packs = 4 * per // PACK
+    count = devices // CHUNKS
+    for chunk in range(CHUNKS):
+        part = slice(chunk * count, (chunk + 1) * count)
+        lines = slice(chunk * count * per, (chunk + 1) * count * per)
+        real, imag = values[part, 0], values[part, 1]
+        turn_real = turn_ref[0, lines].reshape(count, per, LANES)
+        turn_imag = turn_ref[1, lines].reshape(count, per, LANES)
+        packed = []
+        for signal in range(2):
+            lanes = slice(signal * LANES, (signal + 1) * LANES)
+            a, b = real[:, :, lanes], imag[:, :, lanes]
+            packed.append(
+                jnp.concatenate([a * turn_real + b * turn_imag, b * turn_real - a * turn_imag], axis=2)
+            )
+        packed = jnp.concatenate(packed, axis=1).reshape(2 * count * per, 2 * LANES).astype(BF16)
+        spectra = dot(packed, second_ref[...]).reshape(count, 2 * per, 2 * LANES)
+        spectra = jnp.concatenate(
+            [
+                spectra[:, :per, :LANES],
+                spectra[:, :per, LANES:],
+                spectra[:, per:, :LANES],
+                spectra[:, per:, LANES:],
+            ],
+            axis=1,
+        ).astype(BF16)
+        message_ref[part, :packs] = spectra.reshape(count, packs, PACK, LANES)
+        message_ref[part, packs] = jnp.broadcast_to(edges[None], (count, PACK, LANES))
+        copies.append(pltpu.make_async_copy(message_ref.at[part], message_hbm.at[part], out_sems.at[chunk]))
+        copies[-1].start()
+    for copy in copies[9:]:
+        copy.wait()
+
+
+def side_kernel(devices, taps_ref, q_ref, w_ref, q_feat_ref, scalars_ref):
+    rows = q_feat_ref.shape[0]
+    own_chan = lax.axis_index("chan")
+    lane = lax.broadcasted_iota(jnp.int32, (1, LANES), 1)
+    taps = [[taps_ref[stream, :, j : j + 1] for j in range(3)] for stream in range(3)]
     for j in range(3):
         scalars_ref[j : j + 1, :] = jnp.where(lane < 4, taps[1][j], jnp.where(lane < 8, taps[2][j], taps[0][j]))
-    copies[1].wait()
-    key = k_ref[...].astype(F32).reshape(rows, LANES)
-    k_feat = featurized(key, nothing, taps, 1)
-    copies[2].wait()
-    value = v_ref[...].astype(F32).reshape(rows, LANES)
-    v_feat = featurized(value, nothing, taps, 2)
-    product = k_feat.astype(F32) * v_feat.astype(F32)
-    skipped_ref[...] = product
-    copies[3].wait()
-    signals = jnp.concatenate([product, filter_ref[...]], axis=1).astype(BF16)
-    copies[4].wait()
-    values = dot(first_ref[...], signals).reshape(devices, 2, per, 2 * LANES)
-    copies[5].wait()
     query = q_ref[...].astype(F32).reshape(rows, LANES)
-    q_feat_ref[...] = featurized(query, nothing, taps, 0)
-    edges = nothing
-    for first, signal in enumerate((key, value, query)):
-        ends = jnp.where(lane < 2, signal[:1], jnp.where(lane < LANES - 2, 0.0, signal[rows - 1 :]))
-        edges = edges + at_lanes(ends, 4 * first)
-    row = lax.broadcasted_iota(jnp.int32, (8, LANES), 0)
-    edges = jnp.where(row == 0, jnp.broadcast_to(edges, (8, LANES)), 0.0)[:PACK]
-    copies[6].wait()
-    real, imag = values[:, 0], values[:, 1]
-    turn_real = turn_ref[0].reshape(devices, per, LANES)
-    turn_imag = turn_ref[1].reshape(devices, per, LANES)
-    packed = []
-    for signal in range(2):
-        lanes = slice(signal * LANES, (signal + 1) * LANES)
-        a, b = real[:, :, lanes], imag[:, :, lanes]
-        packed.append(
-            jnp.concatenate([a * turn_real + b * turn_imag, b * turn_real - a * turn_imag], axis=2)
-        )
-    packed = jnp.concatenate(packed, axis=1).reshape(2 * rows, 2 * LANES).astype(BF16)
-    copies[7].wait()
-    spectra = dot(packed, second_ref[...]).reshape(devices, 2 * per, 2 * LANES)
-    spectra = jnp.concatenate(
-        [
-            spectra[:, :per, :LANES],
-            spectra[:, :per, LANES:],
-            spectra[:, per:, :LANES],
-            spectra[:, per:, LANES:],
-        ],
-        axis=1,
-    ).astype(BF16)
-    packs = 4 * per // PACK
-    message_ref[:, :packs] = spectra.reshape(devices, packs, PACK, LANES)
-    message_ref[:, packs] = jnp.broadcast_to(edges.astype(BF16)[None], (devices, PACK, LANES))
-    copies[8].wait()
+    q_feat_ref[...] = featurized(query, taps, 0)
     chans = w_ref.shape[0]
     weights = w_ref[...].astype(F32)
     column = lax.broadcasted_iota(jnp.int32, weights.shape, 1)
@@ -259,27 +273,24 @@
     per = rows // devices
     near = chans // 2
     forward_first, turn, forward_second, inverse_second, inverse_first, basis = tables(rows, devices)
-    message, q_feat, skipped, scalars = pl.pallas_call(
+    message_shape = (devices, 4 * per // PACK + 1, PACK, LANES)
+    message, skipped = pl.pallas_call(
         functools.partial(forward_kernel, devices),
-        in_specs=[HBM] * 9,
-        out_specs=[VMEM] * 4,
-        out_shape=[
-            jax.ShapeDtypeStruct((devices, 4 * per // PACK + 1, PACK, LANES), BF16),
-            jax.ShapeDtypeStruct((rows, LANES), BF16),
-            jax.ShapeDtypeStruct((rows, LANES), F32),
-            jax.ShapeDtypeStruct((8 + 2 * chans, LANES), F32),
-        ],
+        in_specs=[HBM] * 8,
+        out_specs=[HBM, VMEM],
+        out_shape=[jax.ShapeDtypeStruct(message_shape, BF16), jax.ShapeDtypeStruct((rows, LANES), F32)],
         scratch_shapes=[
             pltpu.VMEM(short_taps.shape, F32),
             pltpu.VMEM((1, width), BF16),
             pltpu.VMEM((1, width), BF16),
-            pltpu.VMEM((1, width), BF16),
+            pltpu.VMEM((2, 1, LANES), BF16),
             pltpu.VMEM((rows, LANES), F32),
             pltpu.VMEM(forward_first.shape, BF16),
             pltpu.VMEM(turn.shape, F32),
             pltpu.VMEM(forward_second.shape, BF16),
-            pltpu.VMEM(w_out.shape, BF16),
             pltpu.SemaphoreType.DMA((9,)),
+            pltpu.VMEM(message_shape, BF16),
+            pltpu.SemaphoreType.DMA((CHUNKS,)),
         ],
         compiler_params=PARAMS,
         name="forward",
@@ -287,12 +298,20 @@
         *(
             pltpu.with_memory_space_constraint(jnp.asarray(operand), pltpu.HBM)
             for operand in (
-                short_taps,
-                query_in, key_in, value_in, long_filter.reshape(rows, LANES),
-                forward_first, turn, forward_second, w_out,
+                short_taps, key_in, value_in, query_in, long_filter.reshape(rows, LANES),
+                forward_first, turn, forward_second,
             )
         ),
     )
+    q_feat, scalars = pl.pallas_call(
+        functools.partial(side_kernel, devices),
+        in_specs=[VMEM] * 3,
+        out_specs=[VMEM] * 2,
+        out_shape=[jax.ShapeDtypeStruct((rows, LANES), BF16), jax.ShapeDtypeStruct((8 + 2 * chans, LANES), F32)],
+        compiler_params=PARAMS,
+        cost_estimate=pl.CostEstimate(flops=400_000, bytes_accessed=400_000, transcendentals=0),
+        name="side",
+    )(short_taps, query_in, w_out)
     message = lax.all_to_all(message, "seq", 0, 0)
     spectra, heads = pl.pallas_call(
         functools.partial(middle_kernel, devices),

time: 55.1 us -> 54.7 us (level)
  no operation moved by 1% of the time
where the time goes in v5:
time: 54.7 us; the launch traced here: 54.4 us
  starting transfers between devices  19.7 us (36%)
  waiting for transfers between devices  15.5 us (28%)
  blocking collectives  13.3 us (24%)
  Pallas kernels  5.06 us (9%)
  between operations  0.76 us (1%)
    all_to_all x1, blocking collectives, on_device(): spectra = lax.all_to_all(spectra, 'seq', 0, 0)  13.3 us
    all_to_all x1, starting transfers between devices, on_device(): message = lax.all_to_all(message, 'seq', 0, 0)  9.2 us
    all_to_all x1, waiting for transfers between devices, on_device(): message = lax.all_to_all(message, 'seq', 0, 0)  8.45 us
    ppermute x3, starting transfers between devices, on_device(): lax.ppermute(gating, 'chan', [(c, c // near * near + (c + step) % near) f...  5.9 us
    ppermute x1, starting transfers between devices, on_device(): lax.ppermute(other, 'chan', [(c, (c + near) % chans) for c in range(chans)])  4.58 us
    ppermute x1, waiting for transfers between devices, on_device(): lax.ppermute(other, 'chan', [(c, (c + near) % chans) for c in range(chans)])  4.13 us
    ppermute x3, waiting for transfers between devices, on_device(): lax.ppermute(gating, 'chan', [(c, c // near * near + (c + step) % near) f...  2.92 us
    pallas_call x1, Pallas kernels, on_device(): pl.pallas_call(functools.partial(forward_kernel, devices), in_specs=[HBM]...  2.68 us
  transfers between devices with their start and end apart: 5, of which 5 were waited for; matrix products, arithmetic and copies ran while one was open for 0% of the time, Pallas kernels for 0%

profile of v5, /device:TPU:2, one launch (start us, length us, event | category | flops | bytes accessed | tf_op | source)
XLA Modules:
  0.0 54.4 jit_solution(9727536959282204007)
XLA Ops:
  0.0 2.7 %forward.1 = (bf16[32,17,2,128]{3,2,1,0:T(2,128)(2,1)}, f32[256,128]{1,0:T(8,128)S(1)}) custom-call(f32[3,1,3]{2,1,0:T(1,128)} %taps_hbm.1, bf16[1,32768]{1,0:T(2,128)(2,1)} %k_hbm.1, bf16[1,32768]{1,0:T(2,128)(2,1)} %v_hbm.1, bf16[1,32768]{1,0:T(2,128)(2,1)} %q_hbm.1, f32[256,128]{1,0:T(8,128)} %bitcast.3, bf16[512,256]{1,0:T(8,128)(2,1)} %constant.12.clone.first_hbm, ...), custom_call_target="tpu_custom_call" | custom-call | tf_op jit(solution)/shard_map/forward/pallas_call | solution.py:277
  2.7 0.0 copy-start.1
  2.7 0.0 copy-start.5
  2.7 0.0 copy-start.6
  2.7 9.2 %all-to-all-start = ((bf16[32,17,2,128]{3,2,1,0:T(2,128)(2,1)}), bf16[32,17,2,128]{3,2,1,0:T(2,128)(2,1)S(1)}, u32[]{:S(2)}, u32[]{:S(2)}) async-start(bf16[32,17,2,128]{3,2,1,0:T(2,128)(2,1)} %get-tuple-element.14), calls=%async_computation | async-start | bytes 557056 | tf_op jit(solution)/shard_map/all_to_all | solution.py:315
  11.9 0.0 copy-done.1
  11.9 0.0 copy-done.5
  12.0 0.0 copy-done.6
  12.0 0.0 copy-start.4
  12.0 0.0 copy-start.3
  12.0 0.2 side.1
  12.9 8.5 %all-to-all-done = bf16[32,17,2,128]{3,2,1,0:T(2,128)(2,1)S(1)} async-done(((bf16[32,17,2,128]{3,2,1,0:T(2,128)(2,1)}), bf16[32,17,2,128]{3,2,1,0:T(2,128)(2,1)S(1)}, u32[]{:S(2)}, u32[]{:S(2)}) %all-to-all-start) | async-done | bytes 278560 | tf_op jit(solution)/shard_map/all_to_all | solution.py:315
  21.3 0.0 copy-done.4
  21.3 0.0 copy-start
  21.3 0.0 copy-start.2
  21.3 0.8 %middle.1 = (bf16[32,16,128]{2,1,0:T(8,128)(2,1)S(1)}, f32[8,128]{1,0:T(8,128)S(1)}) custom-call(f32[1]{0:T(128)S(6)} %copy.14.skip_ref, f32[24,128]{1,0:T(8,128)S(1)} %get-tuple-element.13.scalars_ref, bf16[1088,128]{1,0:T(8,128)(2,1)S(1)} %bitcast.2, f32[2,8,128]{2,1,0:T(8,128)S(1)} %copy-done.4), custom_call_target="tpu_custom_call" | custom-call | tf_op jit(solution)/shard_map/middle/pallas_call | solution.py:316
  22.1 13.3 %all_to_all.10.spectra_ref = bf16[32,16,128]{2,1,0:T(8,128)(2,1)S(1)} all-to-all(bf16[32,16,128]{2,1,0:T(8,128)(2,1)S(1)} %get-tuple-element.15), channel_id=1, replica_groups=mesh['seq'=32,'chan'=8] {'seq'}, dimensions={0} | all-to-all | bytes 262144 | tf_op jit(solution)/shard_map/all_to_all | solution.py:328
  35.5 0.0 copy-done.3
  35.5 0.0 copy-done
  35.5 0.0 copy-done.2
  35.5 0.5 inverse.1.refs_0_
  35.9 1.7 %collective-permute-start = (bf16[256,128]{1,0:T(8,128)(2,1)S(1)}, bf16[256,128]{1,0:T(8,128)(2,1)S(1)}, u32[]{:S(2)}, u32[]{:S(2)}) collective-permute-start(bf16[256,128]{1,0:T(8,128)(2,1)S(1)} %inverse.1.refs_0_), channel_id=1, source_target_pairs={{0,1},{1,2},{2,3},{3,0},{4,5},{5,6},{6,7},{7,4},{8,9},{9,10},{10,1... | collective-permute-start | bytes 196616 | tf_op jit(solution)/shard_map/ppermute | solution.py:338
  37.6 2.9 %collective-permute-start.1 = (bf16[256,128]{1,0:T(8,128)(2,1)S(1)}, bf16[256,128]{1,0:T(8,128)(2,1)S(1)}, u32[]{:S(2)}, u32[]{:S(2)}) collective-permute-start(bf16[256,128]{1,0:T(8,128)(2,1)S(1)} %inverse.1.refs_0_), channel_id=1, source_target_pairs={{0,2},{1,3},{2,0},{3,1},{4,6},{5,7},{6,4},{7,5},{8,10},{9,11},{10,... | collective-permute-start | bytes 196616 | tf_op jit(solution)/shard_map/ppermute | solution.py:338
  40.5 1.3 %collective-permute-start.2 = (bf16[256,128]{1,0:T(8,128)(2,1)S(1)}, bf16[256,128]{1,0:T(8,128)(2,1)S(1)}, u32[]{:S(2)}, u32[]{:S(2)}) collective-permute-start(bf16[256,128]{1,0:T(8,128)(2,1)S(1)} %inverse.1.refs_0_), channel_id=1, source_target_pairs={{0,3},{1,0},{2,1},{3,2},{4,7},{5,4},{6,5},{7,6},{8,11},{9,8},{10,9... | collective-permute-start | bytes 196616 | tf_op jit(solution)/shard_map/ppermute | solution.py:338
  41.8 0.4 collective-permute-done.refs_1_
  42.2 1.3 %collective-permute-done.1.refs_2_ = bf16[256,128]{1,0:T(8,128)(2,1)S(1)} collective-permute-done((bf16[256,128]{1,0:T(8,128)(2,1)S(1)}, bf16[256,128]{1,0:T(8,128)(2,1)S(1)}, u32[]{:S(2)}, u32[]{:S(2)}) %collective-permute-start.1) | collective-permute-done | bytes 65568 | tf_op jit(solution)/shard_map/ppermute | solution.py:338
  43.5 1.3 %collective-permute-done.2.refs_3_ = bf16[256,128]{1,0:T(8,128)(2,1)S(1)} collective-permute-done((bf16[256,128]{1,0:T(8,128)(2,1)S(1)}, bf16[256,128]{1,0:T(8,128)(2,1)S(1)}, u32[]{:S(2)}, u32[]{:S(2)}) %collective-permute-start.2) | collective-permute-done | bytes 65568 | tf_op jit(solution)/shard_map/ppermute | solution.py:338
  44.8 0.1 mix.1
  44.9 4.6 %collective-permute-start.3 = (bf16[256,128]{1,0:T(8,128)(2,1)S(1)}, bf16[256,128]{1,0:T(8,128)(2,1)S(1)}, u32[]{:S(2)}, u32[]{:S(2)}) collective-permute-start(bf16[256,128]{1,0:T(8,128)(2,1)S(1)} %get-tuple-element.20), channel_id=1, source_target_pairs={{0,4},{1,5},{2,6},{3,7},{4,0},{5,1},{6,2},{7,3},{8,12},{9,13},{10,... | collective-permute-start | bytes 196616 | tf_op jit(solution)/shard_map/ppermute | solution.py:349
  49.5 4.1 %collective-permute-done.3.other_ref = bf16[256,128]{1,0:T(8,128)(2,1)S(1)} collective-permute-done((bf16[256,128]{1,0:T(8,128)(2,1)S(1)}, bf16[256,128]{1,0:T(8,128)(2,1)S(1)}, u32[]{:S(2)}, u32[]{:S(2)}) %collective-permute-start.3) | collective-permute-done | bytes 65568 | tf_op jit(solution)/shard_map/ppermute | solution.py:349
  53.6 0.8 %add.1 = bf16[1,32768]{1,0:T(2,128)(2,1)} custom-call(f32[256,128]{1,0:T(8,128)S(1)} %get-tuple-element.19.own_ref, bf16[256,128]{1,0:T(8,128)(2,1)S(1)} %collective-permute-done.3.other_ref), custom_call_target="tpu_custom_call" | custom-call | tf_op jit(solution)/shard_map/add/pallas_call | solution.py:350
Async XLA Ops:
  2.7 9.2 %copy-start.1 = (bf16[1,32768]{1,0:T(2,128)(2,1)S(1)}, bf16[1,32768]{1,0:T(2,128)(2,1)}, u32[]{:S(2)}) copy-start(bf16[1,32768]{1,0:T(2,128)(2,1)} %q_hbm.1) | copy-start | bytes 196612
  2.7 9.2 %copy-start.5 = (f32[3,1,3]{2,1,0:T(1,128)S(1)}, f32[3,1,3]{2,1,0:T(1,128)}, u32[]{:S(2)}) copy-start(f32[3,1,3]{2,1,0:T(1,128)} %taps_hbm.1) | copy-start | bytes 112
  2.7 9.2 %copy-start.6 = (bf16[8,8]{1,0:T(8,128)(2,1)S(1)}, bf16[8,8]{1,0:T(8,128)(2,1)}, u32[]{:S(2)}) copy-start(bf16[8,8]{1,0:T(8,128)(2,1)} %w_ref.1) | copy-start | bytes 388
  2.7 18.6 %all-to-all-start = ((bf16[32,17,2,128]{3,2,1,0:T(2,128)(2,1)}), bf16[32,17,2,128]{3,2,1,0:T(2,128)(2,1)S(1)}, u32[]{:S(2)}, u32[]{:S(2)}) async-start(bf16[32,17,2,128]{3,2,1,0:T(2,128)(2,1)} %get-tuple-element.14), calls=%async_computation | async-start | bytes 557056 | tf_op jit(solution)/shard_map/all_to_all | solution.py:315
  12.0 9.4 %copy-start.4 = (f32[2,8,128]{2,1,0:T(8,128)S(1)}, f32[2,8,128]{2,1,0:T(8,128)}, u32[]{:S(2)}) copy-start(f32[2,8,128]{2,1,0:T(8,128)} %constant.15.clone.basis_ref) | copy-start | bytes 24580
  12.0 23.5 %copy-start.3 = (bf16[256,256]{1,0:T(8,128)(2,1)S(1)}, bf16[256,256]{1,0:T(8,128)(2,1)}, u32[]{:S(2)}) copy-start(bf16[256,256]{1,0:T(8,128)(2,1)} %constant.16.clone.second_ref) | copy-start | bytes 393220
  21.3 14.1 %copy-start = (f32[2,256,128]{2,1,0:T(8,128)S(1)}, f32[2,256,128]{2,1,0:T(8,128)}, u32[]{:S(2)}) copy-start(f32[2,256,128]{2,1,0:T(8,128)} %constant.13.clone.turn_hbm.turn_ref) | copy-start | bytes 786436
  21.3 14.1 %copy-start.2 = (bf16[256,512]{1,0:T(8,128)(2,1)S(1)}, bf16[256,512]{1,0:T(8,128)(2,1)}, u32[]{:S(2)}) copy-start(bf16[256,512]{1,0:T(8,128)(2,1)} %constant.17.clone.first_ref) | copy-start | bytes 786436
  35.9 6.3 %collective-permute-start = (bf16[256,128]{1,0:T(8,128)(2,1)S(1)}, bf16[256,128]{1,0:T(8,128)(2,1)S(1)}, u32[]{:S(2)}, u32[]{:S(2)}) collective-permute-start(bf16[256,128]{1,0:T(8,128)(2,1)S(1)} %inverse.1.refs_0_), channel_id=1, source_target_pairs={{0,1},{1,2},{2,3},{3,0},{4,5},{5,6},{6,7},{7,4},{8,9},{9,10},{10,1... | collective-permute-start | bytes 196616 | tf_op jit(solution)/shard_map/ppermute | solution.py:338
  37.6 5.9 %collective-permute-start.1 = (bf16[256,128]{1,0:T(8,128)(2,1)S(1)}, bf16[256,128]{1,0:T(8,128)(2,1)S(1)}, u32[]{:S(2)}, u32[]{:S(2)}) collective-permute-start(bf16[256,128]{1,0:T(8,128)(2,1)S(1)} %inverse.1.refs_0_), channel_id=1, source_target_pairs={{0,2},{1,3},{2,0},{3,1},{4,6},{5,7},{6,4},{7,5},{8,10},{9,11},{10,... | collective-permute-start | bytes 196616 | tf_op jit(solution)/shard_map/ppermute | solution.py:338
  40.5 4.3 %collective-permute-start.2 = (bf16[256,128]{1,0:T(8,128)(2,1)S(1)}, bf16[256,128]{1,0:T(8,128)(2,1)S(1)}, u32[]{:S(2)}, u32[]{:S(2)}) collective-permute-start(bf16[256,128]{1,0:T(8,128)(2,1)S(1)} %inverse.1.refs_0_), channel_id=1, source_target_pairs={{0,3},{1,0},{2,1},{3,2},{4,7},{5,4},{6,5},{7,6},{8,11},{9,8},{10,9... | collective-permute-start | bytes 196616 | tf_op jit(solution)/shard_map/ppermute | solution.py:338
  44.9 8.7 %collective-permute-start.3 = (bf16[256,128]{1,0:T(8,128)(2,1)S(1)}, bf16[256,128]{1,0:T(8,128)(2,1)S(1)}, u32[]{:S(2)}, u32[]{:S(2)}) collective-permute-start(bf16[256,128]{1,0:T(8,128)(2,1)S(1)} %get-tuple-element.20), channel_id=1, source_target_pairs={{0,4},{1,5},{2,6},{3,7},{4,0},{5,1},{6,2},{7,3},{8,12},{9,13},{10,... | collective-permute-start | bytes 196616 | tf_op jit(solution)/shard_map/ppermute | solution.py:349

commit v6 on v5

--- a/solution.py
+++ b/solution.py
@@ -43,6 +43,13 @@
         half(inverse_first),
         basis.astype(np.float32),
     )
+
+
+def members(devices):
+    if devices != 32:
+        return list(range(devices))
+    middle = (2, 1, 3, 0)
+    return [x * 8 + z * 2 + core for z in middle for x in middle for core in (1, 0)]
 
 
 def dot(left, right):
@@ -168,7 +175,10 @@
     per = (pitch - PACK) // 4
     message = message_ref[...].astype(F32)
     own = lax.axis_index("seq")
-    edges = jnp.concatenate([message[(p + 1) * pitch - PACK : (p + 1) * pitch - PACK + 1] for p in range(devices)], axis=0)
+    order = members(devices)
+    own_slice = sum(jnp.where(own == device, i, 0) for i, device in enumerate(order))
+    slabs = [order.index(p) * pitch for p in range(devices)]
+    edges = jnp.concatenate([message[slab + 4 * per : slab + 4 * per + 1] for slab in slabs], axis=0)
     before = jnp.concatenate([jnp.zeros((1, LANES), F32), edges[:-1]], axis=0)
     lane = lax.broadcasted_iota(jnp.int32, edges.shape, 1)
     taps = [scalars_ref[j : j + 1, :] for j in range(3)]
@@ -187,7 +197,7 @@
     for i in range(2):
         heads_ref[i : i + 1, :] = heads_scratch[i, pl.ds(own, 1), :]
     heads_ref[2:3, :] = jnp.full((1, LANES), skip_ref[0], F32)
-    angle = jnp.full((per, LANES), own, jnp.int32).astype(F32) * (2.0 * math.pi / (devices * LANES))
+    angle = jnp.full((per, LANES), own_slice, jnp.int32).astype(F32) * (2.0 * math.pi / (devices * LANES))
     square = angle * angle
     cos = 1.0 - square * (0.5 - square * (1.0 / 24.0))
     sin = angle * (1.0 - square * (1.0 / 6.0 - square * (1.0 / 120.0)))
@@ -196,7 +206,7 @@
     point_imag = basis_imag * cos - basis_real * sin
     blocks = []
     for p in range(devices):
-        aligned_ref[p] = message[p * pitch : p * pitch + 4 * per]
+        aligned_ref[p] = message[slabs[p] : slabs[p] + 4 * per]
     for p in range(devices):
         block = aligned_ref[p]
         real, imag = block[:per], block[per : 2 * per]
@@ -215,7 +225,7 @@
                 term = blocks[q][i] * blocks[p - q][3 + i]
                 sums[i] = term if sums[i] is None else sums[i] + term
         real, imag = sums[0] - sums[2], sums[0] + sums[1]
-        out_ref[p] = jnp.concatenate([real - behind_imag, imag + behind_real], axis=0).astype(BF16)
+        out_ref[order.index(p)] = jnp.concatenate([real - behind_imag, imag + behind_real], axis=0).astype(BF16)
         behind_real, behind_imag = real, imag
 
 
@@ -312,7 +322,8 @@
         cost_estimate=pl.CostEstimate(flops=400_000, bytes_accessed=400_000, transcendentals=0),
         name="side",
     )(short_taps, query_in, w_out)
-    message = lax.all_to_all(message, "seq", 0, 0)
+    group = [members(devices)]
+    message = lax.all_to_all(message, "seq", 0, 0, axis_index_groups=group)
     spectra, heads = pl.pallas_call(
         functools.partial(middle_kernel, devices),
         in_specs=[SMEM] + [VMEM] * 3,
@@ -325,7 +336,7 @@
         compiler_params=PARAMS,
         name="middle",
     )(skip_gain, scalars, message.reshape(-1, LANES), basis)
-    spectra = lax.all_to_all(spectra, "seq", 0, 0)
+    spectra = lax.all_to_all(spectra, "seq", 0, 0, axis_index_groups=group)
     gating = pl.pallas_call(
         functools.partial(inverse_kernel, devices),
         in_specs=[VMEM] * 7,

time: 54.7 us -> 49.8 us (0.910)
  waiting for transfers between devices: 15.5 us -> 13.2 us
  blocking collectives: 13.3 us -> 11.1 us
  starting transfers between devices: 19.7 us -> 19.1 us
    all_to_all x1, blocking collectives: 13.3 us -> 11.1 us  [on_device(): spectra = lax.all_to_all(spectra, 'seq', 0, 0, axis_index_groups=group)]
    all_to_all x1, waiting for transfers between devices: 8.45 us -> 7.04 us  [on_device(): message = lax.all_to_all(message, 'seq', 0, 0, axis_index_groups=group)]
    all_to_all x1, starting transfers between devices: 9.2 us -> 8.14 us  [on_device(): message = lax.all_to_all(message, 'seq', 0, 0, axis_index_groups=group)]
    ppermute x1, waiting for transfers between devices: 4.13 us -> 3.25 us  [on_device(): lax.ppermute(other, 'chan', [(c, (c + near) % chans) for c in range(chans)])]
  transfers between devices with their start and end apart: 5 -> 5, of which waited for: 5 -> 4; matrix products, arithmetic and copies ran while one was open for 0% -> 0% of each run, Pallas kernels for 0% -> 0%
where the time goes in v6:
time: 49.8 us; the launch traced here: 49.3 us
  starting transfers between devices  19.1 us (38%)
  waiting for transfers between devices  13.2 us (27%)
  blocking collectives  11.1 us (22%)
  Pallas kernels  5.07 us (10%)
  between operations  0.76 us (2%)
    all_to_all x1, blocking collectives, on_device(): spectra = lax.all_to_all(spectra, 'seq', 0, 0, axis_index_groups=group)  11.1 us
    all_to_all x1, starting transfers between devices, on_device(): message = lax.all_to_all(message, 'seq', 0, 0, axis_index_groups=group)  8.14 us
    all_to_all x1, waiting for transfers between devices, on_device(): message = lax.all_to_all(message, 'seq', 0, 0, axis_index_groups=group)  7.04 us
    ppermute x3, starting transfers between devices, on_device(): lax.ppermute(gating, 'chan', [(c, c // near * near + (c + step) % near) f...  5.9 us
    ppermute x1, starting transfers between devices, on_device(): lax.ppermute(other, 'chan', [(c, (c + near) % chans) for c in range(chans)])  5.01 us
    ppermute x1, waiting for transfers between devices, on_device(): lax.ppermute(other, 'chan', [(c, (c + near) % chans) for c in range(chans)])  3.25 us
    ppermute x3, waiting for transfers between devices, on_device(): lax.ppermute(gating, 'chan', [(c, c // near * near + (c + step) % near) f...  2.92 us
    pallas_call x1, Pallas kernels, on_device(): pl.pallas_call(functools.partial(forward_kernel, devices), in_specs=[HBM]...  2.68 us
  transfers between devices with their start and end apart: 5, of which 4 were waited for; matrix products, arithmetic and copies ran while one was open for 0% of the time, Pallas kernels for 0%

profile of v6, /device:TPU:2, one launch (start us, length us, event | category | flops | bytes accessed | tf_op | source)
XLA Modules:
  0.0 49.3 jit_solution(7797933171072636286)
XLA Ops:
  0.0 2.7 %forward.1 = (bf16[32,17,2,128]{3,2,1,0:T(2,128)(2,1)}, f32[256,128]{1,0:T(8,128)S(1)}) custom-call(f32[3,1,3]{2,1,0:T(1,128)} %taps_hbm.1, bf16[1,32768]{1,0:T(2,128)(2,1)} %k_hbm.1, bf16[1,32768]{1,0:T(2,128)(2,1)} %v_hbm.1, bf16[1,32768]{1,0:T(2,128)(2,1)} %q_hbm.1, f32[256,128]{1,0:T(8,128)} %bitcast.3, bf16[512,256]{1,0:T(8,128)(2,1)} %constant.12.clone.first_hbm, ...), custom_call_target="tpu_custom_call" | custom-call | tf_op jit(solution)/shard_map/forward/pallas_call | solution.py:287
  2.7 0.0 copy-start.1
  2.7 0.0 copy-start.5
  2.7 0.0 copy-start.6
  2.7 8.1 %all-to-all-start = ((bf16[32,17,2,128]{3,2,1,0:T(2,128)(2,1)}), bf16[32,17,2,128]{3,2,1,0:T(2,128)(2,1)S(1)}, u32[]{:S(2)}, u32[]{:S(2)}) async-start(bf16[32,17,2,128]{3,2,1,0:T(2,128)(2,1)} %get-tuple-element.14), calls=%async_computation | async-start | bytes 557056 | tf_op jit(solution)/shard_map/all_to_all | solution.py:326
  10.9 0.0 copy-done.1
  10.9 0.0 copy-done.5
  10.9 0.0 copy-done.6
  10.9 0.0 copy-start.4
  10.9 0.0 copy-start.3
  10.9 0.2 side.1
  11.8 7.0 %all-to-all-done = bf16[32,17,2,128]{3,2,1,0:T(2,128)(2,1)S(1)} async-done(((bf16[32,17,2,128]{3,2,1,0:T(2,128)(2,1)}), bf16[32,17,2,128]{3,2,1,0:T(2,128)(2,1)S(1)}, u32[]{:S(2)}, u32[]{:S(2)}) %all-to-all-start) | async-done | bytes 278560 | tf_op jit(solution)/shard_map/all_to_all | solution.py:326
  18.9 0.0 copy-done.4
  18.9 0.0 copy-start
  18.9 0.0 copy-start.2
  18.9 0.8 %middle.1 = (bf16[32,16,128]{2,1,0:T(8,128)(2,1)S(1)}, f32[8,128]{1,0:T(8,128)S(1)}) custom-call(f32[1]{0:T(128)S(6)} %copy.14.skip_ref, f32[24,128]{1,0:T(8,128)S(1)} %get-tuple-element.13.scalars_ref, bf16[1088,128]{1,0:T(8,128)(2,1)S(1)} %bitcast.2, f32[2,8,128]{2,1,0:T(8,128)S(1)} %copy-done.4), custom_call_target="tpu_custom_call" | custom-call | tf_op jit(solution)/shard_map/middle/pallas_call | solution.py:327
  19.7 11.1 %all_to_all.10.spectra_ref = bf16[32,16,128]{2,1,0:T(8,128)(2,1)S(1)} all-to-all(bf16[32,16,128]{2,1,0:T(8,128)(2,1)S(1)} %get-tuple-element.15), channel_id=1, replica_groups={{168,160,104,96,232,224,40,32,152,144,88,80,216,208,24,16,184,176,120,1..., dimensions={0} | all-to-all | bytes 262144 | tf_op jit(solution)/shard_map/all_to_all | solution.py:339
  30.8 0.0 copy-done.3
  30.8 0.0 copy-done
  30.8 0.0 copy-done.2
  30.8 0.5 inverse.1.refs_0_
  31.3 1.7 %collective-permute-start = (bf16[256,128]{1,0:T(8,128)(2,1)S(1)}, bf16[256,128]{1,0:T(8,128)(2,1)S(1)}, u32[]{:S(2)}, u32[]{:S(2)}) collective-permute-start(bf16[256,128]{1,0:T(8,128)(2,1)S(1)} %inverse.1.refs_0_), channel_id=1, source_target_pairs={{0,1},{1,2},{2,3},{3,0},{4,5},{5,6},{6,7},{7,4},{8,9},{9,10},{10,1... | collective-permute-start | bytes 196616 | tf_op jit(solution)/shard_map/ppermute | solution.py:349
  32.9 2.9 %collective-permute-start.1 = (bf16[256,128]{1,0:T(8,128)(2,1)S(1)}, bf16[256,128]{1,0:T(8,128)(2,1)S(1)}, u32[]{:S(2)}, u32[]{:S(2)}) collective-permute-start(bf16[256,128]{1,0:T(8,128)(2,1)S(1)} %inverse.1.refs_0_), channel_id=1, source_target_pairs={{0,2},{1,3},{2,0},{3,1},{4,6},{5,7},{6,4},{7,5},{8,10},{9,11},{10,... | collective-permute-start | bytes 196616 | tf_op jit(solution)/shard_map/ppermute | solution.py:349
  35.8 1.3 %collective-permute-start.2 = (bf16[256,128]{1,0:T(8,128)(2,1)S(1)}, bf16[256,128]{1,0:T(8,128)(2,1)S(1)}, u32[]{:S(2)}, u32[]{:S(2)}) collective-permute-start(bf16[256,128]{1,0:T(8,128)(2,1)S(1)} %inverse.1.refs_0_), channel_id=1, source_target_pairs={{0,3},{1,0},{2,1},{3,2},{4,7},{5,4},{6,5},{7,6},{8,11},{9,8},{10,9... | collective-permute-start | bytes 196616 | tf_op jit(solution)/shard_map/ppermute | solution.py:349
  37.2 0.0 collective-permute-done.refs_1_
  37.2 2.6 %collective-permute-done.1.refs_2_ = bf16[256,128]{1,0:T(8,128)(2,1)S(1)} collective-permute-done((bf16[256,128]{1,0:T(8,128)(2,1)S(1)}, bf16[256,128]{1,0:T(8,128)(2,1)S(1)}, u32[]{:S(2)}, u32[]{:S(2)}) %collective-permute-start.1) | collective-permute-done | bytes 65568 | tf_op jit(solution)/shard_map/ppermute | solution.py:349
  39.8 0.3 collective-permute-done.2.refs_3_
  40.1 0.1 mix.1
  40.2 5.0 %collective-permute-start.3 = (bf16[256,128]{1,0:T(8,128)(2,1)S(1)}, bf16[256,128]{1,0:T(8,128)(2,1)S(1)}, u32[]{:S(2)}, u32[]{:S(2)}) collective-permute-start(bf16[256,128]{1,0:T(8,128)(2,1)S(1)} %get-tuple-element.20), channel_id=1, source_target_pairs={{0,4},{1,5},{2,6},{3,7},{4,0},{5,1},{6,2},{7,3},{8,12},{9,13},{10,... | collective-permute-start | bytes 196616 | tf_op jit(solution)/shard_map/ppermute | solution.py:360
  45.2 3.2 %collective-permute-done.3.other_ref = bf16[256,128]{1,0:T(8,128)(2,1)S(1)} collective-permute-done((bf16[256,128]{1,0:T(8,128)(2,1)S(1)}, bf16[256,128]{1,0:T(8,128)(2,1)S(1)}, u32[]{:S(2)}, u32[]{:S(2)}) %collective-permute-start.3) | collective-permute-done | bytes 65568 | tf_op jit(solution)/shard_map/ppermute | solution.py:360
  48.5 0.8 %add.1 = bf16[1,32768]{1,0:T(2,128)(2,1)} custom-call(f32[256,128]{1,0:T(8,128)S(1)} %get-tuple-element.19.own_ref, bf16[256,128]{1,0:T(8,128)(2,1)S(1)} %collective-permute-done.3.other_ref), custom_call_target="tpu_custom_call" | custom-call | tf_op jit(solution)/shard_map/add/pallas_call | solution.py:361
Async XLA Ops:
  2.7 8.2 %copy-start.1 = (bf16[1,32768]{1,0:T(2,128)(2,1)S(1)}, bf16[1,32768]{1,0:T(2,128)(2,1)}, u32[]{:S(2)}) copy-start(bf16[1,32768]{1,0:T(2,128)(2,1)} %q_hbm.1) | copy-start | bytes 196612
  2.7 8.2 %copy-start.5 = (f32[3,1,3]{2,1,0:T(1,128)S(1)}, f32[3,1,3]{2,1,0:T(1,128)}, u32[]{:S(2)}) copy-start(f32[3,1,3]{2,1,0:T(1,128)} %taps_hbm.1) | copy-start | bytes 112
  2.7 8.2 %copy-start.6 = (bf16[8,8]{1,0:T(8,128)(2,1)S(1)}, bf16[8,8]{1,0:T(8,128)(2,1)}, u32[]{:S(2)}) copy-start(bf16[8,8]{1,0:T(8,128)(2,1)} %w_ref.1) | copy-start | bytes 388
  2.7 16.1 %all-to-all-start = ((bf16[32,17,2,128]{3,2,1,0:T(2,128)(2,1)}), bf16[32,17,2,128]{3,2,1,0:T(2,128)(2,1)S(1)}, u32[]{:S(2)}, u32[]{:S(2)}) async-start(bf16[32,17,2,128]{3,2,1,0:T(2,128)(2,1)} %get-tuple-element.14), calls=%async_computation | async-start | bytes 557056 | tf_op jit(solution)/shard_map/all_to_all | solution.py:326
  10.9 8.0 %copy-start.4 = (f32[2,8,128]{2,1,0:T(8,128)S(1)}, f32[2,8,128]{2,1,0:T(8,128)}, u32[]{:S(2)}) copy-start(f32[2,8,128]{2,1,0:T(8,128)} %constant.15.clone.basis_ref) | copy-start | bytes 24580
  10.9 19.9 %copy-start.3 = (bf16[256,256]{1,0:T(8,128)(2,1)S(1)}, bf16[256,256]{1,0:T(8,128)(2,1)}, u32[]{:S(2)}) copy-start(bf16[256,256]{1,0:T(8,128)(2,1)} %constant.16.clone.second_ref) | copy-start | bytes 393220
  18.9 12.0 %copy-start = (f32[2,256,128]{2,1,0:T(8,128)S(1)}, f32[2,256,128]{2,1,0:T(8,128)}, u32[]{:S(2)}) copy-start(f32[2,256,128]{2,1,0:T(8,128)} %constant.13.clone.turn_hbm.turn_ref) | copy-start | bytes 786436
  18.9 12.0 %copy-start.2 = (bf16[256,512]{1,0:T(8,128)(2,1)S(1)}, bf16[256,512]{1,0:T(8,128)(2,1)}, u32[]{:S(2)}) copy-start(bf16[256,512]{1,0:T(8,128)(2,1)} %constant.17.clone.first_ref) | copy-start | bytes 786436
  31.3 5.9 %collective-permute-start = (bf16[256,128]{1,0:T(8,128)(2,1)S(1)}, bf16[256,128]{1,0:T(8,128)(2,1)S(1)}, u32[]{:S(2)}, u32[]{:S(2)}) collective-permute-start(bf16[256,128]{1,0:T(8,128)(2,1)S(1)} %inverse.1.refs_0_), channel_id=1, source_target_pairs={{0,1},{1,2},{2,3},{3,0},{4,5},{5,6},{6,7},{7,4},{8,9},{9,10},{10,1... | collective-permute-start | bytes 196616 | tf_op jit(solution)/shard_map/ppermute | solution.py:349
  32.9 6.8 %collective-permute-start.1 = (bf16[256,128]{1,0:T(8,128)(2,1)S(1)}, bf16[256,128]{1,0:T(8,128)(2,1)S(1)}, u32[]{:S(2)}, u32[]{:S(2)}) collective-permute-start(bf16[256,128]{1,0:T(8,128)(2,1)S(1)} %inverse.1.refs_0_), channel_id=1, source_target_pairs={{0,2},{1,3},{2,0},{3,1},{4,6},{5,7},{6,4},{7,5},{8,10},{9,11},{10,... | collective-permute-start | bytes 196616 | tf_op jit(solution)/shard_map/ppermute | solution.py:349
  35.8 4.3 %collective-permute-start.2 = (bf16[256,128]{1,0:T(8,128)(2,1)S(1)}, bf16[256,128]{1,0:T(8,128)(2,1)S(1)}, u32[]{:S(2)}, u32[]{:S(2)}) collective-permute-start(bf16[256,128]{1,0:T(8,128)(2,1)S(1)} %inverse.1.refs_0_), channel_id=1, source_target_pairs={{0,3},{1,0},{2,1},{3,2},{4,7},{5,4},{6,5},{7,6},{8,11},{9,8},{10,9... | collective-permute-start | bytes 196616 | tf_op jit(solution)/shard_map/ppermute | solution.py:349
  40.2 8.3 %collective-permute-start.3 = (bf16[256,128]{1,0:T(8,128)(2,1)S(1)}, bf16[256,128]{1,0:T(8,128)(2,1)S(1)}, u32[]{:S(2)}, u32[]{:S(2)}) collective-permute-start(bf16[256,128]{1,0:T(8,128)(2,1)S(1)} %get-tuple-element.20), channel_id=1, source_target_pairs={{0,4},{1,5},{2,6},{3,7},{4,0},{5,1},{6,2},{7,3},{8,12},{9,13},{10,... | collective-permute-start | bytes 196616 | tf_op jit(solution)/shard_map/ppermute | solution.py:360

commit v7 on v6

--- a/solution.py
+++ b/solution.py
@@ -48,8 +48,7 @@
 def members(devices):
     if devices != 32:
         return list(range(devices))
-    middle = (2, 1, 3, 0)
-    return [x * 8 + z * 2 + core for z in middle for x in middle for core in (1, 0)]
+    return [x * 8 + z * 2 + core for z in (2, 3, 1, 0) for x in (2, 3, 1, 0) for core in (1, 0)]
 
 
 def dot(left, right):
@@ -98,7 +97,7 @@
     lane = lax.broadcasted_iota(jnp.int32, (1, LANES), 1)
     copies[0].wait()
     taps = [[taps_ref[stream, :, j : j + 1] for j in range(3)] for stream in range(3)]
-    for copy in copies[1:]:
+    for copy in copies[1:3]:
         copy.wait()
     key = k_ref[...].astype(F32).reshape(rows, LANES)
     k_feat = featurized(key, taps, 1)
@@ -106,6 +105,8 @@
     v_feat = featurized(value, taps, 2)
     product = k_feat.astype(F32) * v_feat.astype(F32)
     product_ref[...] = product
+    for copy in copies[3:]:
+        copy.wait()
     signals = jnp.concatenate([product, filter_ref[...]], axis=1).astype(BF16)
     values = dot(first_ref[...], signals).reshape(devices, 2, per, 2 * LANES)
     edges = jnp.zeros((1, LANES), F32)

time: 49.8 us -> 49.5 us (level)
  blocking collectives: 11.1 us -> 10.6 us
where the time goes in v7:
time: 49.5 us; the launch traced here: 48.8 us
  starting transfers between devices  19.1 us (39%)
  waiting for transfers between devices  13.4 us (27%)
  blocking collectives  10.6 us (21%)
  Pallas kernels  4.89 us (10%)
  between operations  0.76 us (2%)
    all_to_all x1, blocking collectives, on_device(): spectra = lax.all_to_all(spectra, 'seq', 0, 0, axis_index_groups=group)  10.6 us
    all_to_all x1, starting transfers between devices, on_device(): message = lax.all_to_all(message, 'seq', 0, 0, axis_index_groups=group)  8.15 us
    all_to_all x1, waiting for transfers between devices, on_device(): message = lax.all_to_all(message, 'seq', 0, 0, axis_index_groups=group)  7.25 us
    ppermute x3, starting transfers between devices, on_device(): lax.ppermute(gating, 'chan', [(c, c // near * near + (c + step) % near) f...  5.9 us
    ppermute x1, starting transfers between devices, on_device(): lax.ppermute(other, 'chan', [(c, (c + near) % chans) for c in range(chans)])  5.01 us
    ppermute x1, waiting for transfers between devices, on_device(): lax.ppermute(other, 'chan', [(c, (c + near) % chans) for c in range(chans)])  3.25 us
    ppermute x3, waiting for transfers between devices, on_device(): lax.ppermute(gating, 'chan', [(c, c // near * near + (c + step) % near) f...  2.92 us
    pallas_call x1, Pallas kernels, on_device(): pl.pallas_call(functools.partial(forward_kernel, devices), in_specs=[HBM]...  2.5 us
  transfers between devices with their start and end apart: 5, of which 4 were waited for; matrix products, arithmetic and copies ran while one was open for 0% of the time, Pallas kernels for 0%

profile of v7, /device:TPU:2, one launch (start us, length us, event | category | flops | bytes accessed | tf_op | source)
XLA Modules:
  0.0 48.8 jit_solution(8142895861002599739)
XLA Ops:
  0.0 2.5 %forward.1 = (bf16[32,17,2,128]{3,2,1,0:T(2,128)(2,1)}, f32[256,128]{1,0:T(8,128)S(1)}) custom-call(f32[3,1,3]{2,1,0:T(1,128)} %taps_hbm.1, bf16[1,32768]{1,0:T(2,128)(2,1)} %k_hbm.1, bf16[1,32768]{1,0:T(2,128)(2,1)} %v_hbm.1, bf16[1,32768]{1,0:T(2,128)(2,1)} %q_hbm.1, f32[256,128]{1,0:T(8,128)} %bitcast.3, bf16[512,256]{1,0:T(8,128)(2,1)} %constant.12.clone.first_hbm, ...), custom_call_target="tpu_custom_call" | custom-call | tf_op jit(solution)/shard_map/forward/pallas_call | solution.py:288
  2.5 0.0 copy-start.1
  2.5 0.0 copy-start.5
  2.5 0.0 copy-start.6
  2.5 8.1 %all-to-all-start = ((bf16[32,17,2,128]{3,2,1,0:T(2,128)(2,1)}), bf16[32,17,2,128]{3,2,1,0:T(2,128)(2,1)S(1)}, u32[]{:S(2)}, u32[]{:S(2)}) async-start(bf16[32,17,2,128]{3,2,1,0:T(2,128)(2,1)} %get-tuple-element.14), calls=%async_computation | async-start | bytes 557056 | tf_op jit(solution)/shard_map/all_to_all | solution.py:327
  10.7 0.0 copy-done.1
  10.7 0.0 copy-done.5
  10.7 0.0 copy-done.6
  10.7 0.0 copy-start.4
  10.7 0.0 copy-start.3
  10.8 0.2 side.1
  11.7 7.3 %all-to-all-done = bf16[32,17,2,128]{3,2,1,0:T(2,128)(2,1)S(1)} async-done(((bf16[32,17,2,128]{3,2,1,0:T(2,128)(2,1)}), bf16[32,17,2,128]{3,2,1,0:T(2,128)(2,1)S(1)}, u32[]{:S(2)}, u32[]{:S(2)}) %all-to-all-start) | async-done | bytes 278560 | tf_op jit(solution)/shard_map/all_to_all | solution.py:327
  18.9 0.0 copy-done.4
  18.9 0.0 copy-start
  18.9 0.0 copy-start.2
  18.9 0.8 %middle.1 = (bf16[32,16,128]{2,1,0:T(8,128)(2,1)S(1)}, f32[8,128]{1,0:T(8,128)S(1)}) custom-call(f32[1]{0:T(128)S(6)} %copy.14.skip_ref, f32[24,128]{1,0:T(8,128)S(1)} %get-tuple-element.13.scalars_ref, bf16[1088,128]{1,0:T(8,128)(2,1)S(1)} %bitcast.2, f32[2,8,128]{2,1,0:T(8,128)S(1)} %copy-done.4), custom_call_target="tpu_custom_call" | custom-call | tf_op jit(solution)/shard_map/middle/pallas_call | solution.py:328
  19.7 10.6 %all_to_all.10.spectra_ref = bf16[32,16,128]{2,1,0:T(8,128)(2,1)S(1)} all-to-all(bf16[32,16,128]{2,1,0:T(8,128)(2,1)S(1)} %get-tuple-element.15), channel_id=1, replica_groups={{168,160,232,224,104,96,40,32,184,176,248,240,120,112,56,48,152,144,216..., dimensions={0} | all-to-all | bytes 262144 | tf_op jit(solution)/shard_map/all_to_all | solution.py:340
  30.4 0.0 copy-done.3
  30.4 0.0 copy-done
  30.4 0.0 copy-done.2
  30.4 0.5 inverse.1.refs_0_
  30.8 1.7 %collective-permute-start = (bf16[256,128]{1,0:T(8,128)(2,1)S(1)}, bf16[256,128]{1,0:T(8,128)(2,1)S(1)}, u32[]{:S(2)}, u32[]{:S(2)}) collective-permute-start(bf16[256,128]{1,0:T(8,128)(2,1)S(1)} %inverse.1.refs_0_), channel_id=1, source_target_pairs={{0,1},{1,2},{2,3},{3,0},{4,5},{5,6},{6,7},{7,4},{8,9},{9,10},{10,1... | collective-permute-start | bytes 196616 | tf_op jit(solution)/shard_map/ppermute | solution.py:350
  32.5 2.9 %collective-permute-start.1 = (bf16[256,128]{1,0:T(8,128)(2,1)S(1)}, bf16[256,128]{1,0:T(8,128)(2,1)S(1)}, u32[]{:S(2)}, u32[]{:S(2)}) collective-permute-start(bf16[256,128]{1,0:T(8,128)(2,1)S(1)} %inverse.1.refs_0_), channel_id=1, source_target_pairs={{0,2},{1,3},{2,0},{3,1},{4,6},{5,7},{6,4},{7,5},{8,10},{9,11},{10,... | collective-permute-start | bytes 196616 | tf_op jit(solution)/shard_map/ppermute | solution.py:350
  35.4 1.3 %collective-permute-start.2 = (bf16[256,128]{1,0:T(8,128)(2,1)S(1)}, bf16[256,128]{1,0:T(8,128)(2,1)S(1)}, u32[]{:S(2)}, u32[]{:S(2)}) collective-permute-start(bf16[256,128]{1,0:T(8,128)(2,1)S(1)} %inverse.1.refs_0_), channel_id=1, source_target_pairs={{0,3},{1,0},{2,1},{3,2},{4,7},{5,4},{6,5},{7,6},{8,11},{9,8},{10,9... | collective-permute-start | bytes 196616 | tf_op jit(solution)/shard_map/ppermute | solution.py:350
  36.7 0.0 collective-permute-done.refs_1_
  36.7 2.5 %collective-permute-done.1.refs_2_ = bf16[256,128]{1,0:T(8,128)(2,1)S(1)} collective-permute-done((bf16[256,128]{1,0:T(8,128)(2,1)S(1)}, bf16[256,128]{1,0:T(8,128)(2,1)S(1)}, u32[]{:S(2)}, u32[]{:S(2)}) %collective-permute-start.1) | collective-permute-done | bytes 65568 | tf_op jit(solution)/shard_map/ppermute | solution.py:350
  39.2 0.4 collective-permute-done.2.refs_3_
  39.7 0.1 mix.1
  39.8 5.0 %collective-permute-start.3 = (bf16[256,128]{1,0:T(8,128)(2,1)S(1)}, bf16[256,128]{1,0:T(8,128)(2,1)S(1)}, u32[]{:S(2)}, u32[]{:S(2)}) collective-permute-start(bf16[256,128]{1,0:T(8,128)(2,1)S(1)} %get-tuple-element.20), channel_id=1, source_target_pairs={{0,4},{1,5},{2,6},{3,7},{4,0},{5,1},{6,2},{7,3},{8,12},{9,13},{10,... | collective-permute-start | bytes 196616 | tf_op jit(solution)/shard_map/ppermute | solution.py:361
  44.8 3.2 %collective-permute-done.3.other_ref = bf16[256,128]{1,0:T(8,128)(2,1)S(1)} collective-permute-done((bf16[256,128]{1,0:T(8,128)(2,1)S(1)}, bf16[256,128]{1,0:T(8,128)(2,1)S(1)}, u32[]{:S(2)}, u32[]{:S(2)}) %collective-permute-start.3) | collective-permute-done | bytes 65568 | tf_op jit(solution)/shard_map/ppermute | solution.py:361
  48.0 0.8 %add.1 = bf16[1,32768]{1,0:T(2,128)(2,1)} custom-call(f32[256,128]{1,0:T(8,128)S(1)} %get-tuple-element.19.own_ref, bf16[256,128]{1,0:T(8,128)(2,1)S(1)} %collective-permute-done.3.other_ref), custom_call_target="tpu_custom_call" | custom-call | tf_op jit(solution)/shard_map/add/pallas_call | solution.py:362
Async XLA Ops:
  2.5 8.2 %copy-start.1 = (bf16[1,32768]{1,0:T(2,128)(2,1)S(1)}, bf16[1,32768]{1,0:T(2,128)(2,1)}, u32[]{:S(2)}) copy-start(bf16[1,32768]{1,0:T(2,128)(2,1)} %q_hbm.1) | copy-start | bytes 196612
  2.5 8.2 %copy-start.5 = (f32[3,1,3]{2,1,0:T(1,128)S(1)}, f32[3,1,3]{2,1,0:T(1,128)}, u32[]{:S(2)}) copy-start(f32[3,1,3]{2,1,0:T(1,128)} %taps_hbm.1) | copy-start | bytes 112
  2.5 8.2 %copy-start.6 = (bf16[8,8]{1,0:T(8,128)(2,1)S(1)}, bf16[8,8]{1,0:T(8,128)(2,1)}, u32[]{:S(2)}) copy-start(bf16[8,8]{1,0:T(8,128)(2,1)} %w_ref.1) | copy-start | bytes 388
  2.5 16.4 %all-to-all-start = ((bf16[32,17,2,128]{3,2,1,0:T(2,128)(2,1)}), bf16[32,17,2,128]{3,2,1,0:T(2,128)(2,1)S(1)}, u32[]{:S(2)}, u32[]{:S(2)}) async-start(bf16[32,17,2,128]{3,2,1,0:T(2,128)(2,1)} %get-tuple-element.14), calls=%async_computation | async-start | bytes 557056 | tf_op jit(solution)/shard_map/all_to_all | solution.py:327
  10.7 8.2 %copy-start.4 = (f32[2,8,128]{2,1,0:T(8,128)S(1)}, f32[2,8,128]{2,1,0:T(8,128)}, u32[]{:S(2)}) copy-start(f32[2,8,128]{2,1,0:T(8,128)} %constant.15.clone.basis_ref) | copy-start | bytes 24580
  10.7 19.6 %copy-start.3 = (bf16[256,256]{1,0:T(8,128)(2,1)S(1)}, bf16[256,256]{1,0:T(8,128)(2,1)}, u32[]{:S(2)}) copy-start(bf16[256,256]{1,0:T(8,128)(2,1)} %constant.16.clone.second_ref) | copy-start | bytes 393220
  18.9 11.5 %copy-start = (f32[2,256,128]{2,1,0:T(8,128)S(1)}, f32[2,256,128]{2,1,0:T(8,128)}, u32[]{:S(2)}) copy-start(f32[2,256,128]{2,1,0:T(8,128)} %constant.13.clone.turn_hbm.turn_ref) | copy-start | bytes 786436
  18.9 11.5 %copy-start.2 = (bf16[256,512]{1,0:T(8,128)(2,1)S(1)}, bf16[256,512]{1,0:T(8,128)(2,1)}, u32[]{:S(2)}) copy-start(bf16[256,512]{1,0:T(8,128)(2,1)} %constant.17.clone.first_ref) | copy-start | bytes 786436
  30.8 5.9 %collective-permute-start = (bf16[256,128]{1,0:T(8,128)(2,1)S(1)}, bf16[256,128]{1,0:T(8,128)(2,1)S(1)}, u32[]{:S(2)}, u32[]{:S(2)}) collective-permute-start(bf16[256,128]{1,0:T(8,128)(2,1)S(1)} %inverse.1.refs_0_), channel_id=1, source_target_pairs={{0,1},{1,2},{2,3},{3,0},{4,5},{5,6},{6,7},{7,4},{8,9},{9,10},{10,1... | collective-permute-start | bytes 196616 | tf_op jit(solution)/shard_map/ppermute | solution.py:350
  32.5 6.7 %collective-permute-start.1 = (bf16[256,128]{1,0:T(8,128)(2,1)S(1)}, bf16[256,128]{1,0:T(8,128)(2,1)S(1)}, u32[]{:S(2)}, u32[]{:S(2)}) collective-permute-start(bf16[256,128]{1,0:T(8,128)(2,1)S(1)} %inverse.1.refs_0_), channel_id=1, source_target_pairs={{0,2},{1,3},{2,0},{3,1},{4,6},{5,7},{6,4},{7,5},{8,10},{9,11},{10,... | collective-permute-start | bytes 196616 | tf_op jit(solution)/shard_map/ppermute | solution.py:350
  35.4 4.3 %collective-permute-start.2 = (bf16[256,128]{1,0:T(8,128)(2,1)S(1)}, bf16[256,128]{1,0:T(8,128)(2,1)S(1)}, u32[]{:S(2)}, u32[]{:S(2)}) collective-permute-start(bf16[256,128]{1,0:T(8,128)(2,1)S(1)} %inverse.1.refs_0_), channel_id=1, source_target_pairs={{0,3},{1,0},{2,1},{3,2},{4,7},{5,4},{6,5},{7,6},{8,11},{9,8},{10,9... | collective-permute-start | bytes 196616 | tf_op jit(solution)/shard_map/ppermute | solution.py:350
  39.8 8.3 %collective-permute-start.3 = (bf16[256,128]{1,0:T(8,128)(2,1)S(1)}, bf16[256,128]{1,0:T(8,128)(2,1)S(1)}, u32[]{:S(2)}, u32[]{:S(2)}) collective-permute-start(bf16[256,128]{1,0:T(8,128)(2,1)S(1)} %get-tuple-element.20), channel_id=1, source_target_pairs={{0,4},{1,5},{2,6},{3,7},{4,0},{5,1},{6,2},{7,3},{8,12},{9,13},{10,... | collective-permute-start | bytes 196616 | tf_op jit(solution)/shard_map/ppermute | solution.py:361

commit v8 on v6

--- a/solution.py
+++ b/solution.py
@@ -48,8 +48,7 @@
 def members(devices):
     if devices != 32:
         return list(range(devices))
-    middle = (2, 1, 3, 0)
-    return [x * 8 + z * 2 + core for z in middle for x in middle for core in (1, 0)]
+    return [x * 8 + z * 2 + core for z in (2, 3, 1, 0) for x in (2, 3, 1, 0) for core in (1, 0)]
 
 
 def dot(left, right):
@@ -160,10 +159,13 @@
     q_feat_ref[...] = featurized(query, taps, 0)
     chans = w_ref.shape[0]
     weights = w_ref[...].astype(F32)
-    column = lax.broadcasted_iota(jnp.int32, weights.shape, 1)
-    for i, chan in enumerate((own_chan, (own_chan + chans // 2) % chans)):
-        picked = jnp.sum(jnp.where(column == chan, weights, 0.0), axis=1, keepdims=True)
-        scalars_ref[8 + i * chans : 8 + (i + 1) * chans, :] = jnp.broadcast_to(picked, (chans, LANES))
+    row = lax.broadcasted_iota(jnp.int32, weights.shape, 0)
+    for half in range(2):
+        chan = (own_chan + half * (chans // 2)) % chans
+        picked = jnp.sum(jnp.where(row == chan, weights, 0.0), axis=0, keepdims=True)
+        for d in range(chans):
+            index = 8 + half * chans + d
+            scalars_ref[index : index + 1, :] = jnp.broadcast_to(picked[:, d : d + 1], (1, LANES))
 
 
 def rounded(values):
@@ -249,26 +251,25 @@
     gating_ref[...] = gating
 
 
-def mix_kernel(scalars_ref, *refs):
-    *gating_refs, own_ref, other_ref = refs
-    near = len(gating_refs)
-    chans = 2 * near
+def mix_kernel(scalars_ref, own_gating_ref, other_gating_ref, own_ref, *message_refs):
+    near = len(message_refs) + 1
     own_chan = lax.axis_index("chan")
-    start = 8 + own_chan // near * near
-    own = other = None
-    for step, gating_ref in enumerate(gating_refs):
-        gating = gating_ref[...].astype(F32)
-        row = start + (own_chan + near - step) % near
-        to_own = scalars_ref[pl.ds(row, 1), :] * gating
-        to_other = scalars_ref[pl.ds(row + chans, 1), :] * gating
-        own = to_own if own is None else own + to_own
-        other = to_other if other is None else other + to_other
-    own_ref[...] = own
-    other_ref[...] = other.astype(BF16)
-
-
-def add_kernel(own_ref, other_ref, out_ref):
-    out_ref[...] = (own_ref[...] + other_ref[...].astype(F32)).reshape(out_ref.shape).astype(BF16)
+    own, other = own_gating_ref[...].astype(F32), other_gating_ref[...].astype(F32)
+    for step in range(near):
+        to = 8 + own_chan // near * near + (own_chan + step) % near
+        total = scalars_ref[pl.ds(to, 1), :] * own + scalars_ref[pl.ds(to + 2 * near, 1), :] * other
+        if step == 0:
+            own_ref[...] = total
+        else:
+            message_refs[step - 1][...] = total.astype(BF16)
+
+
+def add_kernel(own_ref, *refs):
+    *message_refs, out_ref = refs
+    total = own_ref[...]
+    for message_ref in message_refs:
+        total = total + message_ref[...].astype(F32)
+    out_ref[...] = total.reshape(out_ref.shape).astype(BF16)
 
 
 SMEM = pl.BlockSpec(memory_space=pltpu.SMEM)
@@ -345,27 +346,27 @@
         compiler_params=PARAMS,
         name="inverse",
     )(spectra, turn, inverse_second, inverse_first, q_feat, skipped, heads)
-    gathered = [gating] + [
-        lax.ppermute(gating, "chan", [(c, c // near * near + (c + step) % near) for c in range(chans)])
-        for step in range(1, near)
+    other_gating = lax.ppermute(gating, "chan", [(c, (c + near) % chans) for c in range(chans)])
+    own, *messages = pl.pallas_call(
+        mix_kernel,
+        in_specs=[VMEM] * 3,
+        out_specs=[VMEM] * near,
+        out_shape=[jax.ShapeDtypeStruct((rows, LANES), BF16 if step else F32) for step in range(near)],
+        compiler_params=PARAMS,
+        name="mix",
+    )(scalars, gating, other_gating)
+    messages = [
+        lax.ppermute(message, "chan", [(c, c // near * near + (c + step) % near) for c in range(chans)])
+        for step, message in enumerate(messages, 1)
     ]
-    own, other = pl.pallas_call(
-        mix_kernel,
-        in_specs=[VMEM] * (near + 1),
-        out_specs=[VMEM] * 2,
-        out_shape=[jax.ShapeDtypeStruct((rows, LANES), F32), jax.ShapeDtypeStruct((rows, LANES), BF16)],
-        compiler_params=PARAMS,
-        name="mix",
-    )(scalars, *gathered)
-    other = lax.ppermute(other, "chan", [(c, (c + near) % chans) for c in range(chans)])
     return pl.pallas_call(
         add_kernel,
-        in_specs=[VMEM] * 2,
+        in_specs=[VMEM] * near,
         out_specs=VMEM,
         out_shape=jax.ShapeDtypeStruct((1, width), BF16),
         compiler_params=PARAMS,
         name="add",
-    )(own, other)
+    )(own, *messages)
 
 
 def solution(mesh):

time: 49.8 us -> 49.7 us (level)
  blocking collectives: 11.1 us -> 10.6 us
  waiting for transfers between devices: 13.2 us -> 13.7 us
  transfers between devices with their start and end apart: 5 -> 5, of which waited for: 4 -> 5; matrix products, arithmetic and copies ran while one was open for 0% -> 0% of each run, Pallas kernels for 0% -> 0%
where the time goes in v8:
time: 49.7 us; the launch traced here: 49.3 us
  starting transfers between devices  19.1 us (38%)
  waiting for transfers between devices  13.7 us (28%)
  blocking collectives  10.6 us (21%)
  Pallas kernels  5.04 us (10%)
  between operations  0.76 us (2%)
    all_to_all x1, blocking collectives, on_device(): spectra = lax.all_to_all(spectra, 'seq', 0, 0, axis_index_groups=group)  10.6 us
    all_to_all x1, starting transfers between devices, on_device(): message = lax.all_to_all(message, 'seq', 0, 0, axis_index_groups=group)  8.15 us
    all_to_all x1, waiting for transfers between devices, on_device(): message = lax.all_to_all(message, 'seq', 0, 0, axis_index_groups=group)  7.26 us
    ppermute x3, starting transfers between devices, on_device(): lax.ppermute(message, 'chan', [(c, c // near * near + (c + step) % near)...  5.9 us
    ppermute x1, starting transfers between devices, on_device(): lax.ppermute(gating, 'chan', [(c, (c + near) % chans) for c in range(chan...  5.01 us
    ppermute x1, waiting for transfers between devices, on_device(): lax.ppermute(gating, 'chan', [(c, (c + near) % chans) for c in range(chan...  3.55 us
    ppermute x3, waiting for transfers between devices, on_device(): lax.ppermute(message, 'chan', [(c, c // near * near + (c + step) % near)...  2.92 us
    pallas_call x1, Pallas kernels, on_device(): pl.pallas_call(functools.partial(forward_kernel, devices), in_specs=[HBM]...  2.68 us
  transfers between devices with their start and end apart: 5, of which 5 were waited for; matrix products, arithmetic and copies ran while one was open for 0% of the time, Pallas kernels for 0%

profile of v8, /device:TPU:2, one launch (start us, length us, event | category | flops | bytes accessed | tf_op | source)
XLA Modules:
  0.0 49.3 jit_solution(8328769641990653576)
XLA Ops:
  0.0 2.7 %forward.1 = (bf16[32,17,2,128]{3,2,1,0:T(2,128)(2,1)}, f32[256,128]{1,0:T(8,128)S(1)}) custom-call(f32[3,1,3]{2,1,0:T(1,128)} %taps_hbm.1, bf16[1,32768]{1,0:T(2,128)(2,1)} %k_hbm.1, bf16[1,32768]{1,0:T(2,128)(2,1)} %v_hbm.1, bf16[1,32768]{1,0:T(2,128)(2,1)} %q_hbm.1, f32[256,128]{1,0:T(8,128)} %bitcast.3, bf16[512,256]{1,0:T(8,128)(2,1)} %constant.12.clone.first_hbm, ...), custom_call_target="tpu_custom_call" | custom-call | tf_op jit(solution)/shard_map/forward/pallas_call | solution.py:288
  2.7 0.0 copy-start.1
  2.7 0.0 copy-start.5
  2.7 0.0 copy-start.6
  2.7 8.2 %all-to-all-start = ((bf16[32,17,2,128]{3,2,1,0:T(2,128)(2,1)}), bf16[32,17,2,128]{3,2,1,0:T(2,128)(2,1)S(1)}, u32[]{:S(2)}, u32[]{:S(2)}) async-start(bf16[32,17,2,128]{3,2,1,0:T(2,128)(2,1)} %get-tuple-element.16), calls=%async_computation | async-start | bytes 557056 | tf_op jit(solution)/shard_map/all_to_all | solution.py:327
  10.9 0.0 copy-done.1
  10.9 0.0 copy-done.5
  10.9 0.0 copy-done.6
  10.9 0.0 copy-start.4
  10.9 0.0 copy-start.3
  10.9 0.2 side.1
  11.8 7.3 %all-to-all-done = bf16[32,17,2,128]{3,2,1,0:T(2,128)(2,1)S(1)} async-done(((bf16[32,17,2,128]{3,2,1,0:T(2,128)(2,1)}), bf16[32,17,2,128]{3,2,1,0:T(2,128)(2,1)S(1)}, u32[]{:S(2)}, u32[]{:S(2)}) %all-to-all-start) | async-done | bytes 278560 | tf_op jit(solution)/shard_map/all_to_all | solution.py:327
  19.1 0.0 copy-done.4
  19.1 0.0 copy-start
  19.1 0.0 copy-start.2
  19.1 0.8 %middle.1 = (bf16[32,16,128]{2,1,0:T(8,128)(2,1)S(1)}, f32[8,128]{1,0:T(8,128)S(1)}) custom-call(f32[1]{0:T(128)S(6)} %copy.14.skip_ref, f32[24,128]{1,0:T(8,128)S(1)} %get-tuple-element.15.scalars_ref, bf16[1088,128]{1,0:T(8,128)(2,1)S(1)} %bitcast.2, f32[2,8,128]{2,1,0:T(8,128)S(1)} %copy-done.4), custom_call_target="tpu_custom_call" | custom-call | tf_op jit(solution)/shard_map/middle/pallas_call | solution.py:328
  19.9 10.6 %all_to_all.10.spectra_ref = bf16[32,16,128]{2,1,0:T(8,128)(2,1)S(1)} all-to-all(bf16[32,16,128]{2,1,0:T(8,128)(2,1)S(1)} %get-tuple-element.17), channel_id=1, replica_groups={{168,160,232,224,104,96,40,32,184,176,248,240,120,112,56,48,152,144,216..., dimensions={0} | all-to-all | bytes 262144 | tf_op jit(solution)/shard_map/all_to_all | solution.py:340
  30.5 0.0 copy-done.3
  30.5 0.0 copy-done
  30.5 0.0 copy-done.2
  30.6 0.5 inverse.1.own_gating_ref
  31.0 5.0 %collective-permute-start = (bf16[256,128]{1,0:T(8,128)(2,1)S(1)}, bf16[256,128]{1,0:T(8,128)(2,1)S(1)}, u32[]{:S(2)}, u32[]{:S(2)}) collective-permute-start(bf16[256,128]{1,0:T(8,128)(2,1)S(1)} %inverse.1.own_gating_ref), channel_id=1, source_target_pairs={{0,4},{1,5},{2,6},{3,7},{4,0},{5,1},{6,2},{7,3},{8,12},{9,13},{10,... | collective-permute-start | bytes 196616 | tf_op jit(solution)/shard_map/ppermute | solution.py:349
  36.0 3.6 %collective-permute-done.other_gating_ref = bf16[256,128]{1,0:T(8,128)(2,1)S(1)} collective-permute-done((bf16[256,128]{1,0:T(8,128)(2,1)S(1)}, bf16[256,128]{1,0:T(8,128)(2,1)S(1)}, u32[]{:S(2)}, u32[]{:S(2)}) %collective-permute-start) | collective-permute-done | bytes 65568 | tf_op jit(solution)/shard_map/ppermute | solution.py:349
  39.6 0.1 mix.1
  39.7 1.7 %collective-permute-start.1 = (bf16[256,128]{1,0:T(8,128)(2,1)S(1)}, bf16[256,128]{1,0:T(8,128)(2,1)S(1)}, u32[]{:S(2)}, u32[]{:S(2)}) collective-permute-start(bf16[256,128]{1,0:T(8,128)(2,1)S(1)} %get-tuple-element.22), channel_id=1, source_target_pairs={{0,1},{1,2},{2,3},{3,0},{4,5},{5,6},{6,7},{7,4},{8,9},{9,10},{10,1... | collective-permute-start | bytes 196616 | tf_op jit(solution)/shard_map/ppermute | solution.py:359
  41.3 2.9 %collective-permute-start.2 = (bf16[256,128]{1,0:T(8,128)(2,1)S(1)}, bf16[256,128]{1,0:T(8,128)(2,1)S(1)}, u32[]{:S(2)}, u32[]{:S(2)}) collective-permute-start(bf16[256,128]{1,0:T(8,128)(2,1)S(1)} %get-tuple-element.23), channel_id=1, source_target_pairs={{0,2},{1,3},{2,0},{3,1},{4,6},{5,7},{6,4},{7,5},{8,10},{9,11},{10,... | collective-permute-start | bytes 196616 | tf_op jit(solution)/shard_map/ppermute | solution.py:359
  44.2 1.3 %collective-permute-start.3 = (bf16[256,128]{1,0:T(8,128)(2,1)S(1)}, bf16[256,128]{1,0:T(8,128)(2,1)S(1)}, u32[]{:S(2)}, u32[]{:S(2)}) collective-permute-start(bf16[256,128]{1,0:T(8,128)(2,1)S(1)} %get-tuple-element.24), channel_id=1, source_target_pairs={{0,3},{1,0},{2,1},{3,2},{4,7},{5,4},{6,5},{7,6},{8,11},{9,8},{10,9... | collective-permute-start | bytes 196616 | tf_op jit(solution)/shard_map/ppermute | solution.py:359
  45.6 0.4 collective-permute-done.1.refs_0_
  45.9 1.3 %collective-permute-done.2.refs_1_ = bf16[256,128]{1,0:T(8,128)(2,1)S(1)} collective-permute-done((bf16[256,128]{1,0:T(8,128)(2,1)S(1)}, bf16[256,128]{1,0:T(8,128)(2,1)S(1)}, u32[]{:S(2)}, u32[]{:S(2)}) %collective-permute-start.2) | collective-permute-done | bytes 65568 | tf_op jit(solution)/shard_map/ppermute | solution.py:359
  47.2 1.3 %collective-permute-done.3.refs_2_ = bf16[256,128]{1,0:T(8,128)(2,1)S(1)} collective-permute-done((bf16[256,128]{1,0:T(8,128)(2,1)S(1)}, bf16[256,128]{1,0:T(8,128)(2,1)S(1)}, u32[]{:S(2)}, u32[]{:S(2)}) %collective-permute-start.3) | collective-permute-done | bytes 65568 | tf_op jit(solution)/shard_map/ppermute | solution.py:359
  48.5 0.8 %add.1 = bf16[1,32768]{1,0:T(2,128)(2,1)} custom-call(f32[256,128]{1,0:T(8,128)S(1)} %get-tuple-element.21.own_ref, bf16[256,128]{1,0:T(8,128)(2,1)S(1)} %collective-permute-done.1.refs_0_, bf16[256,128]{1,0:T(8,128)(2,1)S(1)} %collective-permute-done.2.refs_1_, bf16[256,128]{1,0:T(8,128)(2,1)S(1)} %collective-permute-done.3.refs_2_), custom_call_target="tpu_custom_call" | custom-call | tf_op jit(solution)/shard_map/add/pallas_call | solution.py:362
Async XLA Ops:
  2.7 8.2 %copy-start.1 = (bf16[1,32768]{1,0:T(2,128)(2,1)S(1)}, bf16[1,32768]{1,0:T(2,128)(2,1)}, u32[]{:S(2)}) copy-start(bf16[1,32768]{1,0:T(2,128)(2,1)} %q_hbm.1) | copy-start | bytes 196612
  2.7 8.2 %copy-start.5 = (f32[3,1,3]{2,1,0:T(1,128)S(1)}, f32[3,1,3]{2,1,0:T(1,128)}, u32[]{:S(2)}) copy-start(f32[3,1,3]{2,1,0:T(1,128)} %taps_hbm.1) | copy-start | bytes 112
  2.7 8.2 %copy-start.6 = (bf16[8,8]{1,0:T(8,128)(2,1)S(1)}, bf16[8,8]{1,0:T(8,128)(2,1)}, u32[]{:S(2)}) copy-start(bf16[8,8]{1,0:T(8,128)(2,1)} %w_ref.1) | copy-start | bytes 388
  2.7 16.4 %all-to-all-start = ((bf16[32,17,2,128]{3,2,1,0:T(2,128)(2,1)}), bf16[32,17,2,128]{3,2,1,0:T(2,128)(2,1)S(1)}, u32[]{:S(2)}, u32[]{:S(2)}) async-start(bf16[32,17,2,128]{3,2,1,0:T(2,128)(2,1)} %get-tuple-element.16), calls=%async_computation | async-start | bytes 557056 | tf_op jit(solution)/shard_map/all_to_all | solution.py:327
  10.9 8.2 %copy-start.4 = (f32[2,8,128]{2,1,0:T(8,128)S(1)}, f32[2,8,128]{2,1,0:T(8,128)}, u32[]{:S(2)}) copy-start(f32[2,8,128]{2,1,0:T(8,128)} %constant.15.clone.basis_ref) | copy-start | bytes 24580
  10.9 19.6 %copy-start.3 = (bf16[256,256]{1,0:T(8,128)(2,1)S(1)}, bf16[256,256]{1,0:T(8,128)(2,1)}, u32[]{:S(2)}) copy-start(bf16[256,256]{1,0:T(8,128)(2,1)} %constant.16.clone.second_ref) | copy-start | bytes 393220
  19.1 11.5 %copy-start = (f32[2,256,128]{2,1,0:T(8,128)S(1)}, f32[2,256,128]{2,1,0:T(8,128)}, u32[]{:S(2)}) copy-start(f32[2,256,128]{2,1,0:T(8,128)} %constant.13.clone.turn_hbm.turn_ref) | copy-start | bytes 786436
  19.1 11.5 %copy-start.2 = (bf16[256,512]{1,0:T(8,128)(2,1)S(1)}, bf16[256,512]{1,0:T(8,128)(2,1)}, u32[]{:S(2)}) copy-start(bf16[256,512]{1,0:T(8,128)(2,1)} %constant.17.clone.first_ref) | copy-start | bytes 786436
  31.0 8.6 %collective-permute-start = (bf16[256,128]{1,0:T(8,128)(2,1)S(1)}, bf16[256,128]{1,0:T(8,128)(2,1)S(1)}, u32[]{:S(2)}, u32[]{:S(2)}) collective-permute-start(bf16[256,128]{1,0:T(8,128)(2,1)S(1)} %inverse.1.own_gating_ref), channel_id=1, source_target_pairs={{0,4},{1,5},{2,6},{3,7},{4,0},{5,1},{6,2},{7,3},{8,12},{9,13},{10,... | collective-permute-start | bytes 196616 | tf_op jit(solution)/shard_map/ppermute | solution.py:349
  39.7 6.3 %collective-permute-start.1 = (bf16[256,128]{1,0:T(8,128)(2,1)S(1)}, bf16[256,128]{1,0:T(8,128)(2,1)S(1)}, u32[]{:S(2)}, u32[]{:S(2)}) collective-permute-start(bf16[256,128]{1,0:T(8,128)(2,1)S(1)} %get-tuple-element.22), channel_id=1, source_target_pairs={{0,1},{1,2},{2,3},{3,0},{4,5},{5,6},{6,7},{7,4},{8,9},{9,10},{10,1... | collective-permute-start | bytes 196616 | tf_op jit(solution)/shard_map/ppermute | solution.py:359
  41.3 5.9 %collective-permute-start.2 = (bf16[256,128]{1,0:T(8,128)(2,1)S(1)}, bf16[256,128]{1,0:T(8,128)(2,1)S(1)}, u32[]{:S(2)}, u32[]{:S(2)}) collective-permute-start(bf16[256,128]{1,0:T(8,128)(2,1)S(1)} %get-tuple-element.23), channel_id=1, source_target_pairs={{0,2},{1,3},{2,0},{3,1},{4,6},{5,7},{6,4},{7,5},{8,10},{9,11},{10,... | collective-permute-start | bytes 196616 | tf_op jit(solution)/shard_map/ppermute | solution.py:359
  44.2 4.3 %collective-permute-start.3 = (bf16[256,128]{1,0:T(8,128)(2,1)S(1)}, bf16[256,128]{1,0:T(8,128)(2,1)S(1)}, u32[]{:S(2)}, u32[]{:S(2)}) collective-permute-start(bf16[256,128]{1,0:T(8,128)(2,1)S(1)} %get-tuple-element.24), channel_id=1, source_target_pairs={{0,3},{1,0},{2,1},{3,2},{4,7},{5,4},{6,5},{7,6},{8,11},{9,8},{10,9... | collective-permute-start | bytes 196616 | tf_op jit(solution)/shard_map/ppermute | solution.py:359

commit v9 on v8

--- a/solution.py
+++ b/solution.py
@@ -97,7 +97,7 @@
     lane = lax.broadcasted_iota(jnp.int32, (1, LANES), 1)
     copies[0].wait()
     taps = [[taps_ref[stream, :, j : j + 1] for j in range(3)] for stream in range(3)]
-    for copy in copies[1:]:
+    for copy in copies[1:3]:
         copy.wait()
     key = k_ref[...].astype(F32).reshape(rows, LANES)
     k_feat = featurized(key, taps, 1)
@@ -105,6 +105,8 @@
     v_feat = featurized(value, taps, 2)
     product = k_feat.astype(F32) * v_feat.astype(F32)
     product_ref[...] = product
+    for copy in copies[3:]:
+        copy.wait()
     signals = jnp.concatenate([product, filter_ref[...]], axis=1).astype(BF16)
     values = dot(first_ref[...], signals).reshape(devices, 2, per, 2 * LANES)
     edges = jnp.zeros((1, LANES), F32)

time: 49.7 us -> 49.5 us (level)
  no operation moved by 1% of the time
where the time goes in v9:
time: 49.5 us; the launch traced here: 49.1 us
  starting transfers between devices  19.1 us (39%)
  waiting for transfers between devices  13.7 us (28%)
  blocking collectives  10.6 us (21%)
  Pallas kernels  4.86 us (10%)
  between operations  0.76 us (2%)
    all_to_all x1, blocking collectives, on_device(): spectra = lax.all_to_all(spectra, 'seq', 0, 0, axis_index_groups=group)  10.6 us
    all_to_all x1, starting transfers between devices, on_device(): message = lax.all_to_all(message, 'seq', 0, 0, axis_index_groups=group)  8.15 us
    all_to_all x1, waiting for transfers between devices, on_device(): message = lax.all_to_all(message, 'seq', 0, 0, axis_index_groups=group)  7.26 us
    ppermute x3, starting transfers between devices, on_device(): lax.ppermute(message, 'chan', [(c, c // near * near + (c + step) % near)...  5.9 us
    ppermute x1, starting transfers between devices, on_device(): lax.ppermute(gating, 'chan', [(c, (c + near) % chans) for c in range(chan...  5.01 us
    ppermute x1, waiting for transfers between devices, on_device(): lax.ppermute(gating, 'chan', [(c, (c + near) % chans) for c in range(chan...  3.55 us
    ppermute x3, waiting for transfers between devices, on_device(): lax.ppermute(message, 'chan', [(c, c // near * near + (c + step) % near)...  2.92 us
    pallas_call x1, Pallas kernels, on_device(): pl.pallas_call(functools.partial(forward_kernel, devices), in_specs=[HBM]...  2.5 us
  transfers between devices with their start and end apart: 5, of which 5 were waited for; matrix products, arithmetic and copies ran while one was open for 0% of the time, Pallas kernels for 0%

profile of v9, /device:TPU:2, one launch (start us, length us, event | category | flops | bytes accessed | tf_op | source)
XLA Modules:
  0.0 49.1 jit_solution(7385201140767688016)
XLA Ops:
  0.0 2.5 %forward.1 = (bf16[32,17,2,128]{3,2,1,0:T(2,128)(2,1)}, f32[256,128]{1,0:T(8,128)S(1)}) custom-call(f32[3,1,3]{2,1,0:T(1,128)} %taps_hbm.1, bf16[1,32768]{1,0:T(2,128)(2,1)} %k_hbm.1, bf16[1,32768]{1,0:T(2,128)(2,1)} %v_hbm.1, bf16[1,32768]{1,0:T(2,128)(2,1)} %q_hbm.1, f32[256,128]{1,0:T(8,128)} %bitcast.3, bf16[512,256]{1,0:T(8,128)(2,1)} %constant.12.clone.first_hbm, ...), custom_call_target="tpu_custom_call" | custom-call | tf_op jit(solution)/shard_map/forward/pallas_call | solution.py:290
  2.5 0.0 copy-start.1
  2.5 0.0 copy-start.5
  2.5 0.0 copy-start.6
  2.5 8.1 %all-to-all-start = ((bf16[32,17,2,128]{3,2,1,0:T(2,128)(2,1)}), bf16[32,17,2,128]{3,2,1,0:T(2,128)(2,1)S(1)}, u32[]{:S(2)}, u32[]{:S(2)}) async-start(bf16[32,17,2,128]{3,2,1,0:T(2,128)(2,1)} %get-tuple-element.16), calls=%async_computation | async-start | bytes 557056 | tf_op jit(solution)/shard_map/all_to_all | solution.py:329
  10.7 0.0 copy-done.1
  10.7 0.0 copy-done.5
  10.7 0.0 copy-done.6
  10.7 0.0 copy-start.4
  10.7 0.0 copy-start.3
  10.8 0.2 side.1
  11.6 7.3 %all-to-all-done = bf16[32,17,2,128]{3,2,1,0:T(2,128)(2,1)S(1)} async-done(((bf16[32,17,2,128]{3,2,1,0:T(2,128)(2,1)}), bf16[32,17,2,128]{3,2,1,0:T(2,128)(2,1)S(1)}, u32[]{:S(2)}, u32[]{:S(2)}) %all-to-all-start) | async-done | bytes 278560 | tf_op jit(solution)/shard_map/all_to_all | solution.py:329
  18.9 0.0 copy-done.4
  18.9 0.0 copy-start
  18.9 0.0 copy-start.2
  18.9 0.8 %middle.1 = (bf16[32,16,128]{2,1,0:T(8,128)(2,1)S(1)}, f32[8,128]{1,0:T(8,128)S(1)}) custom-call(f32[1]{0:T(128)S(6)} %copy.14.skip_ref, f32[24,128]{1,0:T(8,128)S(1)} %get-tuple-element.15.scalars_ref, bf16[1088,128]{1,0:T(8,128)(2,1)S(1)} %bitcast.2, f32[2,8,128]{2,1,0:T(8,128)S(1)} %copy-done.4), custom_call_target="tpu_custom_call" | custom-call | tf_op jit(solution)/shard_map/middle/pallas_call | solution.py:330
  19.7 10.6 %all_to_all.10.spectra_ref = bf16[32,16,128]{2,1,0:T(8,128)(2,1)S(1)} all-to-all(bf16[32,16,128]{2,1,0:T(8,128)(2,1)S(1)} %get-tuple-element.17), channel_id=1, replica_groups={{168,160,232,224,104,96,40,32,184,176,248,240,120,112,56,48,152,144,216..., dimensions={0} | all-to-all | bytes 262144 | tf_op jit(solution)/shard_map/all_to_all | solution.py:342
  30.4 0.0 copy-done.3
  30.4 0.0 copy-done
  30.4 0.0 copy-done.2
  30.4 0.5 inverse.1.own_gating_ref
  30.8 5.0 %collective-permute-start = (bf16[256,128]{1,0:T(8,128)(2,1)S(1)}, bf16[256,128]{1,0:T(8,128)(2,1)S(1)}, u32[]{:S(2)}, u32[]{:S(2)}) collective-permute-start(bf16[256,128]{1,0:T(8,128)(2,1)S(1)} %inverse.1.own_gating_ref), channel_id=1, source_target_pairs={{0,4},{1,5},{2,6},{3,7},{4,0},{5,1},{6,2},{7,3},{8,12},{9,13},{10,... | collective-permute-start | bytes 196616 | tf_op jit(solution)/shard_map/ppermute | solution.py:351
  35.8 3.6 %collective-permute-done.other_gating_ref = bf16[256,128]{1,0:T(8,128)(2,1)S(1)} collective-permute-done((bf16[256,128]{1,0:T(8,128)(2,1)S(1)}, bf16[256,128]{1,0:T(8,128)(2,1)S(1)}, u32[]{:S(2)}, u32[]{:S(2)}) %collective-permute-start) | collective-permute-done | bytes 65568 | tf_op jit(solution)/shard_map/ppermute | solution.py:351
  39.4 0.1 mix.1
  39.5 1.7 %collective-permute-start.1 = (bf16[256,128]{1,0:T(8,128)(2,1)S(1)}, bf16[256,128]{1,0:T(8,128)(2,1)S(1)}, u32[]{:S(2)}, u32[]{:S(2)}) collective-permute-start(bf16[256,128]{1,0:T(8,128)(2,1)S(1)} %get-tuple-element.22), channel_id=1, source_target_pairs={{0,1},{1,2},{2,3},{3,0},{4,5},{5,6},{6,7},{7,4},{8,9},{9,10},{10,1... | collective-permute-start | bytes 196616 | tf_op jit(solution)/shard_map/ppermute | solution.py:361
  41.1 2.9 %collective-permute-start.2 = (bf16[256,128]{1,0:T(8,128)(2,1)S(1)}, bf16[256,128]{1,0:T(8,128)(2,1)S(1)}, u32[]{:S(2)}, u32[]{:S(2)}) collective-permute-start(bf16[256,128]{1,0:T(8,128)(2,1)S(1)} %get-tuple-element.23), channel_id=1, source_target_pairs={{0,2},{1,3},{2,0},{3,1},{4,6},{5,7},{6,4},{7,5},{8,10},{9,11},{10,... | collective-permute-start | bytes 196616 | tf_op jit(solution)/shard_map/ppermute | solution.py:361
  44.0 1.3 %collective-permute-start.3 = (bf16[256,128]{1,0:T(8,128)(2,1)S(1)}, bf16[256,128]{1,0:T(8,128)(2,1)S(1)}, u32[]{:S(2)}, u32[]{:S(2)}) collective-permute-start(bf16[256,128]{1,0:T(8,128)(2,1)S(1)} %get-tuple-element.24), channel_id=1, source_target_pairs={{0,3},{1,0},{2,1},{3,2},{4,7},{5,4},{6,5},{7,6},{8,11},{9,8},{10,9... | collective-permute-start | bytes 196616 | tf_op jit(solution)/shard_map/ppermute | solution.py:361
  45.4 0.4 collective-permute-done.1.refs_0_
  45.7 1.3 %collective-permute-done.2.refs_1_ = bf16[256,128]{1,0:T(8,128)(2,1)S(1)} collective-permute-done((bf16[256,128]{1,0:T(8,128)(2,1)S(1)}, bf16[256,128]{1,0:T(8,128)(2,1)S(1)}, u32[]{:S(2)}, u32[]{:S(2)}) %collective-permute-start.2) | collective-permute-done | bytes 65568 | tf_op jit(solution)/shard_map/ppermute | solution.py:361
  47.0 1.3 %collective-permute-done.3.refs_2_ = bf16[256,128]{1,0:T(8,128)(2,1)S(1)} collective-permute-done((bf16[256,128]{1,0:T(8,128)(2,1)S(1)}, bf16[256,128]{1,0:T(8,128)(2,1)S(1)}, u32[]{:S(2)}, u32[]{:S(2)}) %collective-permute-start.3) | collective-permute-done | bytes 65568 | tf_op jit(solution)/shard_map/ppermute | solution.py:361
  48.3 0.8 %add.1 = bf16[1,32768]{1,0:T(2,128)(2,1)} custom-call(f32[256,128]{1,0:T(8,128)S(1)} %get-tuple-element.21.own_ref, bf16[256,128]{1,0:T(8,128)(2,1)S(1)} %collective-permute-done.1.refs_0_, bf16[256,128]{1,0:T(8,128)(2,1)S(1)} %collective-permute-done.2.refs_1_, bf16[256,128]{1,0:T(8,128)(2,1)S(1)} %collective-permute-done.3.refs_2_), custom_call_target="tpu_custom_call" | custom-call | tf_op jit(solution)/shard_map/add/pallas_call | solution.py:364
Async XLA Ops:
  2.5 8.2 %copy-start.1 = (bf16[1,32768]{1,0:T(2,128)(2,1)S(1)}, bf16[1,32768]{1,0:T(2,128)(2,1)}, u32[]{:S(2)}) copy-start(bf16[1,32768]{1,0:T(2,128)(2,1)} %q_hbm.1) | copy-start | bytes 196612
  2.5 8.2 %copy-start.5 = (f32[3,1,3]{2,1,0:T(1,128)S(1)}, f32[3,1,3]{2,1,0:T(1,128)}, u32[]{:S(2)}) copy-start(f32[3,1,3]{2,1,0:T(1,128)} %taps_hbm.1) | copy-start | bytes 112
  2.5 8.2 %copy-start.6 = (bf16[8,8]{1,0:T(8,128)(2,1)S(1)}, bf16[8,8]{1,0:T(8,128)(2,1)}, u32[]{:S(2)}) copy-start(bf16[8,8]{1,0:T(8,128)(2,1)} %w_ref.1) | copy-start | bytes 388
  2.5 16.4 %all-to-all-start = ((bf16[32,17,2,128]{3,2,1,0:T(2,128)(2,1)}), bf16[32,17,2,128]{3,2,1,0:T(2,128)(2,1)S(1)}, u32[]{:S(2)}, u32[]{:S(2)}) async-start(bf16[32,17,2,128]{3,2,1,0:T(2,128)(2,1)} %get-tuple-element.16), calls=%async_computation | async-start | bytes 557056 | tf_op jit(solution)/shard_map/all_to_all | solution.py:329
  10.7 8.2 %copy-start.4 = (f32[2,8,128]{2,1,0:T(8,128)S(1)}, f32[2,8,128]{2,1,0:T(8,128)}, u32[]{:S(2)}) copy-start(f32[2,8,128]{2,1,0:T(8,128)} %constant.15.clone.basis_ref) | copy-start | bytes 24580
  10.7 19.6 %copy-start.3 = (bf16[256,256]{1,0:T(8,128)(2,1)S(1)}, bf16[256,256]{1,0:T(8,128)(2,1)}, u32[]{:S(2)}) copy-start(bf16[256,256]{1,0:T(8,128)(2,1)} %constant.16.clone.second_ref) | copy-start | bytes 393220
  18.9 11.5 %copy-start = (f32[2,256,128]{2,1,0:T(8,128)S(1)}, f32[2,256,128]{2,1,0:T(8,128)}, u32[]{:S(2)}) copy-start(f32[2,256,128]{2,1,0:T(8,128)} %constant.13.clone.turn_hbm.turn_ref) | copy-start | bytes 786436
  18.9 11.5 %copy-start.2 = (bf16[256,512]{1,0:T(8,128)(2,1)S(1)}, bf16[256,512]{1,0:T(8,128)(2,1)}, u32[]{:S(2)}) copy-start(bf16[256,512]{1,0:T(8,128)(2,1)} %constant.17.clone.first_ref) | copy-start | bytes 786436
  30.8 8.6 %collective-permute-start = (bf16[256,128]{1,0:T(8,128)(2,1)S(1)}, bf16[256,128]{1,0:T(8,128)(2,1)S(1)}, u32[]{:S(2)}, u32[]{:S(2)}) collective-permute-start(bf16[256,128]{1,0:T(8,128)(2,1)S(1)} %inverse.1.own_gating_ref), channel_id=1, source_target_pairs={{0,4},{1,5},{2,6},{3,7},{4,0},{5,1},{6,2},{7,3},{8,12},{9,13},{10,... | collective-permute-start | bytes 196616 | tf_op jit(solution)/shard_map/ppermute | solution.py:351
  39.5 6.3 %collective-permute-start.1 = (bf16[256,128]{1,0:T(8,128)(2,1)S(1)}, bf16[256,128]{1,0:T(8,128)(2,1)S(1)}, u32[]{:S(2)}, u32[]{:S(2)}) collective-permute-start(bf16[256,128]{1,0:T(8,128)(2,1)S(1)} %get-tuple-element.22), channel_id=1, source_target_pairs={{0,1},{1,2},{2,3},{3,0},{4,5},{5,6},{6,7},{7,4},{8,9},{9,10},{10,1... | collective-permute-start | bytes 196616 | tf_op jit(solution)/shard_map/ppermute | solution.py:361
  41.1 5.9 %collective-permute-start.2 = (bf16[256,128]{1,0:T(8,128)(2,1)S(1)}, bf16[256,128]{1,0:T(8,128)(2,1)S(1)}, u32[]{:S(2)}, u32[]{:S(2)}) collective-permute-start(bf16[256,128]{1,0:T(8,128)(2,1)S(1)} %get-tuple-element.23), channel_id=1, source_target_pairs={{0,2},{1,3},{2,0},{3,1},{4,6},{5,7},{6,4},{7,5},{8,10},{9,11},{10,... | collective-permute-start | bytes 196616 | tf_op jit(solution)/shard_map/ppermute | solution.py:361
  44.0 4.3 %collective-permute-start.3 = (bf16[256,128]{1,0:T(8,128)(2,1)S(1)}, bf16[256,128]{1,0:T(8,128)(2,1)S(1)}, u32[]{:S(2)}, u32[]{:S(2)}) collective-permute-start(bf16[256,128]{1,0:T(8,128)(2,1)S(1)} %get-tuple-element.24), channel_id=1, source_target_pairs={{0,3},{1,0},{2,1},{3,2},{4,7},{5,4},{6,5},{7,6},{8,11},{9,8},{10,9... | collective-permute-start | bytes 196616 | tf_op jit(solution)/shard_map/ppermute | solution.py:361
